TPU v7x, 32 devices: a whole 2x2x4 slice. The times are simulated.
32 devices in a mesh: chain: 2 (over core), sector: 16 (over z, y, x).
Axes of the slice: x: 2, y: 2, z: 4, core: 2. Of those that a mesh axis runs over, the one named last changes fastest.
Arguments:
- env_first: bfloat16 [2, 16, 15, 128, 128], P(None, 'sector'), may hold values from -6 to 6
- states: bfloat16 [2, 2, 4, 16, 128, 128], P('chain', None, None, 'sector'), may hold values from -0.5 to 0.5
- mpo: bfloat16 [2, 4, 15, 15], P('chain'), may hold values from -1.5 to 1.5
- block_rows: int32 [2, 16], P('chain', 'sector'), may hold values from 1 to 128, 1024 in all within a row
- present: int32 [2, 4, 16], P('chain', None, 'sector'), may hold values 0 or 1
Outputs:
- env_out: bfloat16 [2, 2, 16, 15, 128, 128], P('chain', None, 'sector')
Inputs may be any that keep to these rules, and one draw needn't show every extreme that they name: `block_rows`: in each site's row the 16 live sizes add up to 1024, and one of them equals 128.
All inputs are finite; a program needn't handle non-finite values. No bound on the sum of `block_rows` or of `present` on one device may be relied on, other than what follows from the above.
Results may differ from a plain program's by a relative error of at most 0.008.
Values may be sent and summed in bfloat16 or wider, within the bound.
No kernel may reach another device: no remote copies, remote signals or barrier semaphores. Data moves between devices by JAX's collectives and lax.ppermute only.
A program may use at most 128 MiB of HBM per device.

v0:
```python
import jax
import jax.numpy as jnp
from jax import lax
from jax.sharding import PartitionSpec as P

QD = 4


def from_behind(value, axis, steps):
    count = lax.axis_size(axis)
    initial, last = (max(0, -steps), min(count, count - steps))
    return lax.ppermute(value, axis, [(source, source + steps) for source in range(initial, last)])


def state_mask(exists, inside_grid):
    state_ids = jnp.arange(exists.shape[0])
    return exists.astype(jnp.float32) * jnp.where(
        state_ids >= 2, inside_grid.astype(jnp.float32), 1.0
    )


def contract(incoming, blocks, coupling, exists, inside_grid):
    projected = jnp.einsum(
        "gwab,gsbc->gswac", incoming, blocks, preferred_element_type=jnp.float32
    ).astype(jnp.bfloat16)
    sandwich = jnp.einsum(
        "gsad,gswac->gswdc", blocks, projected, preferred_element_type=jnp.float32
    )
    coupled = jnp.einsum(
        "gswdc,swv->gsvdc", sandwich, coupling.astype(jnp.float32), precision=lax.Precision.HIGHEST
    )
    keep_mask = state_mask(exists, inside_grid)
    return (coupled * keep_mask[None, :, None, None, None]).astype(jnp.bfloat16)


def deliver(partials, rows_live):
    from_down = from_behind(partials[:, 2], "sector", 1)
    from_up = from_behind(partials[:, 1], "sector", QD)
    from_both = from_behind(partials[:, 3], "sector", QD + 1)
    summed = (
        partials[:, 0].astype(jnp.float32)
        + from_down.astype(jnp.float32)
        + from_up.astype(jnp.float32)
        + from_both.astype(jnp.float32)
    )
    block_width = partials.shape[-1]
    live_rows = jnp.arange(block_width) < rows_live
    live_mask = live_rows[:, None] & live_rows[None, :]
    return jnp.where(live_mask, summed, 0.0).astype(jnp.bfloat16)


def on_device(env_first, states, mpo, block_rows, present):
    chains = lax.axis_size("chain")
    chain_id = lax.axis_index("chain")
    down_charge = lax.axis_index("sector") % QD
    inside_grid = down_charge < QD - 1
    targets = env_first.shape[0]
    starting = env_first[:, 0]
    result = jnp.zeros_like(starting)
    blocks = states[0, :, :, 0]
    coupling = mpo[0]
    exists = present[0, :, 0]
    rows_live = block_rows[0, 0]
    current = starting
    zero_parts = jnp.zeros((targets, blocks.shape[1]) + starting.shape[1:], jnp.bfloat16)
    for step_number in range(chains):
        active = chain_id == step_number
        partials = lax.cond(
            active,
            lambda incoming: contract(incoming, blocks, coupling, exists, inside_grid),
            lambda incoming: zero_parts,
            current,
        )
        renewed = deliver(partials, rows_live)
        result = jnp.where(active, renewed, result)
        if step_number + 1 < chains:
            passed = from_behind(renewed, "chain", 1)
            current = jnp.where(chain_id == step_number + 1, passed, current)
    return result[None, :, None]


def solution(mesh):
    placed = (
        P(None, "sector", None, None, None),
        P("chain", None, None, "sector", None, None),
        P("chain", None, None, None),
        P("chain", "sector"),
        P("chain", None, "sector"),
    )
    return jax.shard_map(
        on_device,
        mesh=mesh,
        in_specs=placed,
        out_specs=P("chain", None, "sector", None, None, None),
        check_vma=False,
    )
```

profile of v0, /device:TPU:25, one launch (start us, length us, event | category | flops | bytes accessed | tf_op | source)
XLA Modules:
  0.0 195.8 jit_solution(1461367551936821178)
XLA Ops:
  0.0 0.8 copy.6
  0.8 2.5 %conditional.2 = (bf16[2,4,15,128,128]{4,2,3,0,1:T(8,128)(2,1)}) conditional(s32[]{:T(128)} %convert_element_type.81, () %tuple.18, (bf16[2,4,128,128]{3,2,1,0:T(8,128)(2,1)}, bf16[2,15,128,128]{3,2,1,0:T(8,128)(2,1)}, bf16[4,15,15]{1,2,0:T(8,128)(2,1)S(1)}, s32[4]{0:T(128)}, pred[]{:T(512)}) %tuple.37), branch_computations={%region_0.1_spmd, %region_1.2_spmd} | conditional | flops 1364459520 | bytes 53675968 | solution.py:68
  0.8 2.5 %broadcast_in_dim.32 = bf16[2,4,15,128,128]{4,2,3,0,1:T(8,128)(2,1)} broadcast(bf16[]{:T(256)} %constant.10.clone), dimensions={} | broadcast | bytes 3932162 | tf_op jit(solution)/shard_map/broadcast_in_dim | solution.py:65
  3.4 2.9 %fusion.39 = (bf16[2,1,15,128,128]{4,2,3,0,1:T(8,128)(2,1)S(1)}, bf16[2,1,15,128,128]{4,2,3,0,1:T(8,128)(2,1)S(1)}, bf16[2,1,15,128,128]{4,2,3,0,1:T(8,128)(2,1)S(1)}, bf16[2,1,15,128,128]{4,2,3,0,1:T(8,128)(2,1)S(1)}) fusion(bf16[2,4,15,128,128]{4,2,3,0,1:T(8,128)(2,1)} %get-tuple-element.57), kind=kLoop, calls=%fused_computation.54 | loop fusion | bytes 7864320 | tf_op jit(solution)/shard_map/slice | solution.py:41
  6.3 0.3 copy.64
  6.6 3.1 %collective-permute-start = (bf16[2,15,128,128]{3,2,1,0:T(8,128)(2,1)S(1)}, bf16[2,15,128,128]{3,2,1,0:T(8,128)(2,1)S(1)}, u32[]{:S(2)}, u32[]{:S(2)}) collective-permute-start(bf16[2,15,128,128]{3,2,1,0:T(8,128)(2,1)S(1)} %bitcast.98), channel_id=1, source_target_pairs={{0,1},{1,2},{2,3},{3,4},{4,5},{5,6},{6,7},{7,8},{8,9},{9,10},{10,1... | collective-permute-start | bytes 2949128 | tf_op jit(solution)/shard_map/ppermute | solution.py:12
  9.7 0.0 copy-start
  9.7 0.0 copy-start.2
  9.7 0.0 copy-start.3
  9.7 0.3 copy.63
  10.0 1.4 collective-permute-start.1
  11.4 0.3 copy.62
  11.7 1.3 collective-permute-start.2
  13.7 0.1 broadcast_and_fusion
  13.7 9.5 %collective-permute-done = bf16[2,15,128,128]{3,2,1,0:T(8,128)(2,1)S(1)} collective-permute-done((bf16[2,15,128,128]{3,2,1,0:T(8,128)(2,1)S(1)}, bf16[2,15,128,128]{3,2,1,0:T(8,128)(2,1)S(1)}, u32[]{:S(2)}, u32[]{:S(2)}) %collective-permute-start) | collective-permute-done | bytes 983072 | tf_op jit(solution)/shard_map/ppermute | solution.py:12
  23.2 1.8 collective-permute-done.1
  25.0 40.2 %collective-permute-done.2 = bf16[2,15,128,128]{3,2,1,0:T(8,128)(2,1)S(1)} collective-permute-done((bf16[2,15,128,128]{3,2,1,0:T(8,128)(2,1)S(1)}, bf16[2,15,128,128]{3,2,1,0:T(8,128)(2,1)S(1)}, u32[]{:S(2)}, u32[]{:S(2)}) %collective-permute-start.2) | collective-permute-done | bytes 983072 | tf_op jit(solution)/shard_map/ppermute | solution.py:12
  65.2 0.6 fusion.35
  65.8 1.3 collective-permute-start.3
  67.1 34.4 %collective-permute-done.3 = bf16[2,15,128,128]{3,2,1,0:T(8,128)(2,1)S(1)} collective-permute-done((bf16[2,15,128,128]{3,2,1,0:T(8,128)(2,1)S(1)}, bf16[2,15,128,128]{3,2,1,0:T(8,128)(2,1)S(1)}, u32[]{:S(2)}, u32[]{:S(2)}) %collective-permute-start.3) | collective-permute-done | bytes 983072 | tf_op jit(solution)/shard_map/ppermute | solution.py:12
  101.5 0.0 copy-done
  101.5 0.0 copy-done.2
  101.5 0.0 copy-done.3
  101.5 29.3 %conditional.3 = (bf16[2,4,15,128,128]{4,2,3,0,1:T(8,128)(2,1)}) conditional(s32[]{:T(128)} %convert_element_type.80, () %tuple.17, (pred[]{:T(512)}, bf16[2,15,128,128]{3,2,1,0:T(8,128)(2,1)S(1)}, bf16[2,15,128,128]{3,2,1,0:T(8,128)(2,1)S(1)}, bf16[2,4,128,128]{3,2,1,0:T(8,128)(2,1)S(1)}, bf16[4,15,15]{1,2,0:T(8,128)(2,1)S(1)}, ...), branch_computations={%region_2.3_spmd, %region_3.4_spmd} | conditional | flops 1366917120 | bytes 53610312 | solution.py:68
  101.5 1.2 convolution_convert_fusion
  102.7 3.7 %copy.58 = bf16[2,15,128,4,128]{4,3,2,1,0:T(4,128)(2,1)S(1)} copy(bf16[2,15,128,4,128]{4,2,3,1,0:T(8,128)(2,1)S(1)} %convolution_convert_fusion) | data formatting | bytes 7864320 | tf_op jit(solution)/shard_map/cond
  106.4 4.4 %fusion.17 = f32[2,4,15,128,128]{4,3,2,1,0:T(8,128)} fusion(bf16[2,4,15,128,128]{4,1,3,2,0:T(4,128)(2,1)S(1)} %bitcast.93, bf16[2,4,128,128]{3,2,1,0:T(8,128)(2,1)S(1)} %get-tuple-element.45), kind=kOutput, calls=%fused_computation.20 | convolution fusion | flops 503316480 | bytes 12058624 | tf_op jit(solution)/shard_map/cond/branch_1_fun/gsad,gswac->gswdc/dot_general | solution.py:26
  110.8 10.1 %copy.26 = f32[2,4,15,128,128]{3,2,4,0,1:T(8,128)} copy(f32[2,4,15,128,128]{4,3,2,1,0:T(8,128)} %fusion.17) | data formatting | bytes 15728640 | tf_op jit(solution)/shard_map/cond/branch_1_fun/gsad,gswac->gswdc/dot_general | solution.py:26
  120.9 10.0 %fusion.16 = bf16[2,4,15,128,128]{4,2,3,0,1:T(8,128)(2,1)} fusion(f32[4]{0:T(128)S(1)} %fusion.27, f32[2,4,15,128,128]{3,2,4,0,1:T(8,128)} %copy.26, bf16[4,15,15]{1,2,0:T(8,128)(2,1)S(1)} %get-tuple-element.46), kind=kOutput, calls=%fused_computation.18 | convolution fusion | flops 357826560 | bytes 11798296 | tf_op jit(solution)/shard_map/cond/branch_1_fun/gswdc,swv->gsvdc/dot_general | solution.py:29
  130.8 2.9 %fusion.38 = (bf16[2,1,15,128,128]{4,2,3,0,1:T(8,128)(2,1)S(1)}, bf16[2,1,15,128,128]{4,2,3,0,1:T(8,128)(2,1)S(1)}, bf16[2,1,15,128,128]{4,2,3,0,1:T(8,128)(2,1)S(1)}, bf16[2,1,15,128,128]{4,2,3,0,1:T(8,128)(2,1)S(1)}) fusion(bf16[2,4,15,128,128]{4,2,3,0,1:T(8,128)(2,1)} %get-tuple-element.58), kind=kLoop, calls=%fused_computation.53 | loop fusion | bytes 7864320 | tf_op jit(solution)/shard_map/slice | solution.py:41
  133.8 0.3 copy.61
  134.0 1.9 collective-permute-start.4
  136.0 0.3 copy.60
  136.2 1.3 collective-permute-start.5
  137.5 0.3 copy.59
  137.8 1.3 collective-permute-start.6
  139.1 17.0 %collective-permute-done.4 = bf16[2,15,128,128]{3,2,1,0:T(8,128)(2,1)S(1)} collective-permute-done((bf16[2,15,128,128]{3,2,1,0:T(8,128)(2,1)S(1)}, bf16[2,15,128,128]{3,2,1,0:T(8,128)(2,1)S(1)}, u32[]{:S(2)}, u32[]{:S(2)}) %collective-permute-start.4) | collective-permute-done | bytes 983072 | tf_op jit(solution)/shard_map/ppermute | solution.py:12
  156.2 0.0 collective-permute-done.5
  156.2 37.8 %collective-permute-done.6 = bf16[2,15,128,128]{3,2,1,0:T(8,128)(2,1)S(1)} collective-permute-done((bf16[2,15,128,128]{3,2,1,0:T(8,128)(2,1)S(1)}, bf16[2,15,128,128]{3,2,1,0:T(8,128)(2,1)S(1)}, u32[]{:S(2)}, u32[]{:S(2)}) %collective-permute-start.6) | collective-permute-done | bytes 983072 | tf_op jit(solution)/shard_map/ppermute | solution.py:12
  194.0 1.8 fusion.37
  (2 shorter events, 0.0 us)
Async XLA Ops:
  6.6 16.6 %collective-permute-start = (bf16[2,15,128,128]{3,2,1,0:T(8,128)(2,1)S(1)}, bf16[2,15,128,128]{3,2,1,0:T(8,128)(2,1)S(1)}, u32[]{:S(2)}, u32[]{:S(2)}) collective-permute-start(bf16[2,15,128,128]{3,2,1,0:T(8,128)(2,1)S(1)} %bitcast.98), channel_id=1, source_target_pairs={{0,1},{1,2},{2,3},{3,4},{4,5},{5,6},{6,7},{7,8},{8,9},{9,10},{10,1... | collective-permute-start | bytes 2949128 | tf_op jit(solution)/shard_map/ppermute | solution.py:12
  9.7 91.8 %copy-start = (bf16[1,2,4,1,128,128]{5,4,3,2,1,0:T(8,128)(2,1)S(1)}, bf16[1,2,4,1,128,128]{5,4,3,2,1,0:T(8,128)(2,1)}, u32[]{:S(2)}) copy-start(bf16[1,2,4,1,128,128]{5,4,3,2,1,0:T(8,128)(2,1)} %param.10) | copy-start | bytes 786436
  9.7 91.8 %copy-start.2 = (bf16[2,1,15,128,128]{4,3,2,1,0:T(8,128)(2,1)S(1)}, bf16[2,1,15,128,128]{4,3,2,1,0:T(8,128)(2,1)}, u32[]{:S(2)}) copy-start(bf16[2,1,15,128,128]{4,3,2,1,0:T(8,128)(2,1)} %param.9) | copy-start | bytes 2949124
  9.7 91.8 %copy-start.3 = (s32[1,4,1]{1,2,0:T(1,128)S(1)}, s32[1,4,1]{1,2,0:T(1,128)}, u32[]{:S(2)}) copy-start(s32[1,4,1]{1,2,0:T(1,128)} %param.13) | copy-start | bytes 52
  10.0 15.0 %collective-permute-start.1 = (bf16[2,15,128,128]{3,2,1,0:T(8,128)(2,1)S(1)}, bf16[2,15,128,128]{3,2,1,0:T(8,128)(2,1)S(1)}, u32[]{:S(2)}, u32[]{:S(2)}) collective-permute-start(bf16[2,15,128,128]{3,2,1,0:T(8,128)(2,1)S(1)} %bitcast.99), channel_id=1, source_target_pairs={{0,4},{1,5},{2,6},{3,7},{4,8},{5,9},{6,10},{7,11},{8,12},{9,13},{1... | collective-permute-start | bytes 2949128 | tf_op jit(solution)/shard_map/ppermute | solution.py:12
  11.7 53.5 %collective-permute-start.2 = (bf16[2,15,128,128]{3,2,1,0:T(8,128)(2,1)S(1)}, bf16[2,15,128,128]{3,2,1,0:T(8,128)(2,1)S(1)}, u32[]{:S(2)}, u32[]{:S(2)}) collective-permute-start(bf16[2,15,128,128]{3,2,1,0:T(8,128)(2,1)S(1)} %bitcast.100), channel_id=1, source_target_pairs={{0,5},{1,6},{2,7},{3,8},{4,9},{5,10},{6,11},{7,12},{8,13},{9,14},{... | collective-permute-start | bytes 2949128 | tf_op jit(solution)/shard_map/ppermute | solution.py:12
  65.8 35.7 %collective-permute-start.3 = (bf16[2,15,128,128]{3,2,1,0:T(8,128)(2,1)S(1)}, bf16[2,15,128,128]{3,2,1,0:T(8,128)(2,1)S(1)}, u32[]{:S(2)}, u32[]{:S(2)}) collective-permute-start(bf16[2,15,128,128]{3,2,1,0:T(8,128)(2,1)S(1)} %fusion.35), channel_id=1, source_target_pairs={{0,16},{1,17},{2,18},{3,19},{4,20},{5,21},{6,22},{7,23},{8,24},{9,... | collective-permute-start | bytes 2949128 | tf_op jit(solution)/shard_map/ppermute | solution.py:12
  134.0 22.1 %collective-permute-start.4 = (bf16[2,15,128,128]{3,2,1,0:T(8,128)(2,1)S(1)}, bf16[2,15,128,128]{3,2,1,0:T(8,128)(2,1)S(1)}, u32[]{:S(2)}, u32[]{:S(2)}) collective-permute-start(bf16[2,15,128,128]{3,2,1,0:T(8,128)(2,1)S(1)} %bitcast.101), channel_id=1, source_target_pairs={{0,1},{1,2},{2,3},{3,4},{4,5},{5,6},{6,7},{7,8},{8,9},{9,10},{10,1... | collective-permute-start | bytes 2949128 | tf_op jit(solution)/shard_map/ppermute | solution.py:12
  136.2 19.9 %collective-permute-start.5 = (bf16[2,15,128,128]{3,2,1,0:T(8,128)(2,1)S(1)}, bf16[2,15,128,128]{3,2,1,0:T(8,128)(2,1)S(1)}, u32[]{:S(2)}, u32[]{:S(2)}) collective-permute-start(bf16[2,15,128,128]{3,2,1,0:T(8,128)(2,1)S(1)} %bitcast.102), channel_id=1, source_target_pairs={{0,4},{1,5},{2,6},{3,7},{4,8},{5,9},{6,10},{7,11},{8,12},{9,13},{1... | collective-permute-start | bytes 2949128 | tf_op jit(solution)/shard_map/ppermute | solution.py:12
  137.8 56.2 %collective-permute-start.6 = (bf16[2,15,128,128]{3,2,1,0:T(8,128)(2,1)S(1)}, bf16[2,15,128,128]{3,2,1,0:T(8,128)(2,1)S(1)}, u32[]{:S(2)}, u32[]{:S(2)}) collective-permute-start(bf16[2,15,128,128]{3,2,1,0:T(8,128)(2,1)S(1)} %bitcast.103), channel_id=1, source_target_pairs={{0,5},{1,6},{2,7},{3,8},{4,9},{5,10},{6,11},{7,12},{8,13},{9,14},{... | collective-permute-start | bytes 2949128 | tf_op jit(solution)/shard_map/ppermute | solution.py:12
where the time goes:
time: 196 us
  waiting for transfers between devices  141 us (72%)
  local copies, waits for them, and re-layouts  24.5 us (12%)
  matrix products  15.6 us (8%)
  starting transfers between devices  11.6 us (6%)
  other arithmetic  2.56 us (1%)
    ppermute x7, waiting for transfers between devices, from_behind(): lax.ppermute(value, axis, [(source, source + steps) for source in range(i...  141 us
    ppermute x7, starting transfers between devices, from_behind(): lax.ppermute(value, axis, [(source, source + steps) for source in range(i...  11.6 us
    dot_general x1, local copies, waits for them, and re-layouts, contract(): jnp.einsum('gsad,gswac->gswdc', blocks, projected, preferred_element_type...  10.1 us
    dot_general x1, matrix products, contract(): jnp.einsum('gswdc,swv->gsvdc', sandwich, coupling.astype(jnp.float32), pr...  9.98 us
    slice x2, local copies, waits for them, and re-layouts, deliver(): partials[:, 0].astype(jnp.float32) + from_down.astype(jnp.float32)  5.86 us
    dot_general x1, matrix products, contract(): jnp.einsum('gsad,gswac->gswdc', blocks, projected, preferred_element_type...  4.4 us
  transfers between devices with their start and end apart: 7, of which 6 were waited for; matrix products, arithmetic and copies ran while one was open for 1% of the time, Pallas kernels for 0%

commit v1 on v0

v1 whole, which is shorter than its diff:
```python
import functools

import jax
import jax.numpy as jnp
from jax import lax
from jax.experimental import pallas as pl
from jax.experimental.pallas import tpu as pltpu
from jax.sharding import PartitionSpec as P

QD = 4
LO = 16
AXES = ("chain", "sector")


def rings(sectors):
    down = lambda k: (k // QD) * QD + (k + 1) % QD
    up = lambda k: (k + QD) % sectors
    first = [(k, down(k)) for k in range(sectors)] + [(sectors + k, sectors + up(k)) for k in range(sectors)]
    second = [(k, up(k)) for k in range(sectors)] + [(sectors + k, sectors + down(k)) for k in range(sectors)]
    swap = [(k, sectors + k) for k in range(sectors)] + [(sectors + k, k) for k in range(sectors)]
    return first, second, swap


def place():
    core, sector = lax.axis_index("chain"), lax.axis_index("sector")
    inside = lax.rem(sector, QD) < QD - 1
    from_down, from_up = lax.rem(sector, QD) > 0, sector >= QD
    return core, inside, from_down, from_up


def spread(mpo):
    w = mpo.shape[0]
    rows = lax.broadcasted_iota(jnp.int32, (w * LO, w), 0) // LO
    pick = (rows == lax.broadcasted_iota(jnp.int32, (w * LO, w), 1)).astype(jnp.bfloat16)
    tall = lax.dot_general(pick, mpo, (((1,), (1,)), ((), ())), preferred_element_type=jnp.float32).astype(jnp.bfloat16)
    full = lax.dot_general(tall, pick, (((1,), (1,)), ((), ())), preferred_element_type=jnp.float32)
    i = lax.broadcasted_iota(jnp.int32, full.shape, 0) % LO
    j = lax.broadcasted_iota(jnp.int32, full.shape, 1) % LO
    return jnp.where(i == j, full, 0.0).astype(jnp.bfloat16)


def couple(coupling, projected, column, out):
    w, blk = out.shape[0], out.shape[1]
    part = lambda a: projected[:, a:a + LO, column:column + blk].reshape(w * LO, blk)
    for a in range(0, blk, 2 * LO):
        both = jnp.concatenate([part(a), part(a + LO)], axis=1)
        mixed = jnp.dot(coupling, both, preferred_element_type=jnp.float32).astype(out.dtype)
        out[:, a:a + LO, :] = mixed[:, :blk].reshape(w, LO, blk)
        out[:, a + LO:a + 2 * LO, :] = mixed[:, blk:].reshape(w, LO, blk)


def prepare_kernel(here, other, states, states_other, local, send):
    core, inside, _, _ = place()
    middle, outer = 1 + core, 2 - core

    def block(site, state):
        same = core == site
        exists = jnp.where(same, here[state], other[state]) > 0
        kept = exists & ((state < 2) | inside)
        both = jnp.where(same, states[core, state], states_other[core, state])
        return jnp.where(kept, both, jnp.zeros_like(both))

    for site in range(2):
        local[site, 0] = block(site, middle)
        local[site, 1] = block(site, 0)
        send[site, 0] = block(site, 3)
        send[site, 1] = block(site, outer)


def own_kernel(site, env, local, mpo, mpo_other, out_q, out_r, projected):
    core, _, _, _ = place()
    right = jnp.concatenate([local[site, 0], local[site, 1]], axis=1)
    for w in range(env.shape[0]):
        projected[w] = jnp.dot(env[w], right, preferred_element_type=jnp.float32).astype(jnp.bfloat16)
    pick = lambda state: jnp.where(core == site, mpo[state], mpo_other[state])
    couple(spread(pick(1 + core)), projected, 0, out_q)
    couple(spread(pick(0)), projected, env.shape[1], out_r)


def join_kernel(site, role, env, local, sent, mpo, mpo_other, mine, out, projected, mixed):
    core, _, from_down, from_up = place()
    valid = jnp.where(core == 0, from_down, from_up)
    theirs = jnp.where(valid, sent[site, role], jnp.zeros_like(sent[site, role]))
    for w in range(env.shape[0]):
        projected[w] = jnp.dot(env[w], theirs, preferred_element_type=jnp.float32).astype(jnp.bfloat16)
    state = 3 if role == 0 else 2 - core
    couple(spread(jnp.where(core == site, mpo[state], mpo_other[state])), projected, 0, mixed)
    left = jnp.concatenate([local[site, role], theirs], axis=0)
    for v in range(env.shape[0]):
        right = jnp.concatenate([mine[v], mixed[v]], axis=0)
        out[v] = lax.dot_general(left, right, (((0,), (0,)), ((), ())), preferred_element_type=jnp.float32).astype(out.dtype)


def sum_kernel(site, rows, rows_other, kept, arrived, out):
    core, _, from_down, from_up = place()
    live = jnp.where(core == site, rows[0], rows_other[0])
    valid = jnp.where(core == 0, from_up, from_down)
    blk = out.shape[1]
    inside = (lax.broadcasted_iota(jnp.int32, (blk, blk), 0) < live) & (lax.broadcasted_iota(jnp.int32, (blk, blk), 1) < live)
    for v in range(out.shape[0]):
        total = kept[v] + jnp.where(valid, arrived[v].astype(jnp.float32), 0.0)
        out[v] = jnp.where(inside, total, 0.0).astype(out.dtype)


VMEM = pl.BlockSpec(memory_space=pltpu.VMEM)
SMEM = pl.BlockSpec(memory_space=pltpu.SMEM)


def call(kernel, out_shape, in_specs, scratch=(), flops=0, moved=1 << 20):
    single = not isinstance(out_shape, (tuple, list))
    return pl.pallas_call(
        kernel,
        out_shape=out_shape,
        in_specs=in_specs,
        out_specs=VMEM if single else [VMEM] * len(out_shape),
        scratch_shapes=scratch,
        compiler_params=pltpu.CompilerParams(vmem_limit_bytes=24 << 20),
        cost_estimate=pl.CostEstimate(flops=flops, bytes_accessed=moved, transcendentals=0),
    )


def on_device(env_first, states, mpo, block_rows, present):
    sectors = lax.axis_size("sector")
    first, second, swap = rings(sectors)
    move = lambda value, pairs: lax.ppermute(value, AXES, pairs)
    core = lax.axis_index("chain")
    _, _, width, blk, _ = env_first.shape
    env_shape = (width, blk, blk)
    half = jax.ShapeDtypeStruct(env_shape, jnp.bfloat16)
    whole = jax.ShapeDtypeStruct(env_shape, jnp.float32)

    states, mpo, rows, here = states[0, :, :, 0], mpo[0], block_rows[0], present[0, :, 0]
    states_other, mpo_other, rows_other, other = (move(x, swap) for x in (states, mpo, rows, here))
    env = lax.dynamic_index_in_dim(env_first[:, 0], core, 0, keepdims=False)
    pair = jax.ShapeDtypeStruct((2, 2, blk, blk), jnp.bfloat16)
    local, send = call(prepare_kernel, [pair, pair], [SMEM, SMEM, VMEM, VMEM])(here, other, states, states_other)
    arriving = move(env, first)
    sent = move(send, first)

    envs = []
    for site in range(2):
        mine_q, mine_r = call(
            functools.partial(own_kernel, site), [half, half], [VMEM] * 4,
            [pltpu.VMEM((width, blk, 2 * blk), jnp.bfloat16)], 1 << 29,
        )(env, local, mpo, mpo_other)
        scratch = [pltpu.VMEM(env_shape, jnp.bfloat16)] * 2
        q = call(functools.partial(join_kernel, site, 0), half, [VMEM] * 6, scratch, 1 << 29)(
            arriving, local, sent, mpo, mpo_other, mine_q)
        arrived = move(q, second)
        r = call(functools.partial(join_kernel, site, 1), whole, [VMEM] * 6, scratch, 1 << 29)(
            arriving, local, sent, mpo, mpo_other, mine_r)
        env = call(functools.partial(sum_kernel, site), half, [SMEM, SMEM, VMEM, VMEM])(rows, rows_other, r, arrived)
        envs.append(env)
        if site == 0:
            arriving = move(env, first)

    own = jnp.where(core == 0, envs[0], envs[1])
    given = jnp.where(core == 0, envs[1], envs[0])
    taken = move(given, swap)
    result = jnp.stack([jnp.where(core == 0, own, taken), jnp.where(core == 0, taken, own)])
    return result[None, :, None]


def solution(mesh):
    placed = (
        P(None, "sector", None, None, None),
        P("chain", None, None, "sector", None, None),
        P("chain", None, None, None),
        P("chain", "sector"),
        P("chain", None, "sector"),
    )
    return jax.shard_map(
        on_device,
        mesh=mesh,
        in_specs=placed,
        out_specs=P("chain", None, "sector", None, None, None),
        check_vma=False,
    )
```

time: 196 us -> 52.9 us (0.27)
  the two profiles are of different devices: /device:TPU:25 before, /device:TPU:0 now
where the time goes in v1:
time: 52.9 us; the launch traced here: 52.7 us
  waiting for transfers between devices  31.4 us (59%)
  Pallas kernels  9.82 us (19%)
  starting transfers between devices  7.65 us (14%)
  local copies, waits for them, and re-layouts  1.9 us (4%)
  other arithmetic  1.19 us (2%)
  between operations  0.75 us (1%)
    ppermute x10, waiting for transfers between devices, on_device(): move = lambda value, pairs: lax.ppermute(value, AXES, pairs)  31.4 us
    ppermute x10, starting transfers between devices, on_device(): move = lambda value, pairs: lax.ppermute(value, AXES, pairs)  7.65 us
    pallas_call x2, Pallas kernels, on_device(): call(functools.partial(join_kernel, site, 0), half, [VMEM] * 6, scratch,...  2.92 us
    pallas_call x2, Pallas kernels, on_device(): call(functools.partial(own_kernel, site), [half, half], [VMEM] * 4, [pltp...  2.42 us
    pallas_call x2, Pallas kernels, on_device(): call(functools.partial(join_kernel, site, 1), whole, [VMEM] * 6, scratch,...  2.13 us
    unnamed x9, local copies, waits for them, and re-layouts  1.87 us
    pallas_call x2, Pallas kernels, on_device(): call(functools.partial(sum_kernel, site), half, [SMEM, SMEM, VMEM, VMEM])  1.71 us
  transfers between devices with their start and end apart: 10, of which 7 were waited for; matrix products, arithmetic and copies ran while one was open for 0% of the time, Pallas kernels for 10%

profile of v1, /device:TPU:0, one launch (start us, length us, event | category | flops | bytes accessed | tf_op | source)
XLA Modules:
  0.0 52.7 jit_solution(16819818005478332816)
XLA Ops:
  0.0 0.0 copy-start
  0.0 1.2 %copy-done = bf16[2,1,15,128,128]{4,3,2,1,0:T(8,128)(2,1)S(1)} copy-done((bf16[2,1,15,128,128]{4,3,2,1,0:T(8,128)(2,1)S(1)}, bf16[2,1,15,128,128]{4,3,2,1,0:T(8,128)(2,1)}, u32[]{:S(2)}) %copy-start) | copy-done | bytes 983064
  1.2 0.0 copy-start.1
  1.2 3.0 %collective-permute-start.1 = (bf16[15,128,128]{2,1,0:T(8,128)(2,1)S(1)}, bf16[15,128,128]{2,1,0:T(8,128)(2,1)S(1)}, u32[]{:S(2)}, u32[]{:S(2)}) collective-permute-start(bf16[15,128,128]{2,1,0:T(8,128)(2,1)S(1)} %dynamic-slice_bitcast_fusion.env), channel_id=1, source_target_pairs={{0,1},{1,2},{2,3},{3,0},{4,5},{5,6},{6,7},{7,4},{8,9},{9,10},{10,1... | collective-permute-start | bytes 1474568 | tf_op jit(solution)/shard_map/ppermute | solution.py:125
  4.2 0.0 copy-done.1
  4.2 0.0 copy-start.2
  4.2 0.0 collective-permute-start.3
  4.2 0.7 %copy-done.2 = s32[1,4,1]{1,2,0:T(1,128)S(1)} copy-done((s32[1,4,1]{1,2,0:T(1,128)S(1)}, s32[1,4,1]{1,2,0:T(1,128)}, u32[]{:S(2)}) %copy-start.2) | copy-done | bytes 40
  4.9 0.0 copy-start.3
  4.9 0.0 collective-permute-start.2
  4.9 1.1 %collective-permute-done.2.other = s32[4]{0:T(128)S(1)} collective-permute-done((s32[4]{0:T(128)S(1)}, s32[4]{0:T(128)S(1)}, u32[]{:S(2)}, u32[]{:S(2)}) %collective-permute-start.2) | collective-permute-done | bytes 48 | tf_op jit(solution)/shard_map/ppermute | solution.py:125
  6.0 0.0 collective-permute-done.3.states_other
  6.0 0.6 %shard_map.55 = (bf16[2,2,128,128]{3,2,1,0:T(8,128)(2,1)S(1)}, bf16[2,2,128,128]{3,2,1,0:T(8,128)(2,1)S(1)}) custom-call(s32[4]{0:T(128)S(1)} %bitcast.28, s32[4]{0:T(128)S(1)} %collective-permute-done.2.other, bf16[2,4,128,128]{3,2,1,0:T(8,128)(2,1)S(1)} %bitcast.19, bf16[2,4,128,128]{3,2,1,0:T(8,128)(2,1)S(1)} %collective-permute-done.3.states_other), custom_call_target="tpu_custom_call" | custom-call | bytes 1048576 | tf_op jit(solution)/shard_map/pallas_call | solution.py:136
  6.7 1.5 %collective-permute-start.4 = (bf16[2,2,128,128]{3,2,1,0:T(8,128)(2,1)S(1)}, bf16[2,2,128,128]{3,2,1,0:T(8,128)(2,1)S(1)}, u32[]{:S(2)}, u32[]{:S(2)}) collective-permute-start(bf16[2,2,128,128]{3,2,1,0:T(8,128)(2,1)S(1)} %get-tuple-element.12), channel_id=1, source_target_pairs={{0,1},{1,2},{2,3},{3,0},{4,5},{5,6},{6,7},{7,4},{8,9},{9,10},{10,1... | collective-permute-start | bytes 393224 | tf_op jit(solution)/shard_map/ppermute | solution.py:125
  8.2 0.0 copy-done.3
  8.2 0.1 collective-permute-start.5
  8.3 1.2 %collective-permute-done.5.mpo_other = bf16[4,15,15]{2,1,0:T(8,128)(2,1)S(1)} collective-permute-done((bf16[4,15,15]{2,1,0:T(8,128)(2,1)S(1)}, bf16[4,15,15]{2,1,0:T(8,128)(2,1)S(1)}, u32[]{:S(2)}, u32[]{:S(2)}) %collective-permute-start.5) | collective-permute-done | bytes 1832 | tf_op jit(solution)/shard_map/ppermute | solution.py:125
  9.5 1.2 %shard_map.56 = (bf16[15,128,128]{2,1,0:T(8,128)(2,1)S(1)}, bf16[15,128,128]{2,1,0:T(8,128)(2,1)S(1)}) custom-call(bf16[15,128,128]{2,1,0:T(8,128)(2,1)S(1)} %dynamic-slice_bitcast_fusion.env, bf16[2,2,128,128]{3,2,1,0:T(8,128)(2,1)S(1)} %get-tuple-element.11.local, bf16[4,15,15]{2,1,0:T(8,128)(2,1)S(1)} %bitcast.21, ...), custom_call_target="tpu_custom_call" | custom-call | flops 536870912 | bytes 1048576 | tf_op jit(solution)/shard_map/pallas_call | solution.py:142
  10.7 2.7 %collective-permute-done.4.sent = bf16[2,2,128,128]{3,2,1,0:T(8,128)(2,1)S(1)} collective-permute-done((bf16[2,2,128,128]{3,2,1,0:T(8,128)(2,1)S(1)}, bf16[2,2,128,128]{3,2,1,0:T(8,128)(2,1)S(1)}, u32[]{:S(2)}, u32[]{:S(2)}) %collective-permute-start.4) | collective-permute-done | bytes 131104 | tf_op jit(solution)/shard_map/ppermute | solution.py:125
  13.4 0.0 collective-permute-done.1.env
  13.4 1.1 %shard_map.58 = bf16[15,128,128]{2,1,0:T(8,128)(2,1)S(1)} custom-call(bf16[15,128,128]{2,1,0:T(8,128)(2,1)S(1)} %collective-permute-done.1.env, bf16[2,2,128,128]{3,2,1,0:T(8,128)(2,1)S(1)} %get-tuple-element.11.local, bf16[2,2,128,128]{3,2,1,0:T(8,128)(2,1)S(1)} %collective-permute-done.4.sent, bf16[4,15,15]{2,1,0:T(8,128)(2,1)S(1)} %bitcast.22, ...), custom_call_target="tpu_custom_call" | custom-call | flops 536870912 | bytes 1048576 | tf_op jit(solution)/shard_map/pallas_call | solution.py:147
  14.5 2.1 %collective-permute-start.6 = (bf16[15,128,128]{2,1,0:T(8,128)(2,1)S(1)}, bf16[15,128,128]{2,1,0:T(8,128)(2,1)S(1)}, u32[]{:S(2)}, u32[]{:S(2)}) collective-permute-start(bf16[15,128,128]{2,1,0:T(8,128)(2,1)S(1)} %shard_map.58), channel_id=1, source_target_pairs={{0,4},{1,5},{2,6},{3,7},{4,8},{5,9},{6,10},{7,11},{8,12},{9,13},{1... | collective-permute-start | bytes 1474568 | tf_op jit(solution)/shard_map/ppermute | solution.py:125
  16.6 0.0 collective-permute-start
  17.2 1.1 %shard_map.57.kept = f32[15,128,128]{2,1,0:T(8,128)S(1)} custom-call(bf16[15,128,128]{2,1,0:T(8,128)(2,1)S(1)} %collective-permute-done.1.env, bf16[2,2,128,128]{3,2,1,0:T(8,128)(2,1)S(1)} %get-tuple-element.11.local, bf16[2,2,128,128]{3,2,1,0:T(8,128)(2,1)S(1)} %collective-permute-done.4.sent, bf16[4,15,15]{2,1,0:T(8,128)(2,1)S(1)} %bitcast.23, ...), custom_call_target="tpu_custom_call" | custom-call | flops 536870912 | bytes 1048576 | tf_op jit(solution)/shard_map/pallas_call | solution.py:150
  18.3 0.0 collective-permute-done.rows_other
  18.3 7.1 %collective-permute-done.6.arrived = bf16[15,128,128]{2,1,0:T(8,128)(2,1)S(1)} collective-permute-done((bf16[15,128,128]{2,1,0:T(8,128)(2,1)S(1)}, bf16[15,128,128]{2,1,0:T(8,128)(2,1)S(1)}, u32[]{:S(2)}, u32[]{:S(2)}) %collective-permute-start.6) | collective-permute-done | bytes 491552 | tf_op jit(solution)/shard_map/ppermute | solution.py:125
  25.4 0.9 %shard_map.59.env = bf16[15,128,128]{2,1,0:T(8,128)(2,1)S(1)} custom-call(s32[1]{0:T(128)} %bitcast.16.rows, s32[1]{0:T(128)} %collective-permute-done.rows_other, f32[15,128,128]{2,1,0:T(8,128)S(1)} %shard_map.57.kept, bf16[15,128,128]{2,1,0:T(8,128)(2,1)S(1)} %collective-permute-done.6.arrived), custom_call_target="tpu_custom_call" | custom-call | bytes 1048576 | tf_op jit(solution)/shard_map/pallas_call | solution.py:152
  26.3 0.9 %collective-permute-start.7 = (bf16[15,128,128]{2,1,0:T(8,128)(2,1)S(1)}, bf16[15,128,128]{2,1,0:T(8,128)(2,1)S(1)}, u32[]{:S(2)}, u32[]{:S(2)}) collective-permute-start(bf16[15,128,128]{2,1,0:T(8,128)(2,1)S(1)} %shard_map.59.env), channel_id=1, source_target_pairs={{0,1},{1,2},{2,3},{3,0},{4,5},{5,6},{6,7},{7,4},{8,9},{9,10},{10,1... | collective-permute-start | bytes 1474568 | tf_op jit(solution)/shard_map/ppermute | solution.py:125
  27.1 1.2 %shard_map.60 = (bf16[15,128,128]{2,1,0:T(8,128)(2,1)S(1)}, bf16[15,128,128]{2,1,0:T(8,128)(2,1)S(1)}) custom-call(bf16[15,128,128]{2,1,0:T(8,128)(2,1)S(1)} %shard_map.59.env, bf16[2,2,128,128]{3,2,1,0:T(8,128)(2,1)S(1)} %get-tuple-element.11.local, bf16[4,15,15]{2,1,0:T(8,128)(2,1)S(1)} %bitcast.24, bf16[4,15,15]{2,1,0:T(8,128)(2,1)S(1)} %collective-permute-done.5.mpo_other), custom_call_target="tpu_custom_call" | custom-call | flops 536870912 | bytes 1048576 | tf_op jit(solution)/shard_map/pallas_call | solution.py:142
  28.4 7.7 %collective-permute-done.7.env = bf16[15,128,128]{2,1,0:T(8,128)(2,1)S(1)} collective-permute-done((bf16[15,128,128]{2,1,0:T(8,128)(2,1)S(1)}, bf16[15,128,128]{2,1,0:T(8,128)(2,1)S(1)}, u32[]{:S(2)}, u32[]{:S(2)}) %collective-permute-start.7) | collective-permute-done | bytes 491552 | tf_op jit(solution)/shard_map/ppermute | solution.py:125
  36.1 1.9 %shard_map.62 = bf16[15,128,128]{2,1,0:T(8,128)(2,1)} custom-call(bf16[15,128,128]{2,1,0:T(8,128)(2,1)S(1)} %collective-permute-done.7.env, bf16[2,2,128,128]{3,2,1,0:T(8,128)(2,1)S(1)} %get-tuple-element.11.local, bf16[2,2,128,128]{3,2,1,0:T(8,128)(2,1)S(1)} %collective-permute-done.4.sent, bf16[4,15,15]{2,1,0:T(8,128)(2,1)S(1)} %bitcast.25, ...), custom_call_target="tpu_custom_call" | custom-call | flops 536870912 | bytes 1048576 | tf_op jit(solution)/shard_map/pallas_call | solution.py:147
  37.9 0.0 collective-permute-start.8
  37.9 1.1 %shard_map.61.kept = f32[15,128,128]{2,1,0:T(8,128)S(1)} custom-call(bf16[15,128,128]{2,1,0:T(8,128)(2,1)S(1)} %collective-permute-done.7.env, bf16[2,2,128,128]{3,2,1,0:T(8,128)(2,1)S(1)} %get-tuple-element.11.local, bf16[2,2,128,128]{3,2,1,0:T(8,128)(2,1)S(1)} %collective-permute-done.4.sent, bf16[4,15,15]{2,1,0:T(8,128)(2,1)S(1)} %bitcast.26, ...), custom_call_target="tpu_custom_call" | custom-call | flops 536870912 | bytes 1048576 | tf_op jit(solution)/shard_map/pallas_call | solution.py:150
  39.0 9.8 %collective-permute-done.8.arrived = bf16[15,128,128]{2,1,0:T(8,128)(2,1)S(1)} collective-permute-done((bf16[15,128,128]{2,1,0:T(8,128)(2,1)}, bf16[15,128,128]{2,1,0:T(8,128)(2,1)S(1)}, u32[]{:S(2)}, u32[]{:S(2)}) %collective-permute-start.8) | collective-permute-done | bytes 491552 | tf_op jit(solution)/shard_map/ppermute | solution.py:125
  48.8 0.9 %shard_map.63 = bf16[15,128,128]{2,1,0:T(8,128)(2,1)S(1)} custom-call(s32[1]{0:T(128)} %bitcast.17.rows, s32[1]{0:T(128)} %collective-permute-done.rows_other, f32[15,128,128]{2,1,0:T(8,128)S(1)} %shard_map.61.kept, bf16[15,128,128]{2,1,0:T(8,128)(2,1)S(1)} %collective-permute-done.8.arrived), custom_call_target="tpu_custom_call" | custom-call | bytes 1048576 | tf_op jit(solution)/shard_map/pallas_call | solution.py:152
  49.6 0.1 broadcast_select_fusion
  49.7 0.1 collective-permute-start.9
  49.8 1.9 %collective-permute-done.9 = bf16[15,128,128]{2,1,0:T(8,128)(2,1)S(1)} collective-permute-done((bf16[15,128,128]{2,1,0:T(8,128)(2,1)S(1)}, bf16[15,128,128]{2,1,0:T(8,128)(2,1)S(1)}, u32[]{:S(2)}, u32[]{:S(2)}) %collective-permute-start.9) | collective-permute-done | bytes 491552 | tf_op jit(solution)/shard_map/ppermute | solution.py:125
  51.6 0.1 select_bitcast_fusion.1
  51.7 1.0 %maximum_bitcast_fusion = bf16[1,2,1,15,128,128]{5,4,3,2,1,0:T(8,128)(2,1)} fusion(bf16[1,15,128,128]{3,2,1,0:T(8,128)(2,1)S(1)} %get-tuple-element.18, bf16[1,15,128,128]{3,2,1,0:T(8,128)(2,1)S(1)} %get-tuple-element.17), kind=kLoop, calls=%fused_computation | loop fusion | flops 491520 | bytes 1966080 | tf_op jit(solution)/shard_map/broadcast_in_dim | solution.py:161
  (2 shorter events, 0.0 us)
Async XLA Ops:
  0.0 1.2 %copy-start = (bf16[2,1,15,128,128]{4,3,2,1,0:T(8,128)(2,1)S(1)}, bf16[2,1,15,128,128]{4,3,2,1,0:T(8,128)(2,1)}, u32[]{:S(2)}) copy-start(bf16[2,1,15,128,128]{4,3,2,1,0:T(8,128)(2,1)} %param.5) | copy-start | bytes 2949124
  1.2 3.0 %copy-start.1 = (bf16[1,2,4,1,128,128]{5,4,3,2,1,0:T(8,128)(2,1)S(1)}, bf16[1,2,4,1,128,128]{5,4,3,2,1,0:T(8,128)(2,1)}, u32[]{:S(2)}) copy-start(bf16[1,2,4,1,128,128]{5,4,3,2,1,0:T(8,128)(2,1)} %param.6) | copy-start | bytes 786436
  1.2 12.2 %collective-permute-start.1 = (bf16[15,128,128]{2,1,0:T(8,128)(2,1)S(1)}, bf16[15,128,128]{2,1,0:T(8,128)(2,1)S(1)}, u32[]{:S(2)}, u32[]{:S(2)}) collective-permute-start(bf16[15,128,128]{2,1,0:T(8,128)(2,1)S(1)} %dynamic-slice_bitcast_fusion.env), channel_id=1, source_target_pairs={{0,1},{1,2},{2,3},{3,0},{4,5},{5,6},{6,7},{7,4},{8,9},{9,10},{10,1... | collective-permute-start | bytes 1474568 | tf_op jit(solution)/shard_map/ppermute | solution.py:125
  4.2 0.7 %copy-start.2 = (s32[1,4,1]{1,2,0:T(1,128)S(1)}, s32[1,4,1]{1,2,0:T(1,128)}, u32[]{:S(2)}) copy-start(s32[1,4,1]{1,2,0:T(1,128)} %param.9) | copy-start | bytes 52
  4.2 1.8 %collective-permute-start.3 = (bf16[2,4,128,128]{3,2,1,0:T(8,128)(2,1)S(1)}, bf16[2,4,128,128]{3,2,1,0:T(8,128)(2,1)S(1)}, u32[]{:S(2)}, u32[]{:S(2)}) collective-permute-start(bf16[2,4,128,128]{3,2,1,0:T(8,128)(2,1)S(1)} %bitcast.18), channel_id=1, source_target_pairs={{0,16},{1,17},{2,18},{3,19},{4,20},{5,21},{6,22},{7,23},{8,24},{9,... | collective-permute-start | bytes 786440 | tf_op jit(solution)/shard_map/ppermute | solution.py:125
  4.9 3.3 %copy-start.3 = (bf16[1,4,15,15]{3,1,2,0:T(4,128)(2,1)S(1)}, bf16[1,4,15,15]{3,1,2,0:T(4,128)(2,1)}, u32[]{:S(2)}) copy-start(bf16[1,4,15,15]{3,1,2,0:T(4,128)(2,1)} %param.7) | copy-start | bytes 5404
  4.9 1.1 %collective-permute-start.2 = (s32[4]{0:T(128)S(1)}, s32[4]{0:T(128)S(1)}, u32[]{:S(2)}, u32[]{:S(2)}) collective-permute-start(s32[4]{0:T(128)S(1)} %bitcast.27), channel_id=1, source_target_pairs={{0,16},{1,17},{2,18},{3,19},{4,20},{5,21},{6,22},{7,23},{8,24},{9,... | collective-permute-start | bytes 56 | tf_op jit(solution)/shard_map/ppermute | solution.py:125
  6.7 6.7 %collective-permute-start.4 = (bf16[2,2,128,128]{3,2,1,0:T(8,128)(2,1)S(1)}, bf16[2,2,128,128]{3,2,1,0:T(8,128)(2,1)S(1)}, u32[]{:S(2)}, u32[]{:S(2)}) collective-permute-start(bf16[2,2,128,128]{3,2,1,0:T(8,128)(2,1)S(1)} %get-tuple-element.12), channel_id=1, source_target_pairs={{0,1},{1,2},{2,3},{3,0},{4,5},{5,6},{6,7},{7,4},{8,9},{9,10},{10,1... | collective-permute-start | bytes 393224 | tf_op jit(solution)/shard_map/ppermute | solution.py:125
  8.2 1.2 %collective-permute-start.5 = (bf16[4,15,15]{2,1,0:T(8,128)(2,1)S(1)}, bf16[4,15,15]{2,1,0:T(8,128)(2,1)S(1)}, u32[]{:S(2)}, u32[]{:S(2)}) collective-permute-start(bf16[4,15,15]{2,1,0:T(8,128)(2,1)S(1)} %bitcast.20), channel_id=1, source_target_pairs={{0,16},{1,17},{2,18},{3,19},{4,20},{5,21},{6,22},{7,23},{8,24},{9,... | collective-permute-start | bytes 5408 | tf_op jit(solution)/shard_map/ppermute | solution.py:125
  14.5 10.9 %collective-permute-start.6 = (bf16[15,128,128]{2,1,0:T(8,128)(2,1)S(1)}, bf16[15,128,128]{2,1,0:T(8,128)(2,1)S(1)}, u32[]{:S(2)}, u32[]{:S(2)}) collective-permute-start(bf16[15,128,128]{2,1,0:T(8,128)(2,1)S(1)} %shard_map.58), channel_id=1, source_target_pairs={{0,4},{1,5},{2,6},{3,7},{4,8},{5,9},{6,10},{7,11},{8,12},{9,13},{1... | collective-permute-start | bytes 1474568 | tf_op jit(solution)/shard_map/ppermute | solution.py:125
  16.6 1.7 %collective-permute-start = (s32[1]{0:T(128)}, s32[1]{0:T(128)}, u32[]{:S(2)}, u32[]{:S(2)}) collective-permute-start(s32[1]{0:T(128)} %bitcast), channel_id=1, source_target_pairs={{0,16},{1,17},{2,18},{3,19},{4,20},{5,21},{6,22},{7,23},{8,24},{9,... | collective-permute-start | bytes 20 | tf_op jit(solution)/shard_map/ppermute | solution.py:125
  26.3 9.8 %collective-permute-start.7 = (bf16[15,128,128]{2,1,0:T(8,128)(2,1)S(1)}, bf16[15,128,128]{2,1,0:T(8,128)(2,1)S(1)}, u32[]{:S(2)}, u32[]{:S(2)}) collective-permute-start(bf16[15,128,128]{2,1,0:T(8,128)(2,1)S(1)} %shard_map.59.env), channel_id=1, source_target_pairs={{0,1},{1,2},{2,3},{3,0},{4,5},{5,6},{6,7},{7,4},{8,9},{9,10},{10,1... | collective-permute-start | bytes 1474568 | tf_op jit(solution)/shard_map/ppermute | solution.py:125
  37.9 10.8 %collective-permute-start.8 = (bf16[15,128,128]{2,1,0:T(8,128)(2,1)}, bf16[15,128,128]{2,1,0:T(8,128)(2,1)S(1)}, u32[]{:S(2)}, u32[]{:S(2)}) collective-permute-start(bf16[15,128,128]{2,1,0:T(8,128)(2,1)} %shard_map.62), channel_id=1, source_target_pairs={{0,4},{1,5},{2,6},{3,7},{4,8},{5,9},{6,10},{7,11},{8,12},{9,13},{1... | collective-permute-start | bytes 1474568 | tf_op jit(solution)/shard_map/ppermute | solution.py:125
  49.7 1.9 %collective-permute-start.9 = (bf16[15,128,128]{2,1,0:T(8,128)(2,1)S(1)}, bf16[15,128,128]{2,1,0:T(8,128)(2,1)S(1)}, u32[]{:S(2)}, u32[]{:S(2)}) collective-permute-start(bf16[15,128,128]{2,1,0:T(8,128)(2,1)S(1)} %broadcast_select_fusion), channel_id=1, source_target_pairs={{0,16},{1,17},{2,18},{3,19},{4,20},{5,21},{6,22},{7,23},{8,24},{9,... | collective-permute-start | bytes 1474568 | tf_op jit(solution)/shard_map/ppermute | solution.py:125

commit v2 on v1

v2 whole, which is shorter than its diff:
```python
import functools

import jax
import jax.numpy as jnp
from jax import lax
from jax.experimental import pallas as pl
from jax.experimental.pallas import tpu as pltpu
from jax.sharding import PartitionSpec as P

QD = 4
LO = 16
AXES = ("chain", "sector")


def rings(sectors):
    down = lambda k: (k // QD) * QD + (k + 1) % QD
    up = lambda k: (k + QD) % sectors
    stay = lambda k: k

    def pairs(zero, one, cross):
        to_zero, to_one = (sectors, 0) if cross else (0, sectors)
        return [(k, to_zero + zero(k)) for k in range(sectors)] + [(sectors + k, to_one + one(k)) for k in range(sectors)]

    return pairs(down, up, False), pairs(up, down, False), pairs(up, down, True), pairs(stay, stay, True)


def place():
    core, sector = lax.axis_index("chain"), lax.axis_index("sector")
    return core, lax.rem(sector, QD) < QD - 1, lax.rem(sector, QD) > 0, sector >= QD


def target_of(site):
    core = lax.axis_index("chain")
    return core if site == 0 else 1 - core


def spreads(couplings):
    w = couplings[0].shape[0]
    rows = lax.broadcasted_iota(jnp.int32, (w * LO, w), 0) // LO
    pick = (rows == lax.broadcasted_iota(jnp.int32, (w * LO, w), 1)).astype(jnp.bfloat16)
    i = lax.broadcasted_iota(jnp.int32, (w * LO, w * LO), 0) % LO
    j = lax.broadcasted_iota(jnp.int32, (w * LO, w * LO), 1) % LO
    same = i == j

    def spread(mpo):
        tall = lax.dot_general(pick, mpo, (((1,), (1,)), ((), ())), preferred_element_type=jnp.float32).astype(jnp.bfloat16)
        full = lax.dot_general(tall, pick, (((1,), (1,)), ((), ())), preferred_element_type=jnp.float32)
        return jnp.where(same, full, 0.0).astype(jnp.bfloat16)

    return [spread(mpo) for mpo in couplings]


def couple(coupling, projected, column, out, lowest=0):
    count, blk = out.shape[0], out.shape[1]
    coupling = coupling[lowest * LO:(lowest + count) * LO]

    def part(a):
        pieces = [p[:, a:a + LO, column:column + blk].reshape(p.shape[0] * LO, blk) for p in projected]
        return pieces[0] if len(pieces) == 1 else jnp.concatenate(pieces, axis=0)

    for a in range(0, blk, 2 * LO):
        both = jnp.concatenate([part(a), part(a + LO)], axis=1)
        mixed = jnp.dot(coupling, both, preferred_element_type=jnp.float32).astype(out.dtype)
        out[:, a:a + LO, :] = mixed[:, :blk].reshape(count, LO, blk)
        out[:, a + LO:a + 2 * LO, :] = mixed[:, blk:].reshape(count, LO, blk)


def project(parts, counts, right, projected):
    slots = [(part, i) for part, count in zip(parts, counts) for i in range(count)]
    for w, (part, i) in enumerate(slots):
        projected[w] = jnp.dot(part[i], right, preferred_element_type=jnp.float32).astype(jnp.bfloat16)


def join(ours, theirs, mine, lowest, mixed, outs):
    left = jnp.concatenate([ours.T, theirs.T], axis=1)
    slots = [(out, i) for out in outs for i in range(out.shape[0])]
    blk = left.shape[0]
    for v in range(0, len(slots), 2):
        pair = range(v, min(v + 2, len(slots)))
        right = jnp.concatenate([jnp.concatenate([mine[lowest + u], mixed[u]], axis=0) for u in pair], axis=1)
        both = jnp.dot(left, right, preferred_element_type=jnp.float32)
        for n, u in enumerate(pair):
            out, i = slots[u]
            out[i] = both[:, n * blk:(n + 1) * blk].astype(out.dtype)


def prepare_kernel(here, other, rows, rows_other, states, states_other, local, send, send_later, live):
    core, inside, _, _ = place()

    def block(site, state, choice):
        same, target = core == site, target_of(site)

        def exists(k):
            flag = jnp.where(same, here[:, k:k + 1], other[:, k:k + 1]) > 0
            return flag & inside if k >= 2 else flag

        def of(k):
            both = jnp.where(same, states[target, k], states_other[target, k])
            return jnp.where(exists(k), both, jnp.zeros_like(both))

        return of(state) if state == choice else jnp.where(target == 0, of(state), of(choice))

    for site, out in enumerate((send, send_later)):
        out[0] = block(site, 3, 3)
        out[1] = block(site, 2, 1)
        local[site, 0] = block(site, 1, 2)
        local[site, 1] = block(site, 0, 0)
        live[site] = jnp.broadcast_to(jnp.where(core == site, rows[...], rows_other[...]), live.shape[1:])


def behind(site, sent):
    _, _, from_down, from_up = place()
    valid = jnp.where(target_of(site) == 0, from_down, from_up)
    return jnp.where(valid, sent, jnp.zeros_like(sent))


def own_kernel(site, counts, local, mpo, mpo_other, *refs):
    *parts, out_q, out_r, out_spread, projected = refs
    core = lax.axis_index("chain")
    right = jnp.concatenate([local[site, 0], local[site, 1]], axis=1)
    project(parts, counts, right, projected)
    pick = lambda state: jnp.where(core == site, mpo[state], mpo_other[state])
    target = target_of(site)
    middle, zero, both, outer = spreads([pick(1 + target), pick(0), pick(3), pick(2 - target)])
    couple(middle, [projected], 0, out_q)
    couple(zero, [projected], out_q.shape[1], out_r)
    out_spread[0] = both
    out_spread[1] = outer


def project_kernel(site, at, sent, part, projected):
    project([part], projected.shape[:1], behind(site, sent[at]), projected)


def head_kernel(site, at, local, sent, spread, mine, *refs):
    *projected, part, out, mine_projected, mixed = refs
    theirs = behind(site, sent[at])
    project([part], mine_projected.shape[:1], theirs, mine_projected)
    couple(spread[0], [*projected, mine_projected], 0, mixed)
    join(local[site, 0], theirs, mine, 0, mixed, [out])


def tail_kernel(site, at, local, sent, spread, mine, *refs):
    *projected, out, mixed = refs
    lowest = mine.shape[0] - out.shape[0]
    couple(spread[0], projected, 0, mixed, lowest)
    join(local[site, 0], behind(site, sent[at]), mine, lowest, mixed, [out])


def keep_kernel(site, at, counts, local, sent, spread, mine, after, *refs):
    parts, outs, (projected, mixed) = refs[:len(counts)], refs[len(counts):-2], refs[-2:]
    theirs = behind(site, sent[at + 1])
    project(parts, counts, theirs, projected)
    couple(spread[1], [projected], 0, mixed)
    join(local[site, 1], theirs, mine, 0, mixed, outs)


def total(site, live, kept, arrived, lowest, v):
    core, _, from_down, from_up = place()
    valid = jnp.where(core == 0, from_down, from_up)
    kept, at = [(part, i) for part in kept for i in range(part.shape[0])][lowest + v]
    blk = kept.shape[1]
    rows = live[site, 0:1, :]
    inside = (lax.broadcasted_iota(jnp.int32, (blk, blk), 0) < rows) & (lax.broadcasted_iota(jnp.int32, (blk, blk), 1) < rows)
    both = kept[at].astype(jnp.float32) + jnp.where(valid, arrived[v].astype(jnp.float32), 0.0)
    return jnp.where(inside, both, 0.0).astype(jnp.bfloat16)


def sum_kernel(lowest, pieces, live, arrived, *refs):
    kept, more, out = refs[:pieces], refs[pieces:-1], refs[-1]
    count = arrived.shape[0]
    for v in range(count):
        out[v] = total(0, live, kept, arrived, lowest, v)
    for blocks in more:
        for i in range(blocks.shape[0]):
            out[count + i] = blocks[i]


def last_kernel(live, arrived, kept, before, stays, given):
    core = lax.axis_index("chain")
    for v in range(stays.shape[0]):
        new, old = total(1, live, [kept], arrived, 0, v), before[v]
        stays[v] = jnp.where(core == 0, old, new)
        given[v] = jnp.where(core == 0, new, old)


def copy_all(copies, sems):
    copies = [pltpu.make_async_copy(source, target, sems.at[i]) for i, (source, target) in enumerate(copies)]
    for copy in copies:
        copy.start()
    for copy in copies:
        copy.wait()


def write_kernel(stays_head, stays_tail, taken_head, out, sems):
    core = lax.axis_index("chain")
    n, m = stays_head.shape[0], stays_tail.shape[0]
    copy_all([
        (stays_head, out.at[1 - core, pl.ds(0, n)]),
        (stays_tail, out.at[1 - core, pl.ds(n, m)]),
        (taken_head, out.at[core, pl.ds(0, n)]),
    ], sems)


def finish_kernel(begun, taken_tail, out, sems):
    core = lax.axis_index("chain")
    m = taken_tail.shape[0]
    copy_all([(taken_tail, out.at[core, pl.ds(out.shape[1] - m, m)])], sems)


VMEM = pl.BlockSpec(memory_space=pltpu.VMEM)
SMEM = pl.BlockSpec(memory_space=pltpu.SMEM)


def call(kernel, out_shape, in_specs, scratch=(), flops=0, moved=1):
    single = not isinstance(out_shape, (tuple, list))
    return pl.pallas_call(
        kernel,
        out_shape=out_shape,
        in_specs=in_specs,
        out_specs=VMEM if single else [VMEM] * len(out_shape),
        scratch_shapes=scratch,
        compiler_params=pltpu.CompilerParams(vmem_limit_bytes=24 << 20),
        cost_estimate=pl.CostEstimate(flops=1, bytes_accessed=1, transcendentals=0),
    )


def on_device(env_first, states, mpo, block_rows, present):
    sectors = lax.axis_size("sector")
    first, second, cross, swap = rings(sectors)
    move = lambda value, pairs: lax.ppermute(value, AXES, pairs)
    core = lax.axis_index("chain")
    _, _, width, blk, _ = env_first.shape
    env_shape = (width, blk, blk)
    lengths = (-(-width // 2), width // 2)
    array = lambda *shape, dtype=jnp.bfloat16: jax.ShapeDtypeStruct(shape, dtype)
    scratch = lambda n, m=1: pltpu.VMEM((n, blk, m * blk), jnp.bfloat16)
    half = array(*env_shape)
    pieces = [array(n, blk, blk) for n in lengths]
    wide = [array(n, blk, blk, dtype=jnp.float32) for n in lengths]
    small = [array(len(range(i, min(i + 5, width))), blk, blk) for i in range(0, width, 5)]

    states, mpo, rows, here = states[0, :, :, 0], mpo[0], block_rows, present[:, :, 0]
    parts = [lax.dynamic_index_in_dim(env_first[:, 0], core, 0, keepdims=False)]
    arriving = [move(part, first) for part in parts]
    states_other, mpo_other, rows_other, other = lax.optimization_barrier(tuple(move(x, swap) for x in (states, mpo, rows, here)))
    pair = array(2, blk, blk)
    local, send, send_later, live = call(
        prepare_kernel, [array(2, 2, blk, blk), pair, pair, array(2, 8, blk, dtype=jnp.int32)], [VMEM] * 6,
    )(here, other, rows, rows_other, states, states_other)
    sent = move(send, first)

    for site in range(2):
        counts, at = ((width,), 0) if site == 0 else (lengths, lengths[0])
        mine_q, mine_r, spread = call(
            functools.partial(own_kernel, site, counts), [half, half, array(2, width * LO, width * LO)], [VMEM] * (3 + len(parts)),
            [scratch(width, 2)], 1 << 29,
        )(local, mpo, mpo_other, *parts)
        projected = [
            call(functools.partial(project_kernel, site, at), array(count, blk, blk), [VMEM] * 2, (), 1 << 27)(sent, part)
            for part, count in zip(arriving[:-1], counts)
        ]
        q_head, last = call(
            functools.partial(head_kernel, site, at), [pieces[0], array(counts[-1], blk, blk)],
            [VMEM] * (5 + len(projected)), [scratch(lengths[0])], 1 << 28,
        )(local, sent, spread, mine_q, *projected, arriving[-1])
        projected.append(last)
        q_tail = call(
            functools.partial(tail_kernel, site, at), pieces[1], [VMEM] * (4 + len(projected)), [scratch(lengths[1])], 1 << 27,
        )(local, sent, spread, mine_q, *projected)
        arrived = [move(q, cross if site == 0 else first) for q in (q_head, q_tail)]
        kept = call(
            functools.partial(keep_kernel, site, at, counts), wide if site else small, [VMEM] * (5 + len(arriving)), [scratch(width)] * 2, 1 << 29,
        )(local, sent, spread, mine_r, q_tail, *arriving)
        if site == 0:
            kept = [move(part, swap) for part in kept]
            longer = array(lengths[0] + 2, blk, blk)
            parts = [
                call(functools.partial(sum_kernel, 0, len(kept)), longer, [VMEM] * (3 + len(kept)))(live, arrived[0], *kept, send_later),
                call(functools.partial(sum_kernel, lengths[0], len(kept)), pieces[1], [VMEM] * (2 + len(kept)))(live, arrived[1], *kept),
            ]
            arriving = [move(part, second) for part in parts]
            sent = arriving[0]
        else:
            both = [call(last_kernel, [pieces[i]] * 2, [VMEM] * 4)(live, arrived[i], kept[i], parts[i]) for i in range(2)]
    (stays_head, given_head), (stays_tail, given_tail) = both
    taken_head, taken_tail = move(given_head, swap), move(given_tail, swap)
    whole = array(2, *env_shape)
    hbm = pl.BlockSpec(memory_space=pl.ANY)
    params = pltpu.CompilerParams(vmem_limit_bytes=24 << 20)
    result = pl.pallas_call(
        write_kernel, out_shape=whole, in_specs=[VMEM] * 3, out_specs=hbm,
        scratch_shapes=[pltpu.SemaphoreType.DMA((3,))], compiler_params=params,
    )(stays_head, stays_tail, taken_head)
    result = pl.pallas_call(
        finish_kernel, out_shape=whole, in_specs=[hbm, VMEM], out_specs=hbm, input_output_aliases={0: 0},
        scratch_shapes=[pltpu.SemaphoreType.DMA((1,))], compiler_params=params,
    )(result, taken_tail)
    return result[None, :, None]


def solution(mesh):
    placed = (
        P(None, "sector", None, None, None),
        P("chain", None, None, "sector", None, None),
        P("chain", None, None, None),
        P("chain", "sector"),
        P("chain", None, "sector"),
    )
    return jax.shard_map(
        on_device,
        mesh=mesh,
        in_specs=placed,
        out_specs=P("chain", None, "sector", None, None, None),
        check_vma=False,
    )
```

time: 52.9 us -> 45 us (0.85)
  waiting for transfers between devices: 31.4 us -> 17.6 us
  starting transfers between devices: 7.65 us -> 15.9 us
  other arithmetic: 1.19 us -> 0 us
  Pallas kernels: 9.82 us -> 9.21 us
  local copies, waits for them, and re-layouts: 1.9 us -> 1.34 us
    ppermute x10 -> x17, waiting for transfers between devices: 31.4 us -> 17.6 us  [on_device(): move = lambda value, pairs: lax.ppermute(value, AXES, pairs)]
    ppermute x10 -> x17, starting transfers between devices: 7.65 us -> 15.9 us  [on_device(): move = lambda value, pairs: lax.ppermute(value, AXES, pairs)]
    broadcast_in_dim x1 -> x0, other arithmetic: 1.03 us -> none  [on_device(): return result[None, :, None]]
    pallas_call x9 -> x16, Pallas kernels: 9.82 us -> 9.21 us  [the longest x2 2.1 us: on_device(): call(functools.partial(own_kernel, site, counts), [half, half, array(2, w...]
    unnamed x9, local copies, waits for them, and re-layouts: 1.87 us -> 1.31 us
  transfers between devices with their start and end apart: 10 -> 17, of which waited for: 7 -> 9; matrix products, arithmetic and copies ran while one was open for 0% -> 0% of each run, Pallas kernels for 10% -> 16%
where the time goes in v2:
time: 45 us; the launch traced here: 44.8 us
  waiting for transfers between devices  17.6 us (39%)
  starting transfers between devices  15.9 us (35%)
  Pallas kernels  9.21 us (20%)
  local copies, waits for them, and re-layouts  1.34 us (3%)
  between operations  0.82 us (2%)
    ppermute x17, waiting for transfers between devices, on_device(): move = lambda value, pairs: lax.ppermute(value, AXES, pairs)  17.6 us
    ppermute x17, starting transfers between devices, on_device(): move = lambda value, pairs: lax.ppermute(value, AXES, pairs)  15.9 us
    pallas_call x2, Pallas kernels, on_device(): call(functools.partial(own_kernel, site, counts), [half, half, array(2, w...  2.1 us
    pallas_call x2, Pallas kernels, on_device(): call(functools.partial(keep_kernel, site, at, counts), wide if site else...  1.67 us
    pallas_call x2, Pallas kernels, on_device(): call(functools.partial(head_kernel, site, at), [pieces[0], array(counts[-...  1.36 us
    unnamed x9, local copies, waits for them, and re-layouts  1.31 us
    pallas_call x1, Pallas kernels, on_device(): pl.pallas_call(write_kernel, out_shape=whole, in_specs=[VMEM] * 3, out_sp...  0.9 us
  transfers between devices with their start and end apart: 17, of which 9 were waited for; matrix products, arithmetic and copies ran while one was open for 0% of the time, Pallas kernels for 16%

profile of v2, /device:TPU:0, one launch (start us, length us, event | category | flops | bytes accessed | tf_op | source)
XLA Modules:
  0.0 44.8 jit_solution(3215465735419500294)
XLA Ops:
  0.0 1.2 %copy-done = bf16[2,1,15,128,128]{4,3,2,1,0:T(8,128)(2,1)S(1)} copy-done((bf16[2,1,15,128,128]{4,3,2,1,0:T(8,128)(2,1)S(1)}, bf16[2,1,15,128,128]{4,3,2,1,0:T(8,128)(2,1)}, u32[]{:S(2)}) %copy-start) | copy-done | bytes 983064
  1.2 3.0 %collective-permute-start.5 = (bf16[15,128,128]{2,1,0:T(8,128)(2,1)S(1)}, bf16[15,128,128]{2,1,0:T(8,128)(2,1)S(1)}, u32[]{:S(2)}, u32[]{:S(2)}) collective-permute-start(bf16[15,128,128]{2,1,0:T(8,128)(2,1)S(1)} %dynamic-slice_bitcast_fusion.refs_0_), channel_id=1, source_target_pairs={{0,1},{1,2},{2,3},{3,0},{4,5},{5,6},{6,7},{7,4},{8,9},{9,10},{10,1... | collective-permute-start | bytes 1474568 | tf_op jit(solution)/shard_map/ppermute | solution.py:231
  4.2 0.0 collective-permute-start
  4.3 0.0 copy-start.2
  4.3 0.6 %collective-permute-start.1 = (bf16[4,15,15]{2,1,0:T(8,128)(2,1)S(1)}, bf16[4,15,15]{2,1,0:T(8,128)(2,1)S(1)}, u32[]{:S(2)}, u32[]{:S(2)}) collective-permute-start(bf16[4,15,15]{2,1,0:T(8,128)(2,1)S(1)} %bitcast.12), channel_id=1, source_target_pairs={{0,16},{1,17},{2,18},{3,19},{4,20},{5,21},{6,22},{7,23},{8,24},{9,... | collective-permute-start | bytes 5408 | tf_op jit(solution)/shard_map/ppermute | solution.py:231
  4.8 0.1 copy-done.2
  4.9 0.5 %collective-permute-start.3 = (s32[1,4]{1,0:T(1,128)S(1)}, s32[1,4]{1,0:T(1,128)S(1)}, u32[]{:S(2)}, u32[]{:S(2)}) collective-permute-start(s32[1,4]{1,0:T(1,128)S(1)} %bitcast.15), channel_id=1, source_target_pairs={{0,16},{1,17},{2,18},{3,19},{4,20},{5,21},{6,22},{7,23},{8,24},{9,... | collective-permute-start | bytes 56 | tf_op jit(solution)/shard_map/ppermute | solution.py:231
  5.4 0.0 collective-permute-start.2
  6.1 0.7 %collective-permute-done.2.rows_other = s32[1,1]{1,0:T(1,128)} collective-permute-done((s32[1,1]{1,0:T(1,128)}, s32[1,1]{1,0:T(1,128)}, u32[]{:S(2)}, u32[]{:S(2)}) %collective-permute-start.2) | collective-permute-done | bytes 36 | tf_op jit(solution)/shard_map/ppermute | solution.py:231
  6.8 0.8 %shard_map.55 = (bf16[2,2,128,128]{3,2,1,0:T(8,128)(2,1)S(1)}, bf16[2,128,128]{2,1,0:T(8,128)(2,1)S(1)}, bf16[2,128,128]{2,1,0:T(8,128)(2,1)S(1)}, s32[2,8,128]{2,1,0:T(8,128)S(1)}) custom-call(s32[1,4]{1,0:T(1,128)S(1)} %bitcast.16, s32[1,4]{1,0:T(1,128)S(1)} %collective-permute-done.3.other, s32[1,1]{1,0:T(1,128)S(6)} %copy.12.rows, ...), custom_call_target="tpu_custom_call" | custom-call | flops 1 | bytes 1 | tf_op jit(solution)/shard_map/pallas_call | solution.py:248
  7.6 1.5 %collective-permute-start.4 = (bf16[2,128,128]{2,1,0:T(8,128)(2,1)S(1)}, bf16[2,128,128]{2,1,0:T(8,128)(2,1)S(1)}, u32[]{:S(2)}, u32[]{:S(2)}) collective-permute-start(bf16[2,128,128]{2,1,0:T(8,128)(2,1)S(1)} %get-tuple-element.37), channel_id=1, source_target_pairs={{0,1},{1,2},{2,3},{3,0},{4,5},{5,6},{6,7},{7,4},{8,9},{9,10},{10,1... | collective-permute-start | bytes 196616 | tf_op jit(solution)/shard_map/ppermute | solution.py:231
  9.1 1.0 %shard_map.56 = (bf16[15,128,128]{2,1,0:T(8,128)(2,1)S(1)}, bf16[15,128,128]{2,1,0:T(8,128)(2,1)S(1)}, bf16[2,240,240]{2,1,0:T(8,128)(2,1)S(1)}) custom-call(bf16[2,2,128,128]{3,2,1,0:T(8,128)(2,1)S(1)} %get-tuple-element.36.local, bf16[4,15,15]{2,1,0:T(8,128)(2,1)S(1)} %bitcast.13, bf16[4,15,15]{2,1,0:T(8,128)(2,1)S(1)} %collective-permute-done.1.mpo_other, ...), custom_call_target="tpu_custom_call" | custom-call | flops 1 | bytes 1 | tf_op jit(solution)/shard_map/pallas_call | solution.py:255
  10.2 2.6 %collective-permute-done.4.sent = bf16[2,128,128]{2,1,0:T(8,128)(2,1)S(1)} collective-permute-done((bf16[2,128,128]{2,1,0:T(8,128)(2,1)S(1)}, bf16[2,128,128]{2,1,0:T(8,128)(2,1)S(1)}, u32[]{:S(2)}, u32[]{:S(2)}) %collective-permute-start.4) | collective-permute-done | bytes 65568 | tf_op jit(solution)/shard_map/ppermute | solution.py:231
  12.8 0.0 collective-permute-done.5.refs_0_
  12.8 0.7 %shard_map.57 = (bf16[8,128,128]{2,1,0:T(8,128)(2,1)S(1)}, bf16[15,128,128]{2,1,0:T(8,128)(2,1)S(1)}) custom-call(bf16[2,2,128,128]{3,2,1,0:T(8,128)(2,1)S(1)} %get-tuple-element.36.local, bf16[2,128,128]{2,1,0:T(8,128)(2,1)S(1)} %collective-permute-done.4.sent, bf16[2,240,240]{2,1,0:T(8,128)(2,1)S(1)} %get-tuple-element.39.spread, ...), custom_call_target="tpu_custom_call" | custom-call | flops 1 | bytes 1 | tf_op jit(solution)/shard_map/pallas_call | solution.py:263
  13.5 0.1 collective-permute-start.6
  13.6 0.4 shard_map.58.after
  14.0 0.8 %shard_map.59 = (bf16[5,128,128]{2,1,0:T(8,128)(2,1)S(1)}, bf16[5,128,128]{2,1,0:T(8,128)(2,1)S(1)}, bf16[5,128,128]{2,1,0:T(8,128)(2,1)S(1)}) custom-call(bf16[2,2,128,128]{3,2,1,0:T(8,128)(2,1)S(1)} %get-tuple-element.36.local, bf16[2,128,128]{2,1,0:T(8,128)(2,1)S(1)} %collective-permute-done.4.sent, bf16[2,240,240]{2,1,0:T(8,128)(2,1)S(1)} %get-tuple-element.39.spread, ...), custom_call_target="tpu_custom_call" | custom-call | flops 1 | bytes 1 | tf_op jit(solution)/shard_map/pallas_call | solution.py:272
  14.9 1.1 %collective-permute-start.7 = (bf16[5,128,128]{2,1,0:T(8,128)(2,1)S(1)}, bf16[5,128,128]{2,1,0:T(8,128)(2,1)S(1)}, u32[]{:S(2)}, u32[]{:S(2)}) collective-permute-start(bf16[5,128,128]{2,1,0:T(8,128)(2,1)S(1)} %get-tuple-element.44), channel_id=1, source_target_pairs={{0,16},{1,17},{2,18},{3,19},{4,20},{5,21},{6,22},{7,23},{8,24},{9,... | collective-permute-start | bytes 491528 | tf_op jit(solution)/shard_map/ppermute | solution.py:231
  16.0 0.1 collective-permute-start.8
  16.1 0.4 collective-permute-start.9
  16.5 1.3 %collective-permute-start.11 = (bf16[7,128,128]{2,1,0:T(8,128)(2,1)S(1)}, bf16[7,128,128]{2,1,0:T(8,128)(2,1)S(1)}, u32[]{:S(2)}, u32[]{:S(2)}) collective-permute-start(bf16[7,128,128]{2,1,0:T(8,128)(2,1)S(1)} %shard_map.58.after), channel_id=1, source_target_pairs={{0,20},{1,21},{2,22},{3,23},{4,24},{5,25},{6,26},{7,27},{8,28},{9,... | collective-permute-start | bytes 688136 | tf_op jit(solution)/shard_map/ppermute | solution.py:231
  17.8 0.0 collective-permute-done.7.refs_0_
  17.8 0.0 collective-permute-done.8.refs_1_
  17.8 2.5 %collective-permute-done.6.arrived = bf16[8,128,128]{2,1,0:T(8,128)(2,1)S(1)} collective-permute-done((bf16[8,128,128]{2,1,0:T(8,128)(2,1)S(1)}, bf16[8,128,128]{2,1,0:T(8,128)(2,1)S(1)}, u32[]{:S(2)}, u32[]{:S(2)}) %collective-permute-start.6) | collective-permute-done | bytes 262176 | tf_op jit(solution)/shard_map/ppermute | solution.py:231
  20.3 0.1 shard_map.60.refs_0_.before
  20.4 2.0 %collective-permute-start.10 = (bf16[10,128,128]{2,1,0:T(8,128)(2,1)S(1)}, bf16[10,128,128]{2,1,0:T(8,128)(2,1)S(1)}, u32[]{:S(2)}, u32[]{:S(2)}) collective-permute-start(bf16[10,128,128]{2,1,0:T(8,128)(2,1)S(1)} %shard_map.60.refs_0_.before), channel_id=1, source_target_pairs={{0,4},{1,5},{2,6},{3,7},{4,8},{5,9},{6,10},{7,11},{8,12},{9,13},{1... | collective-permute-start | bytes 983048 | tf_op jit(solution)/shard_map/ppermute | solution.py:231
  22.4 0.4 collective-permute-done.11.arrived
  22.9 0.1 shard_map.61.refs_1_.before
  23.0 1.9 %collective-permute-start.12 = (bf16[7,128,128]{2,1,0:T(8,128)(2,1)S(1)}, bf16[7,128,128]{2,1,0:T(8,128)(2,1)S(1)}, u32[]{:S(2)}, u32[]{:S(2)}) collective-permute-start(bf16[7,128,128]{2,1,0:T(8,128)(2,1)S(1)} %shard_map.61.refs_1_.before), channel_id=1, source_target_pairs={{0,4},{1,5},{2,6},{3,7},{4,8},{5,9},{6,10},{7,11},{8,12},{9,13},{1... | collective-permute-start | bytes 688136 | tf_op jit(solution)/shard_map/ppermute | solution.py:231
  24.9 1.0 %shard_map.62 = (bf16[15,128,128]{2,1,0:T(8,128)(2,1)S(1)}, bf16[15,128,128]{2,1,0:T(8,128)(2,1)S(1)}, bf16[2,240,240]{2,1,0:T(8,128)(2,1)S(1)}) custom-call(bf16[2,2,128,128]{3,2,1,0:T(8,128)(2,1)S(1)} %get-tuple-element.36.local, bf16[4,15,15]{2,1,0:T(8,128)(2,1)S(1)} %bitcast.14, bf16[4,15,15]{2,1,0:T(8,128)(2,1)S(1)} %collective-permute-done.1.mpo_other, ...), custom_call_target="tpu_custom_call" | custom-call | flops 1 | bytes 1 | tf_op jit(solution)/shard_map/pallas_call | solution.py:255
  25.9 3.6 %collective-permute-done.10.sent.part.refs_0_ = bf16[10,128,128]{2,1,0:T(8,128)(2,1)S(1)} collective-permute-done((bf16[10,128,128]{2,1,0:T(8,128)(2,1)S(1)}, bf16[10,128,128]{2,1,0:T(8,128)(2,1)S(1)}, u32[]{:S(2)}, u32[]{:S(2)}) %collective-permute-start.10) | collective-permute-done | bytes 327712 | tf_op jit(solution)/shard_map/ppermute | solution.py:231
  29.5 0.2 shard_map.63.refs_0_
  29.8 2.2 %collective-permute-done.12.refs_1_ = bf16[7,128,128]{2,1,0:T(8,128)(2,1)S(1)} collective-permute-done((bf16[7,128,128]{2,1,0:T(8,128)(2,1)S(1)}, bf16[7,128,128]{2,1,0:T(8,128)(2,1)S(1)}, u32[]{:S(2)}, u32[]{:S(2)}) %collective-permute-start.12) | collective-permute-done | bytes 229408 | tf_op jit(solution)/shard_map/ppermute | solution.py:231
  32.0 0.6 %shard_map.64 = (bf16[8,128,128]{2,1,0:T(8,128)(2,1)S(1)}, bf16[7,128,128]{2,1,0:T(8,128)(2,1)S(1)}) custom-call(bf16[2,2,128,128]{3,2,1,0:T(8,128)(2,1)S(1)} %get-tuple-element.36.local, bf16[10,128,128]{2,1,0:T(8,128)(2,1)S(1)} %collective-permute-done.10.sent.part.refs_0_, bf16[2,240,240]{2,1,0:T(8,128)(2,1)S(1)} %get-tuple-element.48.spread, ...), custom_call_target="tpu_custom_call" | custom-call | flops 1 | bytes 1 | tf_op jit(solution)/shard_map/pallas_call | solution.py:263
  32.6 0.6 %collective-permute-start.13 = (bf16[8,128,128]{2,1,0:T(8,128)(2,1)S(1)}, bf16[8,128,128]{2,1,0:T(8,128)(2,1)S(1)}, u32[]{:S(2)}, u32[]{:S(2)}) collective-permute-start(bf16[8,128,128]{2,1,0:T(8,128)(2,1)S(1)} %get-tuple-element.50), channel_id=1, source_target_pairs={{0,1},{1,2},{2,3},{3,0},{4,5},{5,6},{6,7},{7,4},{8,9},{9,10},{10,1... | collective-permute-start | bytes 786440 | tf_op jit(solution)/shard_map/ppermute | solution.py:231
  33.2 0.4 shard_map.65.after
  33.6 2.7 %collective-permute-start.14 = (bf16[7,128,128]{2,1,0:T(8,128)(2,1)S(1)}, bf16[7,128,128]{2,1,0:T(8,128)(2,1)S(1)}, u32[]{:S(2)}, u32[]{:S(2)}) collective-permute-start(bf16[7,128,128]{2,1,0:T(8,128)(2,1)S(1)} %shard_map.65.after), channel_id=1, source_target_pairs={{0,1},{1,2},{2,3},{3,0},{4,5},{5,6},{6,7},{7,4},{8,9},{9,10},{10,1... | collective-permute-start | bytes 688136 | tf_op jit(solution)/shard_map/ppermute | solution.py:231
  36.3 0.8 %shard_map.66 = (f32[8,128,128]{2,1,0:T(8,128)S(1)}, f32[7,128,128]{2,1,0:T(8,128)S(1)}) custom-call(bf16[2,2,128,128]{3,2,1,0:T(8,128)(2,1)S(1)} %get-tuple-element.36.local, bf16[10,128,128]{2,1,0:T(8,128)(2,1)S(1)} %collective-permute-done.10.sent.part.refs_0_, bf16[2,240,240]{2,1,0:T(8,128)(2,1)S(1)} %get-tuple-element.48.spread, ...), custom_call_target="tpu_custom_call" | custom-call | flops 1 | bytes 1 | tf_op jit(solution)/shard_map/pallas_call | solution.py:272
  37.2 2.8 %collective-permute-done.13.arrived = bf16[8,128,128]{2,1,0:T(8,128)(2,1)S(1)} collective-permute-done((bf16[8,128,128]{2,1,0:T(8,128)(2,1)S(1)}, bf16[8,128,128]{2,1,0:T(8,128)(2,1)S(1)}, u32[]{:S(2)}, u32[]{:S(2)}) %collective-permute-start.13) | collective-permute-done | bytes 262176 | tf_op jit(solution)/shard_map/ppermute | solution.py:231
  39.9 0.2 shard_map.67
  40.1 0.1 collective-permute-start.15
  40.2 2.2 %collective-permute-done.14.arrived = bf16[7,128,128]{2,1,0:T(8,128)(2,1)S(1)} collective-permute-done((bf16[7,128,128]{2,1,0:T(8,128)(2,1)S(1)}, bf16[7,128,128]{2,1,0:T(8,128)(2,1)S(1)}, u32[]{:S(2)}, u32[]{:S(2)}) %collective-permute-start.14) | collective-permute-done | bytes 229408 | tf_op jit(solution)/shard_map/ppermute | solution.py:231
  42.4 0.2 shard_map.68
  42.6 0.1 collective-permute-start.16
  42.7 0.9 %shard_map.69.begun = bf16[2,15,128,128]{3,2,1,0:T(8,128)(2,1)} custom-call(bf16[8,128,128]{2,1,0:T(8,128)(2,1)S(1)} %get-tuple-element.54.stays_head, bf16[7,128,128]{2,1,0:T(8,128)(2,1)S(1)} %get-tuple-element.56.stays_tail, bf16[8,128,128]{2,1,0:T(8,128)(2,1)S(1)} %collective-permute-done.15.taken_head), custom_call_target="tpu_custom_call" | custom-call | tf_op jit(solution)/shard_map/pallas_call | solution.py:291
  43.6 0.6 %collective-permute-done.16.taken_tail = bf16[7,128,128]{2,1,0:T(8,128)(2,1)S(1)} collective-permute-done((bf16[7,128,128]{2,1,0:T(8,128)(2,1)S(1)}, bf16[7,128,128]{2,1,0:T(8,128)(2,1)S(1)}, u32[]{:S(2)}, u32[]{:S(2)}) %collective-permute-start.16) | collective-permute-done | bytes 229408 | tf_op jit(solution)/shard_map/ppermute | solution.py:231
  44.1 0.7 %shard_map.70 = bf16[2,15,128,128]{3,2,1,0:T(8,128)(2,1)} custom-call(bf16[2,15,128,128]{3,2,1,0:T(8,128)(2,1)} %shard_map.69.begun, bf16[7,128,128]{2,1,0:T(8,128)(2,1)S(1)} %collective-permute-done.16.taken_tail), custom_call_target="tpu_custom_call", output_to_operand_aliasing={{}: (0, {})} | custom-call | tf_op jit(solution)/shard_map/pallas_call | solution.py:295
  (12 shorter events, 0.1 us)
Async XLA Ops:
  0.0 1.2 %copy-start = (bf16[2,1,15,128,128]{4,3,2,1,0:T(8,128)(2,1)S(1)}, bf16[2,1,15,128,128]{4,3,2,1,0:T(8,128)(2,1)}, u32[]{:S(2)}) copy-start(bf16[2,1,15,128,128]{4,3,2,1,0:T(8,128)(2,1)} %param.5) | copy-start | bytes 2949124
  1.2 3.0 %copy-start.1 = (bf16[1,2,4,1,128,128]{5,4,3,2,1,0:T(8,128)(2,1)S(1)}, bf16[1,2,4,1,128,128]{5,4,3,2,1,0:T(8,128)(2,1)}, u32[]{:S(2)}) copy-start(bf16[1,2,4,1,128,128]{5,4,3,2,1,0:T(8,128)(2,1)} %param.6) | copy-start | bytes 786436
  1.2 3.0 %copy-start.3 = (bf16[1,4,15,15]{3,1,2,0:T(4,128)(2,1)S(1)}, bf16[1,4,15,15]{3,1,2,0:T(4,128)(2,1)}, u32[]{:S(2)}) copy-start(bf16[1,4,15,15]{3,1,2,0:T(4,128)(2,1)} %param.7) | copy-start | bytes 5404
  1.2 11.6 %collective-permute-start.5 = (bf16[15,128,128]{2,1,0:T(8,128)(2,1)S(1)}, bf16[15,128,128]{2,1,0:T(8,128)(2,1)S(1)}, u32[]{:S(2)}, u32[]{:S(2)}) collective-permute-start(bf16[15,128,128]{2,1,0:T(8,128)(2,1)S(1)} %dynamic-slice_bitcast_fusion.refs_0_), channel_id=1, source_target_pairs={{0,1},{1,2},{2,3},{3,0},{4,5},{5,6},{6,7},{7,4},{8,9},{9,10},{10,1... | collective-permute-start | bytes 1474568 | tf_op jit(solution)/shard_map/ppermute | solution.py:231
  4.2 2.6 %collective-permute-start = (bf16[2,4,128,128]{3,2,1,0:T(8,128)(2,1)S(1)}, bf16[2,4,128,128]{3,2,1,0:T(8,128)(2,1)S(1)}, u32[]{:S(2)}, u32[]{:S(2)}) collective-permute-start(bf16[2,4,128,128]{3,2,1,0:T(8,128)(2,1)S(1)} %bitcast.10), channel_id=1, source_target_pairs={{0,16},{1,17},{2,18},{3,19},{4,20},{5,21},{6,22},{7,23},{8,24},{9,... | collective-permute-start | bytes 786440 | tf_op jit(solution)/shard_map/ppermute | solution.py:231
  4.3 0.7 %copy-start.2 = (s32[1,4,1]{1,2,0:T(1,128)S(1)}, s32[1,4,1]{1,2,0:T(1,128)}, u32[]{:S(2)}) copy-start(s32[1,4,1]{1,2,0:T(1,128)} %param.9) | copy-start | bytes 52
  4.3 2.5 %collective-permute-start.1 = (bf16[4,15,15]{2,1,0:T(8,128)(2,1)S(1)}, bf16[4,15,15]{2,1,0:T(8,128)(2,1)S(1)}, u32[]{:S(2)}, u32[]{:S(2)}) collective-permute-start(bf16[4,15,15]{2,1,0:T(8,128)(2,1)S(1)} %bitcast.12), channel_id=1, source_target_pairs={{0,16},{1,17},{2,18},{3,19},{4,20},{5,21},{6,22},{7,23},{8,24},{9,... | collective-permute-start | bytes 5408 | tf_op jit(solution)/shard_map/ppermute | solution.py:231
  4.9 1.9 %collective-permute-start.3 = (s32[1,4]{1,0:T(1,128)S(1)}, s32[1,4]{1,0:T(1,128)S(1)}, u32[]{:S(2)}, u32[]{:S(2)}) collective-permute-start(s32[1,4]{1,0:T(1,128)S(1)} %bitcast.15), channel_id=1, source_target_pairs={{0,16},{1,17},{2,18},{3,19},{4,20},{5,21},{6,22},{7,23},{8,24},{9,... | collective-permute-start | bytes 56 | tf_op jit(solution)/shard_map/ppermute | solution.py:231
  5.4 1.4 %collective-permute-start.2 = (s32[1,1]{1,0:T(1,128)}, s32[1,1]{1,0:T(1,128)}, u32[]{:S(2)}, u32[]{:S(2)}) collective-permute-start(s32[1,1]{1,0:T(1,128)} %param.8), channel_id=1, source_target_pairs={{0,16},{1,17},{2,18},{3,19},{4,20},{5,21},{6,22},{7,23},{8,24},{9,... | collective-permute-start | bytes 20 | tf_op jit(solution)/shard_map/ppermute | solution.py:231
  7.6 5.2 %collective-permute-start.4 = (bf16[2,128,128]{2,1,0:T(8,128)(2,1)S(1)}, bf16[2,128,128]{2,1,0:T(8,128)(2,1)S(1)}, u32[]{:S(2)}, u32[]{:S(2)}) collective-permute-start(bf16[2,128,128]{2,1,0:T(8,128)(2,1)S(1)} %get-tuple-element.37), channel_id=1, source_target_pairs={{0,1},{1,2},{2,3},{3,0},{4,5},{5,6},{6,7},{7,4},{8,9},{9,10},{10,1... | collective-permute-start | bytes 196616 | tf_op jit(solution)/shard_map/ppermute | solution.py:231
  13.5 6.7 %collective-permute-start.6 = (bf16[8,128,128]{2,1,0:T(8,128)(2,1)S(1)}, bf16[8,128,128]{2,1,0:T(8,128)(2,1)S(1)}, u32[]{:S(2)}, u32[]{:S(2)}) collective-permute-start(bf16[8,128,128]{2,1,0:T(8,128)(2,1)S(1)} %get-tuple-element.41), channel_id=1, source_target_pairs={{0,20},{1,21},{2,22},{3,23},{4,24},{5,25},{6,26},{7,27},{8,28},{9,... | collective-permute-start | bytes 786440 | tf_op jit(solution)/shard_map/ppermute | solution.py:231
  14.9 2.9 %collective-permute-start.7 = (bf16[5,128,128]{2,1,0:T(8,128)(2,1)S(1)}, bf16[5,128,128]{2,1,0:T(8,128)(2,1)S(1)}, u32[]{:S(2)}, u32[]{:S(2)}) collective-permute-start(bf16[5,128,128]{2,1,0:T(8,128)(2,1)S(1)} %get-tuple-element.44), channel_id=1, source_target_pairs={{0,16},{1,17},{2,18},{3,19},{4,20},{5,21},{6,22},{7,23},{8,24},{9,... | collective-permute-start | bytes 491528 | tf_op jit(solution)/shard_map/ppermute | solution.py:231
  16.0 1.8 %collective-permute-start.8 = (bf16[5,128,128]{2,1,0:T(8,128)(2,1)S(1)}, bf16[5,128,128]{2,1,0:T(8,128)(2,1)S(1)}, u32[]{:S(2)}, u32[]{:S(2)}) collective-permute-start(bf16[5,128,128]{2,1,0:T(8,128)(2,1)S(1)} %get-tuple-element.45), channel_id=1, source_target_pairs={{0,16},{1,17},{2,18},{3,19},{4,20},{5,21},{6,22},{7,23},{8,24},{9,... | collective-permute-start | bytes 491528 | tf_op jit(solution)/shard_map/ppermute | solution.py:231
  16.1 1.7 %collective-permute-start.9 = (bf16[5,128,128]{2,1,0:T(8,128)(2,1)S(1)}, bf16[5,128,128]{2,1,0:T(8,128)(2,1)S(1)}, u32[]{:S(2)}, u32[]{:S(2)}) collective-permute-start(bf16[5,128,128]{2,1,0:T(8,128)(2,1)S(1)} %get-tuple-element.46), channel_id=1, source_target_pairs={{0,16},{1,17},{2,18},{3,19},{4,20},{5,21},{6,22},{7,23},{8,24},{9,... | collective-permute-start | bytes 491528 | tf_op jit(solution)/shard_map/ppermute | solution.py:231
  16.5 6.3 %collective-permute-start.11 = (bf16[7,128,128]{2,1,0:T(8,128)(2,1)S(1)}, bf16[7,128,128]{2,1,0:T(8,128)(2,1)S(1)}, u32[]{:S(2)}, u32[]{:S(2)}) collective-permute-start(bf16[7,128,128]{2,1,0:T(8,128)(2,1)S(1)} %shard_map.58.after), channel_id=1, source_target_pairs={{0,20},{1,21},{2,22},{3,23},{4,24},{5,25},{6,26},{7,27},{8,28},{9,... | collective-permute-start | bytes 688136 | tf_op jit(solution)/shard_map/ppermute | solution.py:231
  20.4 9.1 %collective-permute-start.10 = (bf16[10,128,128]{2,1,0:T(8,128)(2,1)S(1)}, bf16[10,128,128]{2,1,0:T(8,128)(2,1)S(1)}, u32[]{:S(2)}, u32[]{:S(2)}) collective-permute-start(bf16[10,128,128]{2,1,0:T(8,128)(2,1)S(1)} %shard_map.60.refs_0_.before), channel_id=1, source_target_pairs={{0,4},{1,5},{2,6},{3,7},{4,8},{5,9},{6,10},{7,11},{8,12},{9,13},{1... | collective-permute-start | bytes 983048 | tf_op jit(solution)/shard_map/ppermute | solution.py:231
  23.0 9.0 %collective-permute-start.12 = (bf16[7,128,128]{2,1,0:T(8,128)(2,1)S(1)}, bf16[7,128,128]{2,1,0:T(8,128)(2,1)S(1)}, u32[]{:S(2)}, u32[]{:S(2)}) collective-permute-start(bf16[7,128,128]{2,1,0:T(8,128)(2,1)S(1)} %shard_map.61.refs_1_.before), channel_id=1, source_target_pairs={{0,4},{1,5},{2,6},{3,7},{4,8},{5,9},{6,10},{7,11},{8,12},{9,13},{1... | collective-permute-start | bytes 688136 | tf_op jit(solution)/shard_map/ppermute | solution.py:231
  32.6 7.3 %collective-permute-start.13 = (bf16[8,128,128]{2,1,0:T(8,128)(2,1)S(1)}, bf16[8,128,128]{2,1,0:T(8,128)(2,1)S(1)}, u32[]{:S(2)}, u32[]{:S(2)}) collective-permute-start(bf16[8,128,128]{2,1,0:T(8,128)(2,1)S(1)} %get-tuple-element.50), channel_id=1, source_target_pairs={{0,1},{1,2},{2,3},{3,0},{4,5},{5,6},{6,7},{7,4},{8,9},{9,10},{10,1... | collective-permute-start | bytes 786440 | tf_op jit(solution)/shard_map/ppermute | solution.py:231
  33.6 8.8 %collective-permute-start.14 = (bf16[7,128,128]{2,1,0:T(8,128)(2,1)S(1)}, bf16[7,128,128]{2,1,0:T(8,128)(2,1)S(1)}, u32[]{:S(2)}, u32[]{:S(2)}) collective-permute-start(bf16[7,128,128]{2,1,0:T(8,128)(2,1)S(1)} %shard_map.65.after), channel_id=1, source_target_pairs={{0,1},{1,2},{2,3},{3,0},{4,5},{5,6},{6,7},{7,4},{8,9},{9,10},{10,1... | collective-permute-start | bytes 688136 | tf_op jit(solution)/shard_map/ppermute | solution.py:231
  40.1 2.5 %collective-permute-start.15 = (bf16[8,128,128]{2,1,0:T(8,128)(2,1)S(1)}, bf16[8,128,128]{2,1,0:T(8,128)(2,1)S(1)}, u32[]{:S(2)}, u32[]{:S(2)}) collective-permute-start(bf16[8,128,128]{2,1,0:T(8,128)(2,1)S(1)} %get-tuple-element.57), channel_id=1, source_target_pairs={{0,16},{1,17},{2,18},{3,19},{4,20},{5,21},{6,22},{7,23},{8,24},{9,... | collective-permute-start | bytes 786440 | tf_op jit(solution)/shard_map/ppermute | solution.py:231
  42.6 1.6 %collective-permute-start.16 = (bf16[7,128,128]{2,1,0:T(8,128)(2,1)S(1)}, bf16[7,128,128]{2,1,0:T(8,128)(2,1)S(1)}, u32[]{:S(2)}, u32[]{:S(2)}) collective-permute-start(bf16[7,128,128]{2,1,0:T(8,128)(2,1)S(1)} %get-tuple-element.58), channel_id=1, source_target_pairs={{0,16},{1,17},{2,18},{3,19},{4,20},{5,21},{6,22},{7,23},{8,24},{9,... | collective-permute-start | bytes 688136 | tf_op jit(solution)/shard_map/ppermute | solution.py:231

commit v3 on v2

v3 whole, which is shorter than its diff:
```python
import functools

import jax
import jax.numpy as jnp
from jax import lax
from jax.experimental import pallas as pl
from jax.experimental.pallas import tpu as pltpu
from jax.sharding import PartitionSpec as P

QD = 4
LO = 16
AXES = ("chain", "sector")


def rings(sectors):
    down = lambda k: (k // QD) * QD + (k + 1) % QD
    up = lambda k: (k + QD) % sectors
    stay = lambda k: k

    def pairs(zero, one, cross):
        to_zero, to_one = (sectors, 0) if cross else (0, sectors)
        return [(k, to_zero + zero(k)) for k in range(sectors)] + [(sectors + k, to_one + one(k)) for k in range(sectors)]

    last = sectors - QD
    column = [(sectors + k, sectors + k + QD if k < last else k) for k in range(sectors)]
    column += [(k, k - QD if k >= QD else sectors + k) for k in range(sectors)]
    return {
        "envs": pairs(down, up, False),
        "partials": pairs(up, down, True),
        "new_envs": pairs(up, down, False),
        "up": column,
        "down": pairs(down, stay, True),
        "swap": pairs(stay, stay, True),
    }


def place():
    core, sector = lax.axis_index("chain"), lax.axis_index("sector")
    return core, lax.rem(sector, QD) < QD - 1, lax.rem(sector, QD) > 0, sector >= QD


def spreads(couplings):
    w = couplings[0].shape[0]
    rows = lax.broadcasted_iota(jnp.int32, (w * LO, w), 0) // LO
    pick = (rows == lax.broadcasted_iota(jnp.int32, (w * LO, w), 1)).astype(jnp.bfloat16)
    i = lax.broadcasted_iota(jnp.int32, (w * LO, w * LO), 0) % LO
    j = lax.broadcasted_iota(jnp.int32, (w * LO, w * LO), 1) % LO
    same = i == j

    def spread(mpo):
        tall = lax.dot_general(pick, mpo, (((1,), (1,)), ((), ())), preferred_element_type=jnp.float32).astype(jnp.bfloat16)
        full = lax.dot_general(tall, pick, (((1,), (1,)), ((), ())), preferred_element_type=jnp.float32)
        return jnp.where(same, full, 0.0).astype(jnp.bfloat16)

    return [spread(mpo) for mpo in couplings]


def couple(coupling, projected, column, out, lowest=0):
    count, blk = out.shape[0], out.shape[1]
    coupling = coupling[lowest * LO:(lowest + count) * LO]

    def part(a):
        pieces = [p[:, a:a + LO, column:column + blk].reshape(p.shape[0] * LO, blk) for p in projected]
        return pieces[0] if len(pieces) == 1 else jnp.concatenate(pieces, axis=0)

    for a in range(0, blk, 2 * LO):
        both = jnp.concatenate([part(a), part(a + LO)], axis=1)
        mixed = jnp.dot(coupling, both, preferred_element_type=jnp.float32).astype(out.dtype)
        out[:, a:a + LO, :] = mixed[:, :blk].reshape(count, LO, blk)
        out[:, a + LO:a + 2 * LO, :] = mixed[:, blk:].reshape(count, LO, blk)


def project(parts, counts, right, projected):
    slots = [(part, i) for part, count in zip(parts, counts) for i in range(count)]
    for w, (part, i) in enumerate(slots):
        projected[w] = jnp.dot(part[i], right, preferred_element_type=jnp.float32).astype(jnp.bfloat16)


def join(ours, theirs, mine, lowest, mixed, outs):
    left = jnp.concatenate([ours.T, theirs.T], axis=1)
    slots = [(out, i) for out in outs for i in range(out.shape[0])]
    blk = left.shape[0]
    for v in range(0, len(slots), 2):
        pair = range(v, min(v + 2, len(slots)))
        right = jnp.concatenate([jnp.concatenate([mine[lowest + u], mixed[u]], axis=0) for u in pair], axis=1)
        both = jnp.dot(left, right, preferred_element_type=jnp.float32)
        for n, u in enumerate(pair):
            out, i = slots[u]
            out[i] = both[:, n * blk:(n + 1) * blk].astype(out.dtype)


def prepare_kernel(here, other, rows, rows_other, states, states_other, local, send, later, live):
    core, inside, _, _ = place()

    def block(site, target, state, choice):
        same = core == site

        def exists(k):
            flag = jnp.where(same, here[:, k:k + 1], other[:, k:k + 1]) > 0
            return flag & inside if k >= 2 else flag

        def of(k):
            both = jnp.where(same, states[target, k], states_other[target, k])
            return jnp.where(exists(k), both, jnp.zeros_like(both))

        return of(state) if state == choice else jnp.where(target == 0, of(state), of(choice))

    send[0] = block(0, core, 3, 3)
    local[0, 0] = block(0, core, 1, 2)
    local[0, 1] = block(0, core, 0, 0)
    local[1, 0] = block(1, 1 - core, 1, 2)
    local[1, 1] = block(1, 1 - core, 0, 0)
    send[1] = block(0, core, 2, 1)
    later[0] = block(1, 1 - core, 3, 3)
    later[1] = block(1, 1 - core, 2, 1)
    for site in range(2):
        live[site] = jnp.broadcast_to(jnp.where(core == site, rows[...], rows_other[...]), live.shape[1:])


def behind(target, sent):
    _, _, from_down, from_up = place()
    return jnp.where(jnp.where(target == 0, from_down, from_up), sent, jnp.zeros_like(sent))


def own_kernel(site, counts, local, mpo, mpo_other, *refs):
    *parts, out_q, out_r, out_spread, projected = refs
    core, target = lax.axis_index("chain"), target_of(site)
    pick = lambda state: jnp.where(core == site, mpo[state], mpo_other[state])
    middle, zero, both, outer = spreads([pick(1 + target), pick(0), pick(3), pick(2 - target)])
    project(parts, counts, jnp.concatenate([local[site, 0], local[site, 1]], axis=1), projected)
    couple(middle, [projected], 0, out_q)
    couple(zero, [projected], out_q.shape[1], out_r)
    out_spread[0] = both
    out_spread[1] = outer


def target_of(site):
    core = lax.axis_index("chain")
    return core if site == 0 else 1 - core


def project_kernel(site, at, sent, part, projected):
    project([part], projected.shape[:1], behind(target_of(site), sent[at]), projected)


def head_kernel(site, at, local, sent, spread, mine, *refs):
    *projected, part, out, mine_projected, mixed = refs
    theirs = behind(target_of(site), sent[at])
    project([part], mine_projected.shape[:1], theirs, mine_projected)
    couple(spread[0], [*projected, mine_projected], 0, mixed)
    join(local[site, 0], theirs, mine, 0, mixed, [out])


def tail_kernel(site, at, local, sent, spread, mine, *refs):
    *projected, out, mixed = refs
    lowest = mine.shape[0] - out.shape[0]
    couple(spread[0], projected, 0, mixed, lowest)
    join(local[site, 0], behind(target_of(site), sent[at]), mine, lowest, mixed, [out])


def keep_kernel(site, at, counts, local, sent, spread, mine, after, *refs):
    parts, refs = refs[:len(counts)], refs[len(counts):]
    theirs = behind(target_of(site), sent[at + 1])
    *outs, projected, mixed = refs
    project(parts, counts, theirs, projected)
    couple(spread[1], [projected], 0, mixed)
    join(local[site, 1], theirs, mine, 0, mixed, outs)


def give_kernel(pieces, *refs):
    kept, envs, outs = refs[:pieces], refs[pieces:2 * pieces], refs[2 * pieces:]
    core = lax.axis_index("chain")
    blocks = [(a, b, i) for a, b in zip(kept, envs) for i in range(a.shape[0])]
    slots = [(out, i) for out in outs for i in range(out.shape[0])]
    for (a, b, i), (out, j) in zip(blocks, slots):
        out[j] = jnp.where(core == 0, a[i].astype(jnp.bfloat16), b[i])


def total(site, live, valid, kept, arrived):
    blk = kept.shape[0]
    rows = live[site, 0:1, :]
    inside = (lax.broadcasted_iota(jnp.int32, (blk, blk), 0) < rows) & (lax.broadcasted_iota(jnp.int32, (blk, blk), 1) < rows)
    both = kept.astype(jnp.float32) + jnp.where(valid, arrived.astype(jnp.float32), 0.0)
    return jnp.where(inside, both, 0.0).astype(jnp.bfloat16)


def sum_kernel(lowest, pieces, live, arrived, *refs):
    kept, more, out = refs[:pieces], refs[pieces:-1], refs[-1]
    core, _, from_down, from_up = place()
    valid = jnp.where(core == 0, from_down, from_up)
    slots = [(part, i) for part in kept for i in range(part.shape[0])]
    count = arrived.shape[0]
    for v in range(count):
        part, i = slots[lowest + v]
        out[v] = total(0, live, valid, part[i], arrived[v])
    for blocks in more:
        for i in range(blocks.shape[0]):
            out[count + i] = blocks[i]


def last_kernel(lowest, pieces, started, live, from_up_arrived, from_down_arrived, kept, env, *refs):
    taken, refs = refs[:pieces], refs[pieces + started:]
    out, new, sems = refs
    core, _, from_down, from_up = place()
    count = kept.shape[0]
    slots = [(part, i) for part in taken for i in range(part.shape[0])][lowest:lowest + count]
    for v in range(count):
        part, i = slots[v]
        received = part[i]
        new[0, v] = jnp.where(core == 0, received, total(1, live, from_up, kept[v], from_up_arrived[v]))
        new[1, v] = jnp.where(core == 0, env[v], total(1, live, from_down, received, from_down_arrived[v]))
    copy_all([(new.at[t], out.at[t, pl.ds(lowest, count)]) for t in range(2)], sems)


def copy_all(copies, sems):
    copies = [pltpu.make_async_copy(source, target, sems.at[i]) for i, (source, target) in enumerate(copies)]
    for copy in copies:
        copy.start()
    for copy in copies:
        copy.wait()


VMEM = pl.BlockSpec(memory_space=pltpu.VMEM)
SMEM = pl.BlockSpec(memory_space=pltpu.SMEM)


def call(kernel, out_shape, in_specs, scratch=()):
    single = not isinstance(out_shape, (tuple, list))
    return pl.pallas_call(
        kernel,
        out_shape=out_shape,
        in_specs=in_specs,
        out_specs=VMEM if single else [VMEM] * len(out_shape),
        scratch_shapes=scratch,
        compiler_params=pltpu.CompilerParams(vmem_limit_bytes=24 << 20),
        cost_estimate=pl.CostEstimate(flops=1, bytes_accessed=1, transcendentals=0),
    )


def on_device(env_first, states, mpo, block_rows, present):
    pairs = rings(lax.axis_size("sector"))
    move = lambda value, name: lax.ppermute(value, AXES, pairs[name])
    core = lax.axis_index("chain")
    _, _, width, blk, _ = env_first.shape
    lengths = (-(-width // 2), width // 2)
    lowest = (0, lengths[0])
    array = lambda *shape, dtype=jnp.bfloat16: jax.ShapeDtypeStruct(shape, dtype)
    scratch = lambda n, m=1: pltpu.VMEM((n, blk, m * blk), jnp.bfloat16)
    half = array(width, blk, blk)
    spread_shape = array(2, width * LO, width * LO)
    pieces = [array(n, blk, blk) for n in lengths]
    wide = [array(n, blk, blk, dtype=jnp.float32) for n in lengths]
    small = [array(len(range(i, min(i + 5, width))), blk, blk) for i in range(0, width, 5)]

    env_first = env_first[:, 0]
    states, mpo, rows, here = states[0, :, :, 0], mpo[0], block_rows, present[:, :, 0]
    env = lax.dynamic_index_in_dim(env_first, core, 0, keepdims=False)
    arriving = move(env, "envs")
    states_other, mpo_other, rows_other, other = lax.optimization_barrier(tuple(move(x, "swap") for x in (states, mpo, rows, here)))
    local, send, later, live = call(
        prepare_kernel, [array(2, 2, blk, blk), array(2, blk, blk), array(2, blk, blk), array(2, 8, blk, dtype=jnp.int32)], [VMEM] * 6,
    )(here, other, rows, rows_other, states, states_other)
    sent = move(send, "envs")

    own = lambda site, counts: call(
        functools.partial(own_kernel, site, counts), [half, half, spread_shape], [VMEM] * (3 + len(counts)), [scratch(width, 2)])
    mine_q, mine_r, spread = own(0, (width,))(local, mpo, mpo_other, env)
    q_head, projected = call(functools.partial(head_kernel, 0, 0), [pieces[0], half], [VMEM] * 5, [scratch(lengths[0])])(
        local, sent, spread, mine_q, arriving)
    q_tail = call(functools.partial(tail_kernel, 0, 0), pieces[1], [VMEM] * 5, [scratch(lengths[1])])(
        local, sent, spread, mine_q, projected)
    arrived = [move(q, "partials") for q in (q_head, q_tail)]
    kept = call(functools.partial(keep_kernel, 0, 0, (width,)), small, [VMEM] * 6, [scratch(width)] * 2)(
        local, sent, spread, mine_r, q_tail, arriving)
    kept = [move(part, "swap") for part in kept]
    with_blocks = array(lengths[0] + 2, blk, blk)
    envs = [
        call(functools.partial(sum_kernel, lowest[0], len(kept)), with_blocks, [VMEM] * (3 + len(kept)))(live, arrived[0], *kept, later),
        call(functools.partial(sum_kernel, lowest[1], len(kept)), pieces[1], [VMEM] * (2 + len(kept)))(live, arrived[1], *kept),
    ]
    arriving = [move(env, "new_envs") for env in envs]
    sent, at = arriving[0], lengths[0]

    mine_q, mine_r, spread = own(1, lengths)(local, mpo, mpo_other, *envs)
    early = call(functools.partial(project_kernel, 1, at), pieces[0], [VMEM] * 2)(sent, arriving[0])
    q_head, projected = call(functools.partial(head_kernel, 1, at), pieces, [VMEM] * 6, [scratch(lengths[0])])(
        local, sent, spread, mine_q, early, arriving[1])
    q_tail = call(functools.partial(tail_kernel, 1, at), pieces[1], [VMEM] * 6, [scratch(lengths[1])])(
        local, sent, spread, mine_q, early, projected)
    downs = [move(q, "down") for q in (q_head, q_tail)]
    ups = [move(q, "up") for q in (q_head, q_tail)]
    kept = call(functools.partial(keep_kernel, 1, at, lengths), wide, [VMEM] * 7, [scratch(width)] * 2)(
        local, sent, spread, mine_r, q_tail, *arriving)
    given = call(functools.partial(give_kernel, 2), small, [VMEM] * 4)(*kept, *envs)
    taken = [move(part, "swap") for part in lax.optimization_barrier((given, downs[0]))[0]]
    hbm = pl.BlockSpec(memory_space=pl.ANY)
    result = []
    for i in range(2):
        result = [pl.pallas_call(
            functools.partial(last_kernel, lowest[i], len(taken), i),
            out_shape=array(2, width, blk, blk),
            in_specs=[VMEM] * (5 + len(taken)) + [hbm] * i,
            out_specs=hbm,
            scratch_shapes=[pltpu.VMEM((2, lengths[i], blk, blk), jnp.bfloat16), pltpu.SemaphoreType.DMA((2,))],
            input_output_aliases={5 + len(taken): 0} if i else {},
            compiler_params=pltpu.CompilerParams(vmem_limit_bytes=24 << 20),
            cost_estimate=pl.CostEstimate(flops=1, bytes_accessed=1, transcendentals=0),
        )(live, ups[i], downs[i], kept[i], envs[i], *taken, *result)]
    return result[0][None, :, None]


def solution(mesh):
    placed = (
        P(None, "sector", None, None, None),
        P("chain", None, None, "sector", None, None),
        P("chain", None, None, None),
        P("chain", "sector"),
        P("chain", None, "sector"),
    )
    return jax.shard_map(
        on_device,
        mesh=mesh,
        in_specs=placed,
        out_specs=P("chain", None, "sector", None, None, None),
        check_vma=False,
    )
```

time: 45 us -> 42.9 us (0.953)
  waiting for transfers between devices: 17.6 us -> 14.1 us
  starting transfers between devices: 15.9 us -> 16.6 us
  Pallas kernels: 9.21 us -> 9.77 us
    ppermute x17 -> x20, waiting for transfers between devices: 17.6 us -> 14.1 us  [on_device(): move = lambda value, name: lax.ppermute(value, AXES, pairs[name])]
    ppermute x17 -> x20, starting transfers between devices: 15.9 us -> 16.6 us  [on_device(): move = lambda value, name: lax.ppermute(value, AXES, pairs[name])]
    pallas_call x16 -> x15, Pallas kernels: 9.21 us -> 9.77 us  [the longest x2 2.17 us: on_device(): pl.pallas_call(functools.partial(last_kernel, lowest[i], len(taken), i),...]
  transfers between devices with their start and end apart: 17 -> 20, of which waited for: 9 -> 11; matrix products, arithmetic and copies ran while one was open for 0% -> 0% of each run, Pallas kernels for 16% -> 17%
where the time goes in v3:
time: 42.9 us; the launch traced here: 42.7 us
  starting transfers between devices  16.6 us (39%)
  waiting for transfers between devices  14.1 us (33%)
  Pallas kernels  9.77 us (23%)
  local copies, waits for them, and re-layouts  1.34 us (3%)
  between operations  0.83 us (2%)
    ppermute x20, starting transfers between devices, on_device(): move = lambda value, name: lax.ppermute(value, AXES, pairs[name])  16.6 us
    ppermute x20, waiting for transfers between devices, on_device(): move = lambda value, name: lax.ppermute(value, AXES, pairs[name])  14.1 us
    pallas_call x2, Pallas kernels, on_device(): pl.pallas_call(functools.partial(last_kernel, lowest[i], len(taken), i),...  2.17 us
    unnamed x9, local copies, waits for them, and re-layouts  1.31 us
    pallas_call x1, Pallas kernels, on_device(): mine_q, mine_r, spread = own(0, (width,))(local, mpo, mpo_other, env)  1.16 us
    pallas_call x1, Pallas kernels, on_device(): mine_q, mine_r, spread = own(1, lengths)(local, mpo, mpo_other, *envs)  1.16 us
  transfers between devices with their start and end apart: 20, of which 11 were waited for; matrix products, arithmetic and copies ran while one was open for 0% of the time, Pallas kernels for 17%

profile of v3, /device:TPU:0, one launch (start us, length us, event | category | flops | bytes accessed | tf_op | source)
XLA Modules:
  0.0 42.7 jit_solution(5228066259197924136)
XLA Ops:
  0.0 1.2 %copy-done = bf16[2,1,15,128,128]{4,3,2,1,0:T(8,128)(2,1)S(1)} copy-done((bf16[2,1,15,128,128]{4,3,2,1,0:T(8,128)(2,1)S(1)}, bf16[2,1,15,128,128]{4,3,2,1,0:T(8,128)(2,1)}, u32[]{:S(2)}) %copy-start) | copy-done | bytes 983064
  1.2 3.0 %collective-permute-start.5 = (bf16[15,128,128]{2,1,0:T(8,128)(2,1)S(1)}, bf16[15,128,128]{2,1,0:T(8,128)(2,1)S(1)}, u32[]{:S(2)}, u32[]{:S(2)}) collective-permute-start(bf16[15,128,128]{2,1,0:T(8,128)(2,1)S(1)} %dynamic-slice_bitcast_fusion.refs_0_), channel_id=1, source_target_pairs={{0,1},{1,2},{2,3},{3,0},{4,5},{5,6},{6,7},{7,4},{8,9},{9,10},{10,1... | collective-permute-start | bytes 1474568 | tf_op jit(solution)/shard_map/ppermute | solution.py:242
  4.3 0.0 copy-start.2
  4.3 0.6 %collective-permute-start.1 = (bf16[4,15,15]{2,1,0:T(8,128)(2,1)S(1)}, bf16[4,15,15]{2,1,0:T(8,128)(2,1)S(1)}, u32[]{:S(2)}, u32[]{:S(2)}) collective-permute-start(bf16[4,15,15]{2,1,0:T(8,128)(2,1)S(1)} %bitcast.12), channel_id=1, source_target_pairs={{0,16},{1,17},{2,18},{3,19},{4,20},{5,21},{6,22},{7,23},{8,24},{9,... | collective-permute-start | bytes 5408 | tf_op jit(solution)/shard_map/ppermute | solution.py:242
  4.8 0.1 copy-done.2
  4.9 0.5 %collective-permute-start.3 = (s32[1,4]{1,0:T(1,128)S(1)}, s32[1,4]{1,0:T(1,128)S(1)}, u32[]{:S(2)}, u32[]{:S(2)}) collective-permute-start(s32[1,4]{1,0:T(1,128)S(1)} %bitcast.15), channel_id=1, source_target_pairs={{0,16},{1,17},{2,18},{3,19},{4,20},{5,21},{6,22},{7,23},{8,24},{9,... | collective-permute-start | bytes 56 | tf_op jit(solution)/shard_map/ppermute | solution.py:242
  5.4 0.0 collective-permute-start.2
  6.1 0.6 %collective-permute-done.2.rows_other = s32[1,1]{1,0:T(1,128)} collective-permute-done((s32[1,1]{1,0:T(1,128)}, s32[1,1]{1,0:T(1,128)}, u32[]{:S(2)}, u32[]{:S(2)}) %collective-permute-start.2) | collective-permute-done | bytes 36 | tf_op jit(solution)/shard_map/ppermute | solution.py:242
  6.7 0.8 %shard_map.55 = (bf16[2,2,128,128]{3,2,1,0:T(8,128)(2,1)S(1)}, bf16[2,128,128]{2,1,0:T(8,128)(2,1)S(1)}, bf16[2,128,128]{2,1,0:T(8,128)(2,1)S(1)}, s32[2,8,128]{2,1,0:T(8,128)S(1)}) custom-call(s32[1,4]{1,0:T(1,128)S(1)} %bitcast.16, s32[1,4]{1,0:T(1,128)S(1)} %collective-permute-done.3.other, s32[1,1]{1,0:T(1,128)S(6)} %copy.12.rows, ...), custom_call_target="tpu_custom_call" | custom-call | flops 1 | bytes 1 | tf_op jit(solution)/shard_map/pallas_call | solution.py:260
  7.5 1.5 %collective-permute-start.4 = (bf16[2,128,128]{2,1,0:T(8,128)(2,1)S(1)}, bf16[2,128,128]{2,1,0:T(8,128)(2,1)S(1)}, u32[]{:S(2)}, u32[]{:S(2)}) collective-permute-start(bf16[2,128,128]{2,1,0:T(8,128)(2,1)S(1)} %get-tuple-element.39), channel_id=1, source_target_pairs={{0,1},{1,2},{2,3},{3,0},{4,5},{5,6},{6,7},{7,4},{8,9},{9,10},{10,1... | collective-permute-start | bytes 196616 | tf_op jit(solution)/shard_map/ppermute | solution.py:242
  9.1 1.2 %shard_map.56 = (bf16[15,128,128]{2,1,0:T(8,128)(2,1)S(1)}, bf16[15,128,128]{2,1,0:T(8,128)(2,1)S(1)}, bf16[2,240,240]{2,1,0:T(8,128)(2,1)S(1)}) custom-call(bf16[2,2,128,128]{3,2,1,0:T(8,128)(2,1)S(1)} %get-tuple-element.38.local, bf16[4,15,15]{2,1,0:T(8,128)(2,1)S(1)} %bitcast.13, bf16[4,15,15]{2,1,0:T(8,128)(2,1)S(1)} %collective-permute-done.1.mpo_other, ...), custom_call_target="tpu_custom_call" | custom-call | flops 1 | bytes 1 | tf_op jit(solution)/shard_map/pallas_call | solution.py:267
  10.2 2.5 %collective-permute-done.4.sent = bf16[2,128,128]{2,1,0:T(8,128)(2,1)S(1)} collective-permute-done((bf16[2,128,128]{2,1,0:T(8,128)(2,1)S(1)}, bf16[2,128,128]{2,1,0:T(8,128)(2,1)S(1)}, u32[]{:S(2)}, u32[]{:S(2)}) %collective-permute-start.4) | collective-permute-done | bytes 65568 | tf_op jit(solution)/shard_map/ppermute | solution.py:242
  12.7 0.7 %shard_map.57 = (bf16[8,128,128]{2,1,0:T(8,128)(2,1)S(1)}, bf16[15,128,128]{2,1,0:T(8,128)(2,1)S(1)}) custom-call(bf16[2,2,128,128]{3,2,1,0:T(8,128)(2,1)S(1)} %get-tuple-element.38.local, bf16[2,128,128]{2,1,0:T(8,128)(2,1)S(1)} %collective-permute-done.4.sent, bf16[2,240,240]{2,1,0:T(8,128)(2,1)S(1)} %get-tuple-element.41.spread, ...), custom_call_target="tpu_custom_call" | custom-call | flops 1 | bytes 1 | tf_op jit(solution)/shard_map/pallas_call | solution.py:268
  13.5 0.1 collective-permute-start.6
  13.5 0.4 shard_map.58.after
  14.0 0.8 %shard_map.59 = (bf16[5,128,128]{2,1,0:T(8,128)(2,1)S(1)}, bf16[5,128,128]{2,1,0:T(8,128)(2,1)S(1)}, bf16[5,128,128]{2,1,0:T(8,128)(2,1)S(1)}) custom-call(bf16[2,2,128,128]{3,2,1,0:T(8,128)(2,1)S(1)} %get-tuple-element.38.local, bf16[2,128,128]{2,1,0:T(8,128)(2,1)S(1)} %collective-permute-done.4.sent, bf16[2,240,240]{2,1,0:T(8,128)(2,1)S(1)} %get-tuple-element.41.spread, ...), custom_call_target="tpu_custom_call" | custom-call | flops 1 | bytes 1 | tf_op jit(solution)/shard_map/pallas_call | solution.py:273
  14.8 1.2 %collective-permute-start.7 = (bf16[5,128,128]{2,1,0:T(8,128)(2,1)S(1)}, bf16[5,128,128]{2,1,0:T(8,128)(2,1)S(1)}, u32[]{:S(2)}, u32[]{:S(2)}) collective-permute-start(bf16[5,128,128]{2,1,0:T(8,128)(2,1)S(1)} %get-tuple-element.46), channel_id=1, source_target_pairs={{0,16},{1,17},{2,18},{3,19},{4,20},{5,21},{6,22},{7,23},{8,24},{9,... | collective-permute-start | bytes 491528 | tf_op jit(solution)/shard_map/ppermute | solution.py:242
  16.0 0.1 collective-permute-start.8
  16.1 0.4 %collective-permute-start.9 = (bf16[5,128,128]{2,1,0:T(8,128)(2,1)S(1)}, bf16[5,128,128]{2,1,0:T(8,128)(2,1)S(1)}, u32[]{:S(2)}, u32[]{:S(2)}) collective-permute-start(bf16[5,128,128]{2,1,0:T(8,128)(2,1)S(1)} %get-tuple-element.48), channel_id=1, source_target_pairs={{0,16},{1,17},{2,18},{3,19},{4,20},{5,21},{6,22},{7,23},{8,24},{9,... | collective-permute-start | bytes 491528 | tf_op jit(solution)/shard_map/ppermute | solution.py:242
  16.5 1.3 %collective-permute-start.11 = (bf16[7,128,128]{2,1,0:T(8,128)(2,1)S(1)}, bf16[7,128,128]{2,1,0:T(8,128)(2,1)S(1)}, u32[]{:S(2)}, u32[]{:S(2)}) collective-permute-start(bf16[7,128,128]{2,1,0:T(8,128)(2,1)S(1)} %shard_map.58.after), channel_id=1, source_target_pairs={{0,20},{1,21},{2,22},{3,23},{4,24},{5,25},{6,26},{7,27},{8,28},{9,... | collective-permute-start | bytes 688136 | tf_op jit(solution)/shard_map/ppermute | solution.py:242
  17.8 2.4 %collective-permute-done.6.arrived = bf16[8,128,128]{2,1,0:T(8,128)(2,1)S(1)} collective-permute-done((bf16[8,128,128]{2,1,0:T(8,128)(2,1)S(1)}, bf16[8,128,128]{2,1,0:T(8,128)(2,1)S(1)}, u32[]{:S(2)}, u32[]{:S(2)}) %collective-permute-start.6) | collective-permute-done | bytes 262176 | tf_op jit(solution)/shard_map/ppermute | solution.py:242
  20.2 0.1 shard_map.60.refs_0_.refs_2_.env
  20.4 2.1 %collective-permute-start.10 = (bf16[10,128,128]{2,1,0:T(8,128)(2,1)S(1)}, bf16[10,128,128]{2,1,0:T(8,128)(2,1)S(1)}, u32[]{:S(2)}, u32[]{:S(2)}) collective-permute-start(bf16[10,128,128]{2,1,0:T(8,128)(2,1)S(1)} %shard_map.60.refs_0_.refs_2_.env), channel_id=1, source_target_pairs={{0,4},{1,5},{2,6},{3,7},{4,8},{5,9},{6,10},{7,11},{8,12},{9,13},{1... | collective-permute-start | bytes 983048 | tf_op jit(solution)/shard_map/ppermute | solution.py:242
  22.4 0.4 %collective-permute-done.11.arrived = bf16[7,128,128]{2,1,0:T(8,128)(2,1)S(1)} collective-permute-done((bf16[7,128,128]{2,1,0:T(8,128)(2,1)S(1)}, bf16[7,128,128]{2,1,0:T(8,128)(2,1)S(1)}, u32[]{:S(2)}, u32[]{:S(2)}) %collective-permute-start.11) | collective-permute-done | bytes 229408 | tf_op jit(solution)/shard_map/ppermute | solution.py:242
  22.9 0.1 shard_map.61.refs_1_.refs_3_.env
  23.0 1.9 %collective-permute-start.12 = (bf16[7,128,128]{2,1,0:T(8,128)(2,1)S(1)}, bf16[7,128,128]{2,1,0:T(8,128)(2,1)S(1)}, u32[]{:S(2)}, u32[]{:S(2)}) collective-permute-start(bf16[7,128,128]{2,1,0:T(8,128)(2,1)S(1)} %shard_map.61.refs_1_.refs_3_.env), channel_id=1, source_target_pairs={{0,4},{1,5},{2,6},{3,7},{4,8},{5,9},{6,10},{7,11},{8,12},{9,13},{1... | collective-permute-start | bytes 688136 | tf_op jit(solution)/shard_map/ppermute | solution.py:242
  24.9 1.2 %shard_map.62 = (bf16[15,128,128]{2,1,0:T(8,128)(2,1)S(1)}, bf16[15,128,128]{2,1,0:T(8,128)(2,1)S(1)}, bf16[2,240,240]{2,1,0:T(8,128)(2,1)S(1)}) custom-call(bf16[2,2,128,128]{3,2,1,0:T(8,128)(2,1)S(1)} %get-tuple-element.38.local, bf16[4,15,15]{2,1,0:T(8,128)(2,1)S(1)} %bitcast.14, bf16[4,15,15]{2,1,0:T(8,128)(2,1)S(1)} %collective-permute-done.1.mpo_other, ...), custom_call_target="tpu_custom_call" | custom-call | flops 1 | bytes 1 | tf_op jit(solution)/shard_map/pallas_call | solution.py:284
  26.0 3.5 %collective-permute-done.10.sent.part.refs_0_ = bf16[10,128,128]{2,1,0:T(8,128)(2,1)S(1)} collective-permute-done((bf16[10,128,128]{2,1,0:T(8,128)(2,1)S(1)}, bf16[10,128,128]{2,1,0:T(8,128)(2,1)S(1)}, u32[]{:S(2)}, u32[]{:S(2)}) %collective-permute-start.10) | collective-permute-done | bytes 327712 | tf_op jit(solution)/shard_map/ppermute | solution.py:242
  29.5 0.2 shard_map.63.refs_0_
  29.8 2.2 %collective-permute-done.12.refs_1_ = bf16[7,128,128]{2,1,0:T(8,128)(2,1)S(1)} collective-permute-done((bf16[7,128,128]{2,1,0:T(8,128)(2,1)S(1)}, bf16[7,128,128]{2,1,0:T(8,128)(2,1)S(1)}, u32[]{:S(2)}, u32[]{:S(2)}) %collective-permute-start.12) | collective-permute-done | bytes 229408 | tf_op jit(solution)/shard_map/ppermute | solution.py:242
  32.0 0.6 %shard_map.64 = (bf16[8,128,128]{2,1,0:T(8,128)(2,1)S(1)}, bf16[7,128,128]{2,1,0:T(8,128)(2,1)S(1)}) custom-call(bf16[2,2,128,128]{3,2,1,0:T(8,128)(2,1)S(1)} %get-tuple-element.38.local, bf16[10,128,128]{2,1,0:T(8,128)(2,1)S(1)} %collective-permute-done.10.sent.part.refs_0_, bf16[2,240,240]{2,1,0:T(8,128)(2,1)S(1)} %get-tuple-element.50.spread, ...), custom_call_target="tpu_custom_call" | custom-call | flops 1 | bytes 1 | tf_op jit(solution)/shard_map/pallas_call | solution.py:286
  32.6 0.1 collective-permute-start.15
  32.7 0.5 %collective-permute-start.19 = (bf16[8,128,128]{2,1,0:T(8,128)(2,1)S(1)}, bf16[8,128,128]{2,1,0:T(8,128)(2,1)S(1)}, u32[]{:S(2)}, u32[]{:S(2)}) collective-permute-start(bf16[8,128,128]{2,1,0:T(8,128)(2,1)S(1)} %get-tuple-element.59), channel_id=1, source_target_pairs={{16,20},{17,21},{18,22},{19,23},{20,24},{21,25},{22,26},{23,27},{2... | collective-permute-start | bytes 786440 | tf_op jit(solution)/shard_map/ppermute | solution.py:242
  33.2 0.4 shard_map.65.after
  33.6 0.0 collective-permute-start.13
  33.6 0.8 %collective-permute-start.14 = (bf16[7,128,128]{2,1,0:T(8,128)(2,1)S(1)}, bf16[7,128,128]{2,1,0:T(8,128)(2,1)S(1)}, u32[]{:S(2)}, u32[]{:S(2)}) collective-permute-start(bf16[7,128,128]{2,1,0:T(8,128)(2,1)S(1)} %shard_map.65.after), channel_id=1, source_target_pairs={{0,17},{1,18},{2,19},{3,16},{4,21},{5,22},{6,23},{7,20},{8,25},{9,... | collective-permute-start | bytes 688136 | tf_op jit(solution)/shard_map/ppermute | solution.py:242
  34.4 0.8 %shard_map.66 = (f32[8,128,128]{2,1,0:T(8,128)S(1)}, f32[7,128,128]{2,1,0:T(8,128)S(1)}) custom-call(bf16[2,2,128,128]{3,2,1,0:T(8,128)(2,1)S(1)} %get-tuple-element.38.local, bf16[10,128,128]{2,1,0:T(8,128)(2,1)S(1)} %collective-permute-done.10.sent.part.refs_0_, bf16[2,240,240]{2,1,0:T(8,128)(2,1)S(1)} %get-tuple-element.50.spread, ...), custom_call_target="tpu_custom_call" | custom-call | flops 1 | bytes 1 | tf_op jit(solution)/shard_map/pallas_call | solution.py:292
  35.2 0.1 shard_map.67
  35.3 1.2 %collective-permute-done.15.from_down_arrived = bf16[8,128,128]{2,1,0:T(8,128)(2,1)S(1)} collective-permute-done((bf16[8,128,128]{2,1,0:T(8,128)(2,1)S(1)}, bf16[8,128,128]{2,1,0:T(8,128)(2,1)S(1)}, u32[]{:S(2)}, u32[]{:S(2)}) %collective-permute-start.15) | collective-permute-done | bytes 262176 | tf_op jit(solution)/shard_map/ppermute | solution.py:242
  36.6 2.3 %collective-permute-start.16 = (bf16[5,128,128]{2,1,0:T(8,128)(2,1)S(1)}, bf16[5,128,128]{2,1,0:T(8,128)(2,1)S(1)}, u32[]{:S(2)}, u32[]{:S(2)}) collective-permute-start(bf16[5,128,128]{2,1,0:T(8,128)(2,1)S(1)} %get-tuple-element.60), channel_id=1, source_target_pairs={{0,16},{1,17},{2,18},{3,19},{4,20},{5,21},{6,22},{7,23},{8,24},{9,... | collective-permute-start | bytes 491528 | tf_op jit(solution)/shard_map/ppermute | solution.py:242
  38.9 0.0 collective-permute-start.17
  38.9 0.2 collective-permute-done.19.from_up_arrived
  39.1 0.4 collective-permute-start.18
  39.4 0.5 %collective-permute-done.16.refs_0_ = bf16[5,128,128]{2,1,0:T(8,128)(2,1)S(1)} collective-permute-done((bf16[5,128,128]{2,1,0:T(8,128)(2,1)S(1)}, bf16[5,128,128]{2,1,0:T(8,128)(2,1)S(1)}, u32[]{:S(2)}, u32[]{:S(2)}) %collective-permute-start.16) | collective-permute-done | bytes 163872 | tf_op jit(solution)/shard_map/ppermute | solution.py:242
  39.9 0.4 collective-permute-done.17.refs_1_
  40.3 0.2 collective-permute-done.18.refs_2_
  40.5 1.1 %shard_map.68.refs_3_ = bf16[2,15,128,128]{3,2,1,0:T(8,128)(2,1)} custom-call(s32[2,8,128]{2,1,0:T(8,128)S(1)} %get-tuple-element.37.live, bf16[8,128,128]{2,1,0:T(8,128)(2,1)S(1)} %collective-permute-done.19.from_up_arrived, bf16[8,128,128]{2,1,0:T(8,128)(2,1)S(1)} %collective-permute-done.15.from_down_arrived, ...), custom_call_target="tpu_custom_call" | custom-call | flops 1 | bytes 1 | tf_op jit(solution)/shard_map/pallas_call | solution.py:299
  41.7 1.1 %shard_map.69 = bf16[2,15,128,128]{3,2,1,0:T(8,128)(2,1)} custom-call(s32[2,8,128]{2,1,0:T(8,128)S(1)} %get-tuple-element.37.live, bf16[7,128,128]{2,1,0:T(8,128)(2,1)S(1)} %collective-permute-done.13.from_up_arrived, bf16[7,128,128]{2,1,0:T(8,128)(2,1)S(1)} %collective-permute-done.14.from_down_arrived, ...), custom_call_target="tpu_custom_call", output_to_operand_aliasing={{}: (8, {})} | custom-call | flops 1 | bytes 1 | tf_op jit(solution)/shard_map/pallas_call | solution.py:299
  (17 shorter events, 0.1 us)
Async XLA Ops:
  0.0 1.2 %copy-start = (bf16[2,1,15,128,128]{4,3,2,1,0:T(8,128)(2,1)S(1)}, bf16[2,1,15,128,128]{4,3,2,1,0:T(8,128)(2,1)}, u32[]{:S(2)}) copy-start(bf16[2,1,15,128,128]{4,3,2,1,0:T(8,128)(2,1)} %param.5) | copy-start | bytes 2949124
  1.2 3.0 %copy-start.1 = (bf16[1,2,4,1,128,128]{5,4,3,2,1,0:T(8,128)(2,1)S(1)}, bf16[1,2,4,1,128,128]{5,4,3,2,1,0:T(8,128)(2,1)}, u32[]{:S(2)}) copy-start(bf16[1,2,4,1,128,128]{5,4,3,2,1,0:T(8,128)(2,1)} %param.6) | copy-start | bytes 786436
  1.2 3.0 %copy-start.3 = (bf16[1,4,15,15]{3,1,2,0:T(4,128)(2,1)S(1)}, bf16[1,4,15,15]{3,1,2,0:T(4,128)(2,1)}, u32[]{:S(2)}) copy-start(bf16[1,4,15,15]{3,1,2,0:T(4,128)(2,1)} %param.7) | copy-start | bytes 5404
  1.2 11.5 %collective-permute-start.5 = (bf16[15,128,128]{2,1,0:T(8,128)(2,1)S(1)}, bf16[15,128,128]{2,1,0:T(8,128)(2,1)S(1)}, u32[]{:S(2)}, u32[]{:S(2)}) collective-permute-start(bf16[15,128,128]{2,1,0:T(8,128)(2,1)S(1)} %dynamic-slice_bitcast_fusion.refs_0_), channel_id=1, source_target_pairs={{0,1},{1,2},{2,3},{3,0},{4,5},{5,6},{6,7},{7,4},{8,9},{9,10},{10,1... | collective-permute-start | bytes 1474568 | tf_op jit(solution)/shard_map/ppermute | solution.py:242
  4.2 2.4 %collective-permute-start = (bf16[2,4,128,128]{3,2,1,0:T(8,128)(2,1)S(1)}, bf16[2,4,128,128]{3,2,1,0:T(8,128)(2,1)S(1)}, u32[]{:S(2)}, u32[]{:S(2)}) collective-permute-start(bf16[2,4,128,128]{3,2,1,0:T(8,128)(2,1)S(1)} %bitcast.10), channel_id=1, source_target_pairs={{0,16},{1,17},{2,18},{3,19},{4,20},{5,21},{6,22},{7,23},{8,24},{9,... | collective-permute-start | bytes 786440 | tf_op jit(solution)/shard_map/ppermute | solution.py:242
  4.3 0.7 %copy-start.2 = (s32[1,4,1]{1,2,0:T(1,128)S(1)}, s32[1,4,1]{1,2,0:T(1,128)}, u32[]{:S(2)}) copy-start(s32[1,4,1]{1,2,0:T(1,128)} %param.9) | copy-start | bytes 52
  4.3 2.4 %collective-permute-start.1 = (bf16[4,15,15]{2,1,0:T(8,128)(2,1)S(1)}, bf16[4,15,15]{2,1,0:T(8,128)(2,1)S(1)}, u32[]{:S(2)}, u32[]{:S(2)}) collective-permute-start(bf16[4,15,15]{2,1,0:T(8,128)(2,1)S(1)} %bitcast.12), channel_id=1, source_target_pairs={{0,16},{1,17},{2,18},{3,19},{4,20},{5,21},{6,22},{7,23},{8,24},{9,... | collective-permute-start | bytes 5408 | tf_op jit(solution)/shard_map/ppermute | solution.py:242
  4.9 1.7 %collective-permute-start.3 = (s32[1,4]{1,0:T(1,128)S(1)}, s32[1,4]{1,0:T(1,128)S(1)}, u32[]{:S(2)}, u32[]{:S(2)}) collective-permute-start(s32[1,4]{1,0:T(1,128)S(1)} %bitcast.15), channel_id=1, source_target_pairs={{0,16},{1,17},{2,18},{3,19},{4,20},{5,21},{6,22},{7,23},{8,24},{9,... | collective-permute-start | bytes 56 | tf_op jit(solution)/shard_map/ppermute | solution.py:242
  5.4 1.2 %collective-permute-start.2 = (s32[1,1]{1,0:T(1,128)}, s32[1,1]{1,0:T(1,128)}, u32[]{:S(2)}, u32[]{:S(2)}) collective-permute-start(s32[1,1]{1,0:T(1,128)} %param.8), channel_id=1, source_target_pairs={{0,16},{1,17},{2,18},{3,19},{4,20},{5,21},{6,22},{7,23},{8,24},{9,... | collective-permute-start | bytes 20 | tf_op jit(solution)/shard_map/ppermute | solution.py:242
  7.5 5.2 %collective-permute-start.4 = (bf16[2,128,128]{2,1,0:T(8,128)(2,1)S(1)}, bf16[2,128,128]{2,1,0:T(8,128)(2,1)S(1)}, u32[]{:S(2)}, u32[]{:S(2)}) collective-permute-start(bf16[2,128,128]{2,1,0:T(8,128)(2,1)S(1)} %get-tuple-element.39), channel_id=1, source_target_pairs={{0,1},{1,2},{2,3},{3,0},{4,5},{5,6},{6,7},{7,4},{8,9},{9,10},{10,1... | collective-permute-start | bytes 196616 | tf_op jit(solution)/shard_map/ppermute | solution.py:242
  13.5 6.7 %collective-permute-start.6 = (bf16[8,128,128]{2,1,0:T(8,128)(2,1)S(1)}, bf16[8,128,128]{2,1,0:T(8,128)(2,1)S(1)}, u32[]{:S(2)}, u32[]{:S(2)}) collective-permute-start(bf16[8,128,128]{2,1,0:T(8,128)(2,1)S(1)} %get-tuple-element.43), channel_id=1, source_target_pairs={{0,20},{1,21},{2,22},{3,23},{4,24},{5,25},{6,26},{7,27},{8,28},{9,... | collective-permute-start | bytes 786440 | tf_op jit(solution)/shard_map/ppermute | solution.py:242
  14.8 3.0 %collective-permute-start.7 = (bf16[5,128,128]{2,1,0:T(8,128)(2,1)S(1)}, bf16[5,128,128]{2,1,0:T(8,128)(2,1)S(1)}, u32[]{:S(2)}, u32[]{:S(2)}) collective-permute-start(bf16[5,128,128]{2,1,0:T(8,128)(2,1)S(1)} %get-tuple-element.46), channel_id=1, source_target_pairs={{0,16},{1,17},{2,18},{3,19},{4,20},{5,21},{6,22},{7,23},{8,24},{9,... | collective-permute-start | bytes 491528 | tf_op jit(solution)/shard_map/ppermute | solution.py:242
  16.0 1.8 %collective-permute-start.8 = (bf16[5,128,128]{2,1,0:T(8,128)(2,1)S(1)}, bf16[5,128,128]{2,1,0:T(8,128)(2,1)S(1)}, u32[]{:S(2)}, u32[]{:S(2)}) collective-permute-start(bf16[5,128,128]{2,1,0:T(8,128)(2,1)S(1)} %get-tuple-element.47), channel_id=1, source_target_pairs={{0,16},{1,17},{2,18},{3,19},{4,20},{5,21},{6,22},{7,23},{8,24},{9,... | collective-permute-start | bytes 491528 | tf_op jit(solution)/shard_map/ppermute | solution.py:242
  16.1 1.7 %collective-permute-start.9 = (bf16[5,128,128]{2,1,0:T(8,128)(2,1)S(1)}, bf16[5,128,128]{2,1,0:T(8,128)(2,1)S(1)}, u32[]{:S(2)}, u32[]{:S(2)}) collective-permute-start(bf16[5,128,128]{2,1,0:T(8,128)(2,1)S(1)} %get-tuple-element.48), channel_id=1, source_target_pairs={{0,16},{1,17},{2,18},{3,19},{4,20},{5,21},{6,22},{7,23},{8,24},{9,... | collective-permute-start | bytes 491528 | tf_op jit(solution)/shard_map/ppermute | solution.py:242
  16.5 6.3 %collective-permute-start.11 = (bf16[7,128,128]{2,1,0:T(8,128)(2,1)S(1)}, bf16[7,128,128]{2,1,0:T(8,128)(2,1)S(1)}, u32[]{:S(2)}, u32[]{:S(2)}) collective-permute-start(bf16[7,128,128]{2,1,0:T(8,128)(2,1)S(1)} %shard_map.58.after), channel_id=1, source_target_pairs={{0,20},{1,21},{2,22},{3,23},{4,24},{5,25},{6,26},{7,27},{8,28},{9,... | collective-permute-start | bytes 688136 | tf_op jit(solution)/shard_map/ppermute | solution.py:242
  20.4 9.2 %collective-permute-start.10 = (bf16[10,128,128]{2,1,0:T(8,128)(2,1)S(1)}, bf16[10,128,128]{2,1,0:T(8,128)(2,1)S(1)}, u32[]{:S(2)}, u32[]{:S(2)}) collective-permute-start(bf16[10,128,128]{2,1,0:T(8,128)(2,1)S(1)} %shard_map.60.refs_0_.refs_2_.env), channel_id=1, source_target_pairs={{0,4},{1,5},{2,6},{3,7},{4,8},{5,9},{6,10},{7,11},{8,12},{9,13},{1... | collective-permute-start | bytes 983048 | tf_op jit(solution)/shard_map/ppermute | solution.py:242
  23.0 9.0 %collective-permute-start.12 = (bf16[7,128,128]{2,1,0:T(8,128)(2,1)S(1)}, bf16[7,128,128]{2,1,0:T(8,128)(2,1)S(1)}, u32[]{:S(2)}, u32[]{:S(2)}) collective-permute-start(bf16[7,128,128]{2,1,0:T(8,128)(2,1)S(1)} %shard_map.61.refs_1_.refs_3_.env), channel_id=1, source_target_pairs={{0,4},{1,5},{2,6},{3,7},{4,8},{5,9},{6,10},{7,11},{8,12},{9,13},{1... | collective-permute-start | bytes 688136 | tf_op jit(solution)/shard_map/ppermute | solution.py:242
  32.6 3.9 %collective-permute-start.15 = (bf16[8,128,128]{2,1,0:T(8,128)(2,1)S(1)}, bf16[8,128,128]{2,1,0:T(8,128)(2,1)S(1)}, u32[]{:S(2)}, u32[]{:S(2)}) collective-permute-start(bf16[8,128,128]{2,1,0:T(8,128)(2,1)S(1)} %get-tuple-element.59), channel_id=1, source_target_pairs={{0,17},{1,18},{2,19},{3,16},{4,21},{5,22},{6,23},{7,20},{8,25},{9,... | collective-permute-start | bytes 786440 | tf_op jit(solution)/shard_map/ppermute | solution.py:242
  32.7 6.4 %collective-permute-start.19 = (bf16[8,128,128]{2,1,0:T(8,128)(2,1)S(1)}, bf16[8,128,128]{2,1,0:T(8,128)(2,1)S(1)}, u32[]{:S(2)}, u32[]{:S(2)}) collective-permute-start(bf16[8,128,128]{2,1,0:T(8,128)(2,1)S(1)} %get-tuple-element.59), channel_id=1, source_target_pairs={{16,20},{17,21},{18,22},{19,23},{20,24},{21,25},{22,26},{23,27},{2... | collective-permute-start | bytes 786440 | tf_op jit(solution)/shard_map/ppermute | solution.py:242
  33.6 8.1 %collective-permute-start.13 = (bf16[7,128,128]{2,1,0:T(8,128)(2,1)S(1)}, bf16[7,128,128]{2,1,0:T(8,128)(2,1)S(1)}, u32[]{:S(2)}, u32[]{:S(2)}) collective-permute-start(bf16[7,128,128]{2,1,0:T(8,128)(2,1)S(1)} %shard_map.65.after), channel_id=1, source_target_pairs={{16,20},{17,21},{18,22},{19,23},{20,24},{21,25},{22,26},{23,27},{2... | collective-permute-start | bytes 688136 | tf_op jit(solution)/shard_map/ppermute | solution.py:242
  33.6 8.0 %collective-permute-start.14 = (bf16[7,128,128]{2,1,0:T(8,128)(2,1)S(1)}, bf16[7,128,128]{2,1,0:T(8,128)(2,1)S(1)}, u32[]{:S(2)}, u32[]{:S(2)}) collective-permute-start(bf16[7,128,128]{2,1,0:T(8,128)(2,1)S(1)} %shard_map.65.after), channel_id=1, source_target_pairs={{0,17},{1,18},{2,19},{3,16},{4,21},{5,22},{6,23},{7,20},{8,25},{9,... | collective-permute-start | bytes 688136 | tf_op jit(solution)/shard_map/ppermute | solution.py:242
  36.6 3.4 %collective-permute-start.16 = (bf16[5,128,128]{2,1,0:T(8,128)(2,1)S(1)}, bf16[5,128,128]{2,1,0:T(8,128)(2,1)S(1)}, u32[]{:S(2)}, u32[]{:S(2)}) collective-permute-start(bf16[5,128,128]{2,1,0:T(8,128)(2,1)S(1)} %get-tuple-element.60), channel_id=1, source_target_pairs={{0,16},{1,17},{2,18},{3,19},{4,20},{5,21},{6,22},{7,23},{8,24},{9,... | collective-permute-start | bytes 491528 | tf_op jit(solution)/shard_map/ppermute | solution.py:242
  38.9 1.4 %collective-permute-start.17 = (bf16[5,128,128]{2,1,0:T(8,128)(2,1)S(1)}, bf16[5,128,128]{2,1,0:T(8,128)(2,1)S(1)}, u32[]{:S(2)}, u32[]{:S(2)}) collective-permute-start(bf16[5,128,128]{2,1,0:T(8,128)(2,1)S(1)} %get-tuple-element.61), channel_id=1, source_target_pairs={{0,16},{1,17},{2,18},{3,19},{4,20},{5,21},{6,22},{7,23},{8,24},{9,... | collective-permute-start | bytes 491528 | tf_op jit(solution)/shard_map/ppermute | solution.py:242
  39.1 1.5 %collective-permute-start.18 = (bf16[5,128,128]{2,1,0:T(8,128)(2,1)S(1)}, bf16[5,128,128]{2,1,0:T(8,128)(2,1)S(1)}, u32[]{:S(2)}, u32[]{:S(2)}) collective-permute-start(bf16[5,128,128]{2,1,0:T(8,128)(2,1)S(1)} %get-tuple-element.62), channel_id=1, source_target_pairs={{0,16},{1,17},{2,18},{3,19},{4,20},{5,21},{6,22},{7,23},{8,24},{9,... | collective-permute-start | bytes 491528 | tf_op jit(solution)/shard_map/ppermute | solution.py:242

commit v4 on v3

v4 whole, which is shorter than its diff:
```python
import functools

import jax
import jax.numpy as jnp
from jax import lax
from jax.experimental import pallas as pl
from jax.experimental.pallas import tpu as pltpu
from jax.sharding import PartitionSpec as P

QD = 4
LO = 16
AXES = ("chain", "sector")
BC = (7, 8)
EE = (8, 7)
DD = (7, 8)
GG = (5, 5, 5)
ACROSS = [(4, 5), (5, 6), (6, 7), (7, 1), (1, 3), (3, 2), (2, 0), (0, 4)]


def cut(width, shares):
    ends = [round(width * sum(shares[:i]) / sum(shares)) for i in range(len(shares) + 1)]
    return tuple(b - a for a, b in zip(ends, ends[1:]))


def rings(sectors):
    down = lambda k: (k // QD) * QD + (k + 1) % QD
    up = lambda k: (k + QD) % sectors
    stay = lambda k: k

    def pairs(zero, one, cross):
        to_zero, to_one = (sectors, 0) if cross else (0, sectors)
        return [(k, to_zero + zero(k)) for k in range(sectors)] + [(sectors + k, to_one + one(k)) for k in range(sectors)]

    last = sectors - QD
    column = [(sectors + k, sectors + k + QD if k < last else k) for k in range(sectors)]
    column += [(k, k - QD if k >= QD else sectors + k) for k in range(sectors)]
    lift = [(k, k + QD if k < last else sectors + k) for k in range(sectors)]
    lift += [(sectors + k, sectors + k - QD if k >= QD else k) for k in range(sectors)]
    across = [(a // QD * sectors + g + a % QD, b // QD * sectors + g + b % QD) for g in range(0, sectors, QD) for a, b in ACROSS]

    return {
        "lift": lift,
        "across": across,
        "envs": pairs(down, up, True),
        "partials": pairs(down, up, False),
        "up": column,
        "down": pairs(down, stay, True),
        "swap": pairs(stay, stay, True),
    }


def place():
    core, sector = lax.axis_index("chain"), lax.axis_index("sector")
    return core, lax.rem(sector, QD) < QD - 1, lax.rem(sector, QD) > 0, sector >= QD


def spreads(couplings):
    w = couplings[0].shape[0]
    rows = lax.broadcasted_iota(jnp.int32, (w * LO, w), 0) // LO
    pick = (rows == lax.broadcasted_iota(jnp.int32, (w * LO, w), 1)).astype(jnp.bfloat16)
    i = lax.broadcasted_iota(jnp.int32, (w * LO, w * LO), 0) % LO
    j = lax.broadcasted_iota(jnp.int32, (w * LO, w * LO), 1) % LO
    same = i == j

    def spread(mpo):
        tall = lax.dot_general(pick, mpo, (((1,), (1,)), ((), ())), preferred_element_type=jnp.float32).astype(jnp.bfloat16)
        full = lax.dot_general(tall, pick, (((1,), (1,)), ((), ())), preferred_element_type=jnp.float32)
        return jnp.where(same, full, 0.0).astype(jnp.bfloat16)

    return [spread(mpo) for mpo in couplings]


def couple(coupling, projected, column, out, lowest=0):
    count, blk = out.shape[0], out.shape[1]
    coupling = coupling[lowest * LO:(lowest + count) * LO]

    def part(a):
        pieces = [p[:, a:a + LO, column:column + blk].reshape(p.shape[0] * LO, blk) for p in projected]
        return pieces[0] if len(pieces) == 1 else jnp.concatenate(pieces, axis=0)

    for a in range(0, blk, 2 * LO):
        both = jnp.concatenate([part(a), part(a + LO)], axis=1)
        mixed = jnp.dot(coupling, both, preferred_element_type=jnp.float32).astype(out.dtype)
        out[:, a:a + LO, :] = mixed[:, :blk].reshape(count, LO, blk)
        out[:, a + LO:a + 2 * LO, :] = mixed[:, blk:].reshape(count, LO, blk)


def project(parts, counts, right, projected):
    slots = [(part, i) for part, count in zip(parts, counts) for i in range(count)]
    for w, (part, i) in enumerate(slots):
        projected[w] = jnp.dot(part[i], right, preferred_element_type=jnp.float32).astype(jnp.bfloat16)


def join(ours, theirs, mine, lowest, mixed, outs):
    left = jnp.concatenate([ours.T, theirs.T], axis=1)
    slots = [(out, i) for out in outs for i in range(out.shape[0])]
    blk = left.shape[0]
    for v in range(0, len(slots), 2):
        pair = range(v, min(v + 2, len(slots)))
        right = jnp.concatenate([jnp.concatenate([mine[lowest + u], mixed[u]], axis=0) for u in pair], axis=1)
        both = jnp.dot(left, right, preferred_element_type=jnp.float32)
        for n, u in enumerate(pair):
            out, i = slots[u]
            out[i] = both[:, n * blk:(n + 1) * blk].astype(out.dtype)


def prepare_kernel(here, other, rows, rows_other, states, states_other, local, send, later, live):
    core, inside, _, _ = place()

    def block(site, target, state, choice):
        same = core == site

        def exists(k):
            flag = jnp.where(same, here[:, k:k + 1], other[:, k:k + 1]) > 0
            return flag & inside if k >= 2 else flag

        def of(k):
            both = jnp.where(same, states[target, k], states_other[target, k])
            return jnp.where(exists(k), both, jnp.zeros_like(both))

        return of(state) if state == choice else jnp.where(target == 0, of(state), of(choice))

    send[0] = block(0, core, 3, 3)
    local[0, 0] = block(0, 1 - core, 1, 2)
    local[0, 1] = block(0, 1 - core, 0, 0)
    local[1, 0] = block(1, 1 - core, 1, 2)
    local[1, 1] = block(1, 1 - core, 0, 0)
    send[1] = block(0, core, 2, 1)
    later[0] = block(1, 1 - core, 3, 3)
    later[1] = block(1, 1 - core, 2, 1)
    for site in range(2):
        live[site] = jnp.broadcast_to(jnp.where(core == site, rows[...], rows_other[...]), live.shape[1:])


def behind(sent):
    core, _, from_down, from_up = place()
    return jnp.where(jnp.where(core == 1, from_down, from_up), sent, jnp.zeros_like(sent))


def own_kernel(site, counts, local, mpo, mpo_other, *refs):
    *parts, out_q, out_r, out_spread, projected = refs
    core = lax.axis_index("chain")
    pick = lambda state: jnp.where(core == site, mpo[state], mpo_other[state])
    middle, zero, both, outer = spreads([pick(2 - core), pick(0), pick(3), pick(1 + core)])
    project(parts, counts, jnp.concatenate([local[site, 0], local[site, 1]], axis=1), projected)
    couple(middle, [projected], 0, out_q)
    couple(zero, [projected], out_q.shape[1], out_r)
    out_spread[0] = both
    out_spread[1] = outer


def project_kernel(site, at, sent, part, projected):
    project([part], projected.shape[:1], behind(sent[at]), projected)


def head_kernel(site, at, local, sent, spread, mine, *refs):
    *projected, part, out, mine_projected, mixed = refs
    theirs = behind(sent[at])
    project([part], mine_projected.shape[:1], theirs, mine_projected)
    couple(spread[0], [*projected, mine_projected], 0, mixed)
    join(local[site, 0], theirs, mine, 0, mixed, [out])


def tail_kernel(site, at, lowest, pieces, local, sent, spread, mine, *refs):
    projected, out, mixed = refs[:pieces], refs[-2], refs[-1]
    couple(spread[0], projected, 0, mixed, lowest)
    join(local[site, 0], behind(sent[at]), mine, lowest, mixed, [out])


def keep_kernel(site, at, counts, local, sent, spread, mine, after, *refs):
    parts, refs = refs[:len(counts)], refs[len(counts):]
    *outs, projected, mixed = refs
    theirs = behind(sent[at + 1])
    project(parts, counts, theirs, projected)
    couple(spread[1], [projected], 0, mixed)
    join(local[site, 1], theirs, mine, 0, mixed, outs)


def give_kernel(parts, kept, *refs):
    envs, outs = refs[:parts], refs[parts:]
    core, width = lax.axis_index("chain"), kept.shape[0]
    for v, ((env, i), (out, j)) in enumerate(zip(blocks_of(envs, width), blocks_of(outs, width))):
        out[j] = jnp.where(core == 0, kept[v].astype(jnp.bfloat16), env[i])


def blocks_of(parts, width):
    extra = sum(part.shape[0] for part in parts) - width
    return [(part, i) for n, part in enumerate(parts) for i in range(part.shape[0] - (0 if n else extra))]


def total(site, live, valid, kept, arrived):
    blk = kept.shape[0]
    rows = live[site, 0:1, :]
    inside = (lax.broadcasted_iota(jnp.int32, (blk, blk), 0) < rows) & (lax.broadcasted_iota(jnp.int32, (blk, blk), 1) < rows)
    both = kept.astype(jnp.float32) + jnp.where(valid, arrived.astype(jnp.float32), 0.0)
    return jnp.where(inside, both, 0.0).astype(jnp.bfloat16)


def sum_kernel(lowest, live, arrived, kept, *refs):
    more, out = refs[0], refs[-1]
    core, _, from_down, from_up = place()
    valid = jnp.where(core == 0, from_down, from_up)
    count = arrived.shape[0]
    for v in range(count):
        out[v] = total(0, live, valid, kept[lowest + v], arrived[v])
    for i in range(out.shape[0] - count):
        out[count + i] = more[i]


def pick_kernel(from_down, from_up, out):
    core = lax.axis_index("chain")
    for i in range(out.shape[0]):
        out[i] = jnp.where(core == 0, from_up[i], from_down[i])


def last_kernel(lowest, parts, started, live, from_up_arrived, from_down_arrived, kept, *refs):
    *refs, out, new, sems = refs
    taken, envs = refs[:parts], refs[parts + started:]
    core, _, from_down, from_up = place()
    count, width = from_up_arrived.shape[0], kept.shape[0]
    received = [part[i] for part, i in blocks_of(taken, width)[lowest:lowest + count]]
    slots = blocks_of(envs, width)[lowest:lowest + count]
    copies = [pltpu.make_async_copy(new.at[t], out.at[t, pl.ds(lowest, count)], sems.at[t]) for t in range(2)]
    for v in range(count):
        here = total(1, live, from_up, kept[lowest + v], from_up_arrived[v])
        new[0, v] = jnp.where(core == 0, received[v], here)
    copies[0].start()
    for v, (env, i) in enumerate(slots):
        here = total(1, live, from_down, received[v], from_down_arrived[v])
        new[1, v] = jnp.where(core == 0, env[i], here)
    copies[1].start()
    for copy in copies:
        copy.wait()


VMEM = pl.BlockSpec(memory_space=pltpu.VMEM)
SMEM = pl.BlockSpec(memory_space=pltpu.SMEM)


def call(kernel, out_shape, in_specs, scratch=()):
    single = not isinstance(out_shape, (tuple, list))
    return pl.pallas_call(
        kernel,
        out_shape=out_shape,
        in_specs=in_specs,
        out_specs=VMEM if single else [VMEM] * len(out_shape),
        scratch_shapes=scratch,
        compiler_params=pltpu.CompilerParams(vmem_limit_bytes=24 << 20),
        cost_estimate=pl.CostEstimate(flops=1, bytes_accessed=1, transcendentals=0),
    )


def on_device(env_first, states, mpo, block_rows, present):
    pairs = rings(lax.axis_size("sector"))
    move = lambda value, name: lax.ppermute(value, AXES, pairs[name])
    core = lax.axis_index("chain")
    _, _, width, blk, _ = env_first.shape
    array = lambda *shape, dtype=jnp.bfloat16: jax.ShapeDtypeStruct(shape, dtype)
    blocks = lambda n, dtype=jnp.bfloat16: array(n, blk, blk, dtype=dtype)
    scratch = lambda n, m=1: pltpu.VMEM((n, blk, m * blk), jnp.bfloat16)
    half = blocks(width)
    spread_shape = array(2, width * LO, width * LO)
    lengths = cut(width, BC)
    ends = cut(width, DD)
    starts = lambda counts: [sum(counts[:i]) for i in range(len(counts))]

    env_first = env_first[:, 0]
    states, mpo, rows, here = states[0, :, :, 0], mpo[0], block_rows, present[:, :, 0]
    env = lax.dynamic_index_in_dim(env_first, core, 0, keepdims=False)
    arriving = move(env, "envs")
    states_other, mpo_other, rows_other, other = lax.optimization_barrier(tuple(move(x, "swap") for x in (states, mpo, rows, here)))
    local, send, later, live = call(
        prepare_kernel, [array(2, 2, blk, blk), array(2, blk, blk), array(2, blk, blk), array(2, 8, blk, dtype=jnp.int32)], [VMEM] * 6,
    )(here, other, rows, rows_other, states, states_other)
    sent = move(send, "envs")
    env = lax.optimization_barrier((env, local))[0]
    given = cut(width, EE)
    env = [move(env[low:low + n], "swap") for low, n in zip(starts(given), given)]

    own = lambda site, counts: call(
        functools.partial(own_kernel, site, counts), [half, half, spread_shape], [VMEM] * (3 + len(counts)), [scratch(width, 2)])

    def outgoing(site, at, sent, spread, mine, projected, part, count, counts):
        fixed = (local, sent, spread, mine)
        first, last = call(
            functools.partial(head_kernel, site, at), [blocks(counts[0]), blocks(count)], [VMEM] * (5 + len(projected)), [scratch(counts[0])],
        )(*fixed, *projected, part)
        projected = [*projected, last]
        out = [first]
        for low, n in list(zip(starts(counts), counts))[1:]:
            out.append(call(
                functools.partial(tail_kernel, site, at, low, len(projected)), blocks(n), [VMEM] * (4 + len(projected) + len(out)), [scratch(n)],
            )(*fixed, *projected, *out))
        return out

    mine_q, mine_r, spread = own(0, given)(local, mpo, mpo_other, *env)
    q = outgoing(0, 0, sent, spread, mine_q, [], arriving, width, lengths)
    arrived = [move(part, "partials") for part in q]
    whole = blocks(width, jnp.float32)
    kept = call(functools.partial(keep_kernel, 0, 0, (width,)), whole, [VMEM] * 6, [scratch(width)] * 2)(
        local, sent, spread, mine_r, q[-1], arriving)
    envs = []
    for low, n, part in zip(starts(lengths), lengths, arrived):
        extra = 0 if envs else later.shape[0]
        envs.append(call(functools.partial(sum_kernel, low), blocks(n + extra), [VMEM] * (4 + len(envs)))(live, part, kept, later, *envs))
    arriving = [
        call(pick_kernel, blocks(env.shape[0]), [VMEM] * 2)(move(env, "across"), move(env, "lift")) for env in envs
    ]
    sent, at = arriving[0], lengths[0]

    mine_q, mine_r, spread = own(1, lengths)(local, mpo, mpo_other, *envs)
    early = [
        call(functools.partial(project_kernel, 1, at), blocks(n), [VMEM] * 2)(sent, part) for part, n in zip(arriving[:-1], lengths)
    ]
    q = outgoing(1, at, sent, spread, mine_q, early, arriving[-1], lengths[-1], ends)
    downs = [move(part, "down") for part in q]
    ups = [move(part, "up") for part in q]
    kept = call(functools.partial(keep_kernel, 1, at, lengths), whole, [VMEM] * (5 + len(arriving)), [scratch(width)] * 2)(
        local, sent, spread, mine_r, q[-1], *arriving)
    given = call(functools.partial(give_kernel, len(envs)), [blocks(n) for n in cut(width, GG)], [VMEM] * (1 + len(envs)))(kept, *envs)
    taken = [move(part, "swap") for part in lax.optimization_barrier((given, downs[0]))[0]]
    hbm = pl.BlockSpec(memory_space=pl.ANY)
    result = []
    for i, low in enumerate(starts(ends)):
        result = [pl.pallas_call(
            functools.partial(last_kernel, low, len(taken), len(result)),
            out_shape=array(2, width, blk, blk),
            in_specs=[VMEM] * (4 + len(taken)) + [hbm] * len(result) + [VMEM] * len(envs),
            out_specs=hbm,
            scratch_shapes=[pltpu.VMEM((2, ends[i], blk, blk), jnp.bfloat16), pltpu.SemaphoreType.DMA((2,))],
            input_output_aliases={4 + len(taken): 0} if result else {},
            compiler_params=pltpu.CompilerParams(vmem_limit_bytes=24 << 20),
            cost_estimate=pl.CostEstimate(flops=1, bytes_accessed=1, transcendentals=0),
        )(live, ups[i], downs[i], kept, *taken, *result, *envs)]
    return result[0][None, :, None]


def solution(mesh):
    placed = (
        P(None, "sector", None, None, None),
        P("chain", None, None, "sector", None, None),
        P("chain", None, None, None),
        P("chain", "sector"),
        P("chain", None, "sector"),
    )
    return jax.shard_map(
        on_device,
        mesh=mesh,
        in_specs=placed,
        out_specs=P("chain", None, "sector", None, None, None),
        check_vma=False,
    )
```

time: 42.9 us -> 41.6 us (0.970)
  starting transfers between devices: 16.6 us -> 14.5 us
  waiting for transfers between devices: 14.1 us -> 15.6 us
  local copies, waits for them, and re-layouts: 1.34 us -> 0.83 us
    ppermute x20 -> x21, starting transfers between devices: 16.6 us -> 14.5 us  [on_device(): move = lambda value, name: lax.ppermute(value, AXES, pairs[name])]
    ppermute x20 -> x21, waiting for transfers between devices: 14.1 us -> 15.6 us  [on_device(): move = lambda value, name: lax.ppermute(value, AXES, pairs[name])]
    unnamed x9, local copies, waits for them, and re-layouts: 1.31 us -> 0.76 us
    pallas_call x13 -> x15, Pallas kernels: 7.76 us -> 7.71 us  [the longest x2 2.01 us: on_device(): pl.pallas_call(functools.partial(last_kernel, low, len(taken), len(result...]
  transfers between devices with their start and end apart: 20 -> 21, of which waited for: 11 -> 13; matrix products, arithmetic and copies ran while one was open for 0% -> 0% of each run, Pallas kernels for 17% -> 17%
where the time goes in v4:
time: 41.6 us; the launch traced here: 41.4 us
  waiting for transfers between devices  15.6 us (38%)
  starting transfers between devices  14.5 us (35%)
  Pallas kernels  9.65 us (23%)
  between operations  0.85 us (2%)
  local copies, waits for them, and re-layouts  0.83 us (2%)
    ppermute x21, waiting for transfers between devices, on_device(): move = lambda value, name: lax.ppermute(value, AXES, pairs[name])  15.6 us
    ppermute x21, starting transfers between devices, on_device(): move = lambda value, name: lax.ppermute(value, AXES, pairs[name])  14.5 us
    pallas_call x2, Pallas kernels, on_device(): pl.pallas_call(functools.partial(last_kernel, low, len(taken), len(result...  2.01 us
    pallas_call x2, Pallas kernels, outgoing(): call(functools.partial(head_kernel, site, at), [blocks(counts[0]), blocks...  1.33 us
    pallas_call x1, Pallas kernels, on_device(): mine_q, mine_r, spread = own(0, given)(local, mpo, mpo_other, *env)  1.17 us
    pallas_call x1, Pallas kernels, on_device(): mine_q, mine_r, spread = own(1, lengths)(local, mpo, mpo_other, *envs)  1.17 us
    pallas_call x2, Pallas kernels, outgoing(): call(functools.partial(tail_kernel, site, at, low, len(projected)), block...  0.86 us
  transfers between devices with their start and end apart: 21, of which 13 were waited for; matrix products, arithmetic and copies ran while one was open for 0% of the time, Pallas kernels for 17%

profile of v4, /device:TPU:0, one launch (start us, length us, event | category | flops | bytes accessed | tf_op | source)
XLA Modules:
  0.0 41.4 jit_solution(4557117111433197008)
XLA Ops:
  0.0 0.5 %collective-permute-start = (bf16[2,4,128,128]{3,2,1,0:T(8,128)(2,1)}, bf16[2,4,128,128]{3,2,1,0:T(8,128)(2,1)S(1)}, u32[]{:S(2)}, u32[]{:S(2)}) collective-permute-start(bf16[2,4,128,128]{3,2,1,0:T(8,128)(2,1)} %bitcast.10), channel_id=1, source_target_pairs={{0,16},{1,17},{2,18},{3,19},{4,20},{5,21},{6,22},{7,23},{8,24},{9,... | collective-permute-start | bytes 786440 | tf_op jit(solution)/shard_map/ppermute | solution.py:255
  0.5 0.7 %copy-done = bf16[2,1,15,128,128]{4,3,2,1,0:T(8,128)(2,1)S(1)} copy-done((bf16[2,1,15,128,128]{4,3,2,1,0:T(8,128)(2,1)S(1)}, bf16[2,1,15,128,128]{4,3,2,1,0:T(8,128)(2,1)}, u32[]{:S(2)}) %copy-start) | copy-done | bytes 983064
  1.3 2.4 %collective-permute-start.7 = (bf16[15,128,128]{2,1,0:T(8,128)(2,1)S(1)}, bf16[15,128,128]{2,1,0:T(8,128)(2,1)S(1)}, u32[]{:S(2)}, u32[]{:S(2)}) collective-permute-start(bf16[15,128,128]{2,1,0:T(8,128)(2,1)S(1)} %dynamic-slice_bitcast_fusion), channel_id=1, source_target_pairs={{0,17},{1,18},{2,19},{3,16},{4,21},{5,22},{6,23},{7,20},{8,25},{9,... | collective-permute-start | bytes 1474568 | tf_op jit(solution)/shard_map/ppermute | solution.py:255
  3.7 0.8 %collective-permute-start.1 = (bf16[4,15,15]{2,1,0:T(8,128)(2,1)S(1)}, bf16[4,15,15]{2,1,0:T(8,128)(2,1)S(1)}, u32[]{:S(2)}, u32[]{:S(2)}) collective-permute-start(bf16[4,15,15]{2,1,0:T(8,128)(2,1)S(1)} %bitcast.12), channel_id=1, source_target_pairs={{0,16},{1,17},{2,18},{3,19},{4,20},{5,21},{6,22},{7,23},{8,24},{9,... | collective-permute-start | bytes 5408 | tf_op jit(solution)/shard_map/ppermute | solution.py:255
  4.5 0.6 %collective-permute-start.3 = (s32[1,4]{1,0:T(1,128)S(1)}, s32[1,4]{1,0:T(1,128)S(1)}, u32[]{:S(2)}, u32[]{:S(2)}) collective-permute-start(s32[1,4]{1,0:T(1,128)S(1)} %bitcast.15), channel_id=1, source_target_pairs={{0,16},{1,17},{2,18},{3,19},{4,20},{5,21},{6,22},{7,23},{8,24},{9,... | collective-permute-start | bytes 56 | tf_op jit(solution)/shard_map/ppermute | solution.py:255
  5.8 0.6 %collective-permute-done.2.rows_other = s32[1,1]{1,0:T(1,128)} collective-permute-done((s32[1,1]{1,0:T(1,128)}, s32[1,1]{1,0:T(1,128)}, u32[]{:S(2)}, u32[]{:S(2)}) %collective-permute-start.2) | collective-permute-done | bytes 36 | tf_op jit(solution)/shard_map/ppermute | solution.py:255
  6.4 0.8 %shard_map.55 = (bf16[2,2,128,128]{3,2,1,0:T(8,128)(2,1)S(1)}, bf16[2,128,128]{2,1,0:T(8,128)(2,1)S(1)}, bf16[2,128,128]{2,1,0:T(8,128)(2,1)S(1)}, s32[2,8,128]{2,1,0:T(8,128)S(1)}) custom-call(s32[1,4]{1,0:T(1,128)S(1)} %bitcast.16, s32[1,4]{1,0:T(1,128)S(1)} %collective-permute-done.3.other, s32[1,1]{1,0:T(1,128)S(6)} %copy.12.rows, ...), custom_call_target="tpu_custom_call" | custom-call | flops 1 | bytes 1 | tf_op jit(solution)/shard_map/pallas_call | solution.py:272
  7.2 0.3 collective-permute-start.5
  7.5 0.3 collective-permute-start.6
  7.8 1.3 %collective-permute-start.4 = (bf16[2,128,128]{2,1,0:T(8,128)(2,1)S(1)}, bf16[2,128,128]{2,1,0:T(8,128)(2,1)S(1)}, u32[]{:S(2)}, u32[]{:S(2)}) collective-permute-start(bf16[2,128,128]{2,1,0:T(8,128)(2,1)S(1)} %get-tuple-element.35), channel_id=1, source_target_pairs={{0,17},{1,18},{2,19},{3,16},{4,21},{5,22},{6,23},{7,20},{8,25},{9,... | collective-permute-start | bytes 196616 | tf_op jit(solution)/shard_map/ppermute | solution.py:255
  9.2 1.2 %shard_map.56 = (bf16[15,128,128]{2,1,0:T(8,128)(2,1)S(1)}, bf16[15,128,128]{2,1,0:T(8,128)(2,1)S(1)}, bf16[2,240,240]{2,1,0:T(8,128)(2,1)S(1)}) custom-call(bf16[2,2,128,128]{3,2,1,0:T(8,128)(2,1)S(1)} %get-tuple-element.34.local, bf16[4,15,15]{2,1,0:T(8,128)(2,1)S(1)} %bitcast.13, bf16[4,15,15]{2,1,0:T(8,128)(2,1)S(1)} %collective-permute-done.1.mpo_other, ...), custom_call_target="tpu_custom_call" | custom-call | flops 1 | bytes 1 | tf_op jit(solution)/shard_map/pallas_call | solution.py:296
  10.3 3.0 %collective-permute-done.4.sent = bf16[2,128,128]{2,1,0:T(8,128)(2,1)S(1)} collective-permute-done((bf16[2,128,128]{2,1,0:T(8,128)(2,1)S(1)}, bf16[2,128,128]{2,1,0:T(8,128)(2,1)S(1)}, u32[]{:S(2)}, u32[]{:S(2)}) %collective-permute-start.4) | collective-permute-done | bytes 65568 | tf_op jit(solution)/shard_map/ppermute | solution.py:255
  13.3 0.7 %shard_map.57 = (bf16[7,128,128]{2,1,0:T(8,128)(2,1)S(1)}, bf16[15,128,128]{2,1,0:T(8,128)(2,1)S(1)}) custom-call(bf16[2,2,128,128]{3,2,1,0:T(8,128)(2,1)S(1)} %get-tuple-element.34.local, bf16[2,128,128]{2,1,0:T(8,128)(2,1)S(1)} %collective-permute-done.4.sent, bf16[2,240,240]{2,1,0:T(8,128)(2,1)S(1)} %get-tuple-element.38.spread, ...), custom_call_target="tpu_custom_call" | custom-call | flops 1 | bytes 1 | tf_op jit(solution)/shard_map/pallas_call | solution.py:285
  14.0 1.7 %collective-permute-start.8 = (bf16[7,128,128]{2,1,0:T(8,128)(2,1)S(1)}, bf16[7,128,128]{2,1,0:T(8,128)(2,1)S(1)}, u32[]{:S(2)}, u32[]{:S(2)}) collective-permute-start(bf16[7,128,128]{2,1,0:T(8,128)(2,1)S(1)} %get-tuple-element.40.refs_1_), channel_id=1, source_target_pairs={{0,1},{1,2},{2,3},{3,0},{4,5},{5,6},{6,7},{7,4},{8,9},{9,10},{10,1... | collective-permute-start | bytes 688136 | tf_op jit(solution)/shard_map/ppermute | solution.py:255
  15.8 0.4 %shard_map.58.after = bf16[8,128,128]{2,1,0:T(8,128)(2,1)S(1)} custom-call(bf16[2,2,128,128]{3,2,1,0:T(8,128)(2,1)S(1)} %get-tuple-element.34.local, bf16[2,128,128]{2,1,0:T(8,128)(2,1)S(1)} %collective-permute-done.4.sent, bf16[2,240,240]{2,1,0:T(8,128)(2,1)S(1)} %get-tuple-element.38.spread, bf16[15,128,128]{2,1,0:T(8,128)(2,1)S(1)} %get-tuple-element.39.mine, ...), custom_call_target="tpu_custom_call" | custom-call | flops 1 | bytes 1 | tf_op jit(solution)/shard_map/pallas_call | solution.py:291
  16.2 1.5 %collective-permute-start.11 = (bf16[8,128,128]{2,1,0:T(8,128)(2,1)S(1)}, bf16[8,128,128]{2,1,0:T(8,128)(2,1)S(1)}, u32[]{:S(2)}, u32[]{:S(2)}) collective-permute-start(bf16[8,128,128]{2,1,0:T(8,128)(2,1)S(1)} %shard_map.58.after), channel_id=1, source_target_pairs={{0,1},{1,2},{2,3},{3,0},{4,5},{5,6},{6,7},{7,4},{8,9},{9,10},{10,1... | collective-permute-start | bytes 786440 | tf_op jit(solution)/shard_map/ppermute | solution.py:255
  17.8 0.8 %shard_map.59.kept = f32[15,128,128]{2,1,0:T(8,128)S(1)} custom-call(bf16[2,2,128,128]{3,2,1,0:T(8,128)(2,1)S(1)} %get-tuple-element.34.local, bf16[2,128,128]{2,1,0:T(8,128)(2,1)S(1)} %collective-permute-done.4.sent, bf16[2,240,240]{2,1,0:T(8,128)(2,1)S(1)} %get-tuple-element.38.spread, bf16[15,128,128]{2,1,0:T(8,128)(2,1)S(1)} %get-tuple-element.41.mine, ...), custom_call_target="tpu_custom_call" | custom-call | flops 1 | bytes 1 | tf_op jit(solution)/shard_map/pallas_call | solution.py:300
  18.6 2.4 %collective-permute-done.8.arrived = bf16[7,128,128]{2,1,0:T(8,128)(2,1)S(1)} collective-permute-done((bf16[7,128,128]{2,1,0:T(8,128)(2,1)S(1)}, bf16[7,128,128]{2,1,0:T(8,128)(2,1)S(1)}, u32[]{:S(2)}, u32[]{:S(2)}) %collective-permute-start.8) | collective-permute-done | bytes 229408 | tf_op jit(solution)/shard_map/ppermute | solution.py:255
  21.0 0.1 shard_map.60.refs_1_.refs_0_.refs_3_.refs_4_
  21.2 0.5 %collective-permute-start.9 = (bf16[9,128,128]{2,1,0:T(8,128)(2,1)S(1)}, bf16[9,128,128]{2,1,0:T(8,128)(2,1)S(1)}, u32[]{:S(2)}, u32[]{:S(2)}) collective-permute-start(bf16[9,128,128]{2,1,0:T(8,128)(2,1)S(1)} %shard_map.60.refs_1_.refs_0_.refs_3_.refs_4_), channel_id=1, source_target_pairs={{16,17},{17,18},{18,19},{19,1},{1,3},{3,2},{2,0},{0,16},{20,21},{2... | collective-permute-start | bytes 884744 | tf_op jit(solution)/shard_map/ppermute | solution.py:255
  21.6 2.2 %collective-permute-done.11.arrived = bf16[8,128,128]{2,1,0:T(8,128)(2,1)S(1)} collective-permute-done((bf16[8,128,128]{2,1,0:T(8,128)(2,1)S(1)}, bf16[8,128,128]{2,1,0:T(8,128)(2,1)S(1)}, u32[]{:S(2)}, u32[]{:S(2)}) %collective-permute-start.11) | collective-permute-done | bytes 262176 | tf_op jit(solution)/shard_map/ppermute | solution.py:255
  23.8 0.1 shard_map.62.refs_1_.refs_4_.refs_5_
  24.0 0.5 %collective-permute-start.12 = (bf16[8,128,128]{2,1,0:T(8,128)(2,1)S(1)}, bf16[8,128,128]{2,1,0:T(8,128)(2,1)S(1)}, u32[]{:S(2)}, u32[]{:S(2)}) collective-permute-start(bf16[8,128,128]{2,1,0:T(8,128)(2,1)S(1)} %shard_map.62.refs_1_.refs_4_.refs_5_), channel_id=1, source_target_pairs={{16,17},{17,18},{18,19},{19,1},{1,3},{3,2},{2,0},{0,16},{20,21},{2... | collective-permute-start | bytes 786440 | tf_op jit(solution)/shard_map/ppermute | solution.py:255
  24.5 0.9 %collective-permute-done.10.from_up = bf16[9,128,128]{2,1,0:T(8,128)(2,1)S(1)} collective-permute-done((bf16[9,128,128]{2,1,0:T(8,128)(2,1)S(1)}, bf16[9,128,128]{2,1,0:T(8,128)(2,1)S(1)}, u32[]{:S(2)}, u32[]{:S(2)}) %collective-permute-start.10) | collective-permute-done | bytes 294944 | tf_op jit(solution)/shard_map/ppermute | solution.py:255
  25.4 2.5 %collective-permute-done.9.from_down = bf16[9,128,128]{2,1,0:T(8,128)(2,1)S(1)} collective-permute-done((bf16[9,128,128]{2,1,0:T(8,128)(2,1)S(1)}, bf16[9,128,128]{2,1,0:T(8,128)(2,1)S(1)}, u32[]{:S(2)}, u32[]{:S(2)}) %collective-permute-start.9) | collective-permute-done | bytes 294944 | tf_op jit(solution)/shard_map/ppermute | solution.py:255
  27.9 0.1 shard_map.61.sent.part.refs_0_
  28.0 1.2 %shard_map.63 = (bf16[15,128,128]{2,1,0:T(8,128)(2,1)S(1)}, bf16[15,128,128]{2,1,0:T(8,128)(2,1)S(1)}, bf16[2,240,240]{2,1,0:T(8,128)(2,1)S(1)}) custom-call(bf16[2,2,128,128]{3,2,1,0:T(8,128)(2,1)S(1)} %get-tuple-element.34.local, bf16[4,15,15]{2,1,0:T(8,128)(2,1)S(1)} %bitcast.14, bf16[4,15,15]{2,1,0:T(8,128)(2,1)S(1)} %collective-permute-done.1.mpo_other, ...), custom_call_target="tpu_custom_call" | custom-call | flops 1 | bytes 1 | tf_op jit(solution)/shard_map/pallas_call | solution.py:311
  29.2 0.2 shard_map.64.refs_0_
  29.4 1.3 %collective-permute-done.12.from_down = bf16[8,128,128]{2,1,0:T(8,128)(2,1)S(1)} collective-permute-done((bf16[8,128,128]{2,1,0:T(8,128)(2,1)S(1)}, bf16[8,128,128]{2,1,0:T(8,128)(2,1)S(1)}, u32[]{:S(2)}, u32[]{:S(2)}) %collective-permute-start.12) | collective-permute-done | bytes 262176 | tf_op jit(solution)/shard_map/ppermute | solution.py:255
  30.7 0.1 shard_map.65.refs_1_
  30.8 0.6 %shard_map.66 = (bf16[7,128,128]{2,1,0:T(8,128)(2,1)S(1)}, bf16[8,128,128]{2,1,0:T(8,128)(2,1)S(1)}) custom-call(bf16[2,2,128,128]{3,2,1,0:T(8,128)(2,1)S(1)} %get-tuple-element.34.local, bf16[9,128,128]{2,1,0:T(8,128)(2,1)S(1)} %shard_map.61.sent.part.refs_0_, bf16[2,240,240]{2,1,0:T(8,128)(2,1)S(1)} %get-tuple-element.44.spread, ...), custom_call_target="tpu_custom_call" | custom-call | flops 1 | bytes 1 | tf_op jit(solution)/shard_map/pallas_call | solution.py:285
  31.4 0.1 collective-permute-start.16
  31.5 0.5 %collective-permute-start.20 = (bf16[7,128,128]{2,1,0:T(8,128)(2,1)S(1)}, bf16[7,128,128]{2,1,0:T(8,128)(2,1)S(1)}, u32[]{:S(2)}, u32[]{:S(2)}) collective-permute-start(bf16[7,128,128]{2,1,0:T(8,128)(2,1)S(1)} %get-tuple-element.47.refs_2_), channel_id=1, source_target_pairs={{16,20},{17,21},{18,22},{19,23},{20,24},{21,25},{22,26},{23,27},{2... | collective-permute-start | bytes 688136 | tf_op jit(solution)/shard_map/ppermute | solution.py:255
  32.0 0.4 %shard_map.67.after = bf16[8,128,128]{2,1,0:T(8,128)(2,1)S(1)} custom-call(bf16[2,2,128,128]{3,2,1,0:T(8,128)(2,1)S(1)} %get-tuple-element.34.local, bf16[9,128,128]{2,1,0:T(8,128)(2,1)S(1)} %shard_map.61.sent.part.refs_0_, bf16[2,240,240]{2,1,0:T(8,128)(2,1)S(1)} %get-tuple-element.44.spread, bf16[15,128,128]{2,1,0:T(8,128)(2,1)S(1)} %get-tuple-element.45.mine, ...), custom_call_target="tpu_custom_call" | custom-call | flops 1 | bytes 1 | tf_op jit(solution)/shard_map/pallas_call | solution.py:291
  32.4 1.1 %collective-permute-start.15 = (bf16[8,128,128]{2,1,0:T(8,128)(2,1)S(1)}, bf16[8,128,128]{2,1,0:T(8,128)(2,1)S(1)}, u32[]{:S(2)}, u32[]{:S(2)}) collective-permute-start(bf16[8,128,128]{2,1,0:T(8,128)(2,1)S(1)} %shard_map.67.after), channel_id=1, source_target_pairs={{0,17},{1,18},{2,19},{3,16},{4,21},{5,22},{6,23},{7,20},{8,25},{9,... | collective-permute-start | bytes 786440 | tf_op jit(solution)/shard_map/ppermute | solution.py:255
  33.6 0.2 collective-permute-start.14
  33.7 0.8 %shard_map.68.kept = f32[15,128,128]{2,1,0:T(8,128)S(1)} custom-call(bf16[2,2,128,128]{3,2,1,0:T(8,128)(2,1)S(1)} %get-tuple-element.34.local, bf16[9,128,128]{2,1,0:T(8,128)(2,1)S(1)} %shard_map.61.sent.part.refs_0_, bf16[2,240,240]{2,1,0:T(8,128)(2,1)S(1)} %get-tuple-element.44.spread, bf16[15,128,128]{2,1,0:T(8,128)(2,1)S(1)} %get-tuple-element.48.mine, ...), custom_call_target="tpu_custom_call" | custom-call | flops 1 | bytes 1 | tf_op jit(solution)/shard_map/pallas_call | solution.py:318
  34.6 0.1 shard_map.69
  34.7 0.4 collective-permute-done.16.from_down_arrived
  35.0 2.0 %collective-permute-start.17 = (bf16[5,128,128]{2,1,0:T(8,128)(2,1)S(1)}, bf16[5,128,128]{2,1,0:T(8,128)(2,1)S(1)}, u32[]{:S(2)}, u32[]{:S(2)}) collective-permute-start(bf16[5,128,128]{2,1,0:T(8,128)(2,1)S(1)} %get-tuple-element.52), channel_id=1, source_target_pairs={{0,16},{1,17},{2,18},{3,19},{4,20},{5,21},{6,22},{7,23},{8,24},{9,... | collective-permute-start | bytes 491528 | tf_op jit(solution)/shard_map/ppermute | solution.py:255
  37.1 0.5 %collective-permute-done.20.from_up_arrived = bf16[7,128,128]{2,1,0:T(8,128)(2,1)S(1)} collective-permute-done((bf16[7,128,128]{2,1,0:T(8,128)(2,1)S(1)}, bf16[7,128,128]{2,1,0:T(8,128)(2,1)S(1)}, u32[]{:S(2)}, u32[]{:S(2)}) %collective-permute-start.20) | collective-permute-done | bytes 229408 | tf_op jit(solution)/shard_map/ppermute | solution.py:255
  37.5 0.0 collective-permute-start.19
  37.6 0.5 %collective-permute-done.17.refs_0_ = bf16[5,128,128]{2,1,0:T(8,128)(2,1)S(1)} collective-permute-done((bf16[5,128,128]{2,1,0:T(8,128)(2,1)S(1)}, bf16[5,128,128]{2,1,0:T(8,128)(2,1)S(1)}, u32[]{:S(2)}, u32[]{:S(2)}) %collective-permute-start.17) | collective-permute-done | bytes 163872 | tf_op jit(solution)/shard_map/ppermute | solution.py:255
  38.1 0.4 collective-permute-done.18.refs_1_
  38.5 0.5 %collective-permute-done.19.refs_2_ = bf16[5,128,128]{2,1,0:T(8,128)(2,1)S(1)} collective-permute-done((bf16[5,128,128]{2,1,0:T(8,128)(2,1)S(1)}, bf16[5,128,128]{2,1,0:T(8,128)(2,1)S(1)}, u32[]{:S(2)}, u32[]{:S(2)}) %collective-permute-start.19) | collective-permute-done | bytes 163872 | tf_op jit(solution)/shard_map/ppermute | solution.py:255
  38.9 1.0 %shard_map.70.refs_3_ = bf16[2,15,128,128]{3,2,1,0:T(8,128)(2,1)} custom-call(s32[2,8,128]{2,1,0:T(8,128)S(1)} %get-tuple-element.33.live, bf16[7,128,128]{2,1,0:T(8,128)(2,1)S(1)} %collective-permute-done.20.from_up_arrived, bf16[7,128,128]{2,1,0:T(8,128)(2,1)S(1)} %collective-permute-done.16.from_down_arrived, f32[15,128,128]{2,1,0:T(8,128)S(1)} %shard_map.68.kept, ...), custom_call_target="tpu_custom_call" | custom-call | flops 1 | bytes 1 | tf_op jit(solution)/shard_map/pallas_call | solution.py:325
  39.9 0.4 %collective-permute-done.14.from_up_arrived = bf16[8,128,128]{2,1,0:T(8,128)(2,1)S(1)} collective-permute-done((bf16[8,128,128]{2,1,0:T(8,128)(2,1)S(1)}, bf16[8,128,128]{2,1,0:T(8,128)(2,1)S(1)}, u32[]{:S(2)}, u32[]{:S(2)}) %collective-permute-start.14) | collective-permute-done | bytes 262176 | tf_op jit(solution)/shard_map/ppermute | solution.py:255
  40.4 1.0 %shard_map.71 = bf16[2,15,128,128]{3,2,1,0:T(8,128)(2,1)} custom-call(s32[2,8,128]{2,1,0:T(8,128)S(1)} %get-tuple-element.33.live, bf16[8,128,128]{2,1,0:T(8,128)(2,1)S(1)} %collective-permute-done.14.from_up_arrived, bf16[8,128,128]{2,1,0:T(8,128)(2,1)S(1)} %collective-permute-done.15.from_down_arrived, ...), custom_call_target="tpu_custom_call", output_to_operand_aliasing={{}: (7, {})} | custom-call | flops 1 | bytes 1 | tf_op jit(solution)/shard_map/pallas_call | solution.py:325
  (23 shorter events, 0.2 us)
Async XLA Ops:
  0.0 1.2 %copy-start = (bf16[2,1,15,128,128]{4,3,2,1,0:T(8,128)(2,1)S(1)}, bf16[2,1,15,128,128]{4,3,2,1,0:T(8,128)(2,1)}, u32[]{:S(2)}) copy-start(bf16[2,1,15,128,128]{4,3,2,1,0:T(8,128)(2,1)} %param.5) | copy-start | bytes 2949124
  0.0 6.3 %collective-permute-start = (bf16[2,4,128,128]{3,2,1,0:T(8,128)(2,1)}, bf16[2,4,128,128]{3,2,1,0:T(8,128)(2,1)S(1)}, u32[]{:S(2)}, u32[]{:S(2)}) collective-permute-start(bf16[2,4,128,128]{3,2,1,0:T(8,128)(2,1)} %bitcast.10), channel_id=1, source_target_pairs={{0,16},{1,17},{2,18},{3,19},{4,20},{5,21},{6,22},{7,23},{8,24},{9,... | collective-permute-start | bytes 786440 | tf_op jit(solution)/shard_map/ppermute | solution.py:255
  1.2 2.5 %copy-start.3 = (bf16[1,4,15,15]{3,1,2,0:T(4,128)(2,1)S(1)}, bf16[1,4,15,15]{3,1,2,0:T(4,128)(2,1)}, u32[]{:S(2)}) copy-start(bf16[1,4,15,15]{3,1,2,0:T(4,128)(2,1)} %param.7) | copy-start | bytes 5404
  1.2 5.2 %copy-start.1 = (bf16[1,2,4,1,128,128]{5,4,3,2,1,0:T(8,128)(2,1)S(1)}, bf16[1,2,4,1,128,128]{5,4,3,2,1,0:T(8,128)(2,1)}, u32[]{:S(2)}) copy-start(bf16[1,2,4,1,128,128]{5,4,3,2,1,0:T(8,128)(2,1)} %param.6) | copy-start | bytes 786436
  1.3 12.1 %collective-permute-start.7 = (bf16[15,128,128]{2,1,0:T(8,128)(2,1)S(1)}, bf16[15,128,128]{2,1,0:T(8,128)(2,1)S(1)}, u32[]{:S(2)}, u32[]{:S(2)}) collective-permute-start(bf16[15,128,128]{2,1,0:T(8,128)(2,1)S(1)} %dynamic-slice_bitcast_fusion), channel_id=1, source_target_pairs={{0,17},{1,18},{2,19},{3,16},{4,21},{5,22},{6,23},{7,20},{8,25},{9,... | collective-permute-start | bytes 1474568 | tf_op jit(solution)/shard_map/ppermute | solution.py:255
  3.7 0.8 %copy-start.2 = (s32[1,4,1]{1,2,0:T(1,128)S(1)}, s32[1,4,1]{1,2,0:T(1,128)}, u32[]{:S(2)}) copy-start(s32[1,4,1]{1,2,0:T(1,128)} %param.9) | copy-start | bytes 52
  3.7 2.7 %collective-permute-start.1 = (bf16[4,15,15]{2,1,0:T(8,128)(2,1)S(1)}, bf16[4,15,15]{2,1,0:T(8,128)(2,1)S(1)}, u32[]{:S(2)}, u32[]{:S(2)}) collective-permute-start(bf16[4,15,15]{2,1,0:T(8,128)(2,1)S(1)} %bitcast.12), channel_id=1, source_target_pairs={{0,16},{1,17},{2,18},{3,19},{4,20},{5,21},{6,22},{7,23},{8,24},{9,... | collective-permute-start | bytes 5408 | tf_op jit(solution)/shard_map/ppermute | solution.py:255
  4.5 1.8 %collective-permute-start.3 = (s32[1,4]{1,0:T(1,128)S(1)}, s32[1,4]{1,0:T(1,128)S(1)}, u32[]{:S(2)}, u32[]{:S(2)}) collective-permute-start(s32[1,4]{1,0:T(1,128)S(1)} %bitcast.15), channel_id=1, source_target_pairs={{0,16},{1,17},{2,18},{3,19},{4,20},{5,21},{6,22},{7,23},{8,24},{9,... | collective-permute-start | bytes 56 | tf_op jit(solution)/shard_map/ppermute | solution.py:255
  5.1 1.2 %collective-permute-start.2 = (s32[1,1]{1,0:T(1,128)}, s32[1,1]{1,0:T(1,128)}, u32[]{:S(2)}, u32[]{:S(2)}) collective-permute-start(s32[1,1]{1,0:T(1,128)} %param.8), channel_id=1, source_target_pairs={{0,16},{1,17},{2,18},{3,19},{4,20},{5,21},{6,22},{7,23},{8,24},{9,... | collective-permute-start | bytes 20 | tf_op jit(solution)/shard_map/ppermute | solution.py:255
  7.2 2.0 %collective-permute-start.5 = (bf16[8,128,128]{2,1,0:T(8,128)(2,1)S(1)}, bf16[8,128,128]{2,1,0:T(8,128)(2,1)S(1)}, u32[]{:S(2)}, u32[]{:S(2)}) collective-permute-start(bf16[8,128,128]{2,1,0:T(8,128)(2,1)S(1)} %slice.6), channel_id=1, source_target_pairs={{0,16},{1,17},{2,18},{3,19},{4,20},{5,21},{6,22},{7,23},{8,24},{9,... | collective-permute-start | bytes 786440 | tf_op jit(solution)/shard_map/ppermute | solution.py:255
  7.5 1.7 %collective-permute-start.6 = (bf16[7,128,128]{2,1,0:T(8,128)(2,1)S(1)}, bf16[7,128,128]{2,1,0:T(8,128)(2,1)S(1)}, u32[]{:S(2)}, u32[]{:S(2)}) collective-permute-start(bf16[7,128,128]{2,1,0:T(8,128)(2,1)S(1)} %slice.7), channel_id=1, source_target_pairs={{0,16},{1,17},{2,18},{3,19},{4,20},{5,21},{6,22},{7,23},{8,24},{9,... | collective-permute-start | bytes 688136 | tf_op jit(solution)/shard_map/ppermute | solution.py:255
  7.8 5.5 %collective-permute-start.4 = (bf16[2,128,128]{2,1,0:T(8,128)(2,1)S(1)}, bf16[2,128,128]{2,1,0:T(8,128)(2,1)S(1)}, u32[]{:S(2)}, u32[]{:S(2)}) collective-permute-start(bf16[2,128,128]{2,1,0:T(8,128)(2,1)S(1)} %get-tuple-element.35), channel_id=1, source_target_pairs={{0,17},{1,18},{2,19},{3,16},{4,21},{5,22},{6,23},{7,20},{8,25},{9,... | collective-permute-start | bytes 196616 | tf_op jit(solution)/shard_map/ppermute | solution.py:255
  14.0 7.0 %collective-permute-start.8 = (bf16[7,128,128]{2,1,0:T(8,128)(2,1)S(1)}, bf16[7,128,128]{2,1,0:T(8,128)(2,1)S(1)}, u32[]{:S(2)}, u32[]{:S(2)}) collective-permute-start(bf16[7,128,128]{2,1,0:T(8,128)(2,1)S(1)} %get-tuple-element.40.refs_1_), channel_id=1, source_target_pairs={{0,1},{1,2},{2,3},{3,0},{4,5},{5,6},{6,7},{7,4},{8,9},{9,10},{10,1... | collective-permute-start | bytes 688136 | tf_op jit(solution)/shard_map/ppermute | solution.py:255
  16.2 7.6 %collective-permute-start.11 = (bf16[8,128,128]{2,1,0:T(8,128)(2,1)S(1)}, bf16[8,128,128]{2,1,0:T(8,128)(2,1)S(1)}, u32[]{:S(2)}, u32[]{:S(2)}) collective-permute-start(bf16[8,128,128]{2,1,0:T(8,128)(2,1)S(1)} %shard_map.58.after), channel_id=1, source_target_pairs={{0,1},{1,2},{2,3},{3,0},{4,5},{5,6},{6,7},{7,4},{8,9},{9,10},{10,1... | collective-permute-start | bytes 786440 | tf_op jit(solution)/shard_map/ppermute | solution.py:255
  21.1 4.3 %collective-permute-start.10 = (bf16[9,128,128]{2,1,0:T(8,128)(2,1)S(1)}, bf16[9,128,128]{2,1,0:T(8,128)(2,1)S(1)}, u32[]{:S(2)}, u32[]{:S(2)}) collective-permute-start(bf16[9,128,128]{2,1,0:T(8,128)(2,1)S(1)} %shard_map.60.refs_1_.refs_0_.refs_3_.refs_4_), channel_id=1, source_target_pairs={{0,4},{1,5},{2,6},{3,7},{4,8},{5,9},{6,10},{7,11},{8,12},{9,13},{1... | collective-permute-start | bytes 884744 | tf_op jit(solution)/shard_map/ppermute | solution.py:255
  21.2 6.8 %collective-permute-start.9 = (bf16[9,128,128]{2,1,0:T(8,128)(2,1)S(1)}, bf16[9,128,128]{2,1,0:T(8,128)(2,1)S(1)}, u32[]{:S(2)}, u32[]{:S(2)}) collective-permute-start(bf16[9,128,128]{2,1,0:T(8,128)(2,1)S(1)} %shard_map.60.refs_1_.refs_0_.refs_3_.refs_4_), channel_id=1, source_target_pairs={{16,17},{17,18},{18,19},{19,1},{1,3},{3,2},{2,0},{0,16},{20,21},{2... | collective-permute-start | bytes 884744 | tf_op jit(solution)/shard_map/ppermute | solution.py:255
  23.9 5.5 %collective-permute-start.13 = (bf16[8,128,128]{2,1,0:T(8,128)(2,1)S(1)}, bf16[8,128,128]{2,1,0:T(8,128)(2,1)S(1)}, u32[]{:S(2)}, u32[]{:S(2)}) collective-permute-start(bf16[8,128,128]{2,1,0:T(8,128)(2,1)S(1)} %shard_map.62.refs_1_.refs_4_.refs_5_), channel_id=1, source_target_pairs={{0,4},{1,5},{2,6},{3,7},{4,8},{5,9},{6,10},{7,11},{8,12},{9,13},{1... | collective-permute-start | bytes 786440 | tf_op jit(solution)/shard_map/ppermute | solution.py:255
  24.0 6.8 %collective-permute-start.12 = (bf16[8,128,128]{2,1,0:T(8,128)(2,1)S(1)}, bf16[8,128,128]{2,1,0:T(8,128)(2,1)S(1)}, u32[]{:S(2)}, u32[]{:S(2)}) collective-permute-start(bf16[8,128,128]{2,1,0:T(8,128)(2,1)S(1)} %shard_map.62.refs_1_.refs_4_.refs_5_), channel_id=1, source_target_pairs={{16,17},{17,18},{18,19},{19,1},{1,3},{3,2},{2,0},{0,16},{20,21},{2... | collective-permute-start | bytes 786440 | tf_op jit(solution)/shard_map/ppermute | solution.py:255
  31.4 3.6 %collective-permute-start.16 = (bf16[7,128,128]{2,1,0:T(8,128)(2,1)S(1)}, bf16[7,128,128]{2,1,0:T(8,128)(2,1)S(1)}, u32[]{:S(2)}, u32[]{:S(2)}) collective-permute-start(bf16[7,128,128]{2,1,0:T(8,128)(2,1)S(1)} %get-tuple-element.47.refs_2_), channel_id=1, source_target_pairs={{0,17},{1,18},{2,19},{3,16},{4,21},{5,22},{6,23},{7,20},{8,25},{9,... | collective-permute-start | bytes 688136 | tf_op jit(solution)/shard_map/ppermute | solution.py:255
  31.5 6.0 %collective-permute-start.20 = (bf16[7,128,128]{2,1,0:T(8,128)(2,1)S(1)}, bf16[7,128,128]{2,1,0:T(8,128)(2,1)S(1)}, u32[]{:S(2)}, u32[]{:S(2)}) collective-permute-start(bf16[7,128,128]{2,1,0:T(8,128)(2,1)S(1)} %get-tuple-element.47.refs_2_), channel_id=1, source_target_pairs={{16,20},{17,21},{18,22},{19,23},{20,24},{21,25},{22,26},{23,27},{2... | collective-permute-start | bytes 688136 | tf_op jit(solution)/shard_map/ppermute | solution.py:255
  32.4 7.5 %collective-permute-start.15 = (bf16[8,128,128]{2,1,0:T(8,128)(2,1)S(1)}, bf16[8,128,128]{2,1,0:T(8,128)(2,1)S(1)}, u32[]{:S(2)}, u32[]{:S(2)}) collective-permute-start(bf16[8,128,128]{2,1,0:T(8,128)(2,1)S(1)} %shard_map.67.after), channel_id=1, source_target_pairs={{0,17},{1,18},{2,19},{3,16},{4,21},{5,22},{6,23},{7,20},{8,25},{9,... | collective-permute-start | bytes 786440 | tf_op jit(solution)/shard_map/ppermute | solution.py:255
  33.6 6.8 %collective-permute-start.14 = (bf16[8,128,128]{2,1,0:T(8,128)(2,1)S(1)}, bf16[8,128,128]{2,1,0:T(8,128)(2,1)S(1)}, u32[]{:S(2)}, u32[]{:S(2)}) collective-permute-start(bf16[8,128,128]{2,1,0:T(8,128)(2,1)S(1)} %shard_map.67.after), channel_id=1, source_target_pairs={{16,20},{17,21},{18,22},{19,23},{20,24},{21,25},{22,26},{23,27},{2... | collective-permute-start | bytes 786440 | tf_op jit(solution)/shard_map/ppermute | solution.py:255
  35.0 3.1 %collective-permute-start.17 = (bf16[5,128,128]{2,1,0:T(8,128)(2,1)S(1)}, bf16[5,128,128]{2,1,0:T(8,128)(2,1)S(1)}, u32[]{:S(2)}, u32[]{:S(2)}) collective-permute-start(bf16[5,128,128]{2,1,0:T(8,128)(2,1)S(1)} %get-tuple-element.52), channel_id=1, source_target_pairs={{0,16},{1,17},{2,18},{3,19},{4,20},{5,21},{6,22},{7,23},{8,24},{9,... | collective-permute-start | bytes 491528 | tf_op jit(solution)/shard_map/ppermute | solution.py:255
  37.1 1.4 %collective-permute-start.18 = (bf16[5,128,128]{2,1,0:T(8,128)(2,1)S(1)}, bf16[5,128,128]{2,1,0:T(8,128)(2,1)S(1)}, u32[]{:S(2)}, u32[]{:S(2)}) collective-permute-start(bf16[5,128,128]{2,1,0:T(8,128)(2,1)S(1)} %get-tuple-element.53), channel_id=1, source_target_pairs={{0,16},{1,17},{2,18},{3,19},{4,20},{5,21},{6,22},{7,23},{8,24},{9,... | collective-permute-start | bytes 491528 | tf_op jit(solution)/shard_map/ppermute | solution.py:255
  37.5 1.4 %collective-permute-start.19 = (bf16[5,128,128]{2,1,0:T(8,128)(2,1)S(1)}, bf16[5,128,128]{2,1,0:T(8,128)(2,1)S(1)}, u32[]{:S(2)}, u32[]{:S(2)}) collective-permute-start(bf16[5,128,128]{2,1,0:T(8,128)(2,1)S(1)} %get-tuple-element.54), channel_id=1, source_target_pairs={{0,16},{1,17},{2,18},{3,19},{4,20},{5,21},{6,22},{7,23},{8,24},{9,... | collective-permute-start | bytes 491528 | tf_op jit(solution)/shard_map/ppermute | solution.py:255

commit v5 on v4

--- a/solution.py
+++ b/solution.py
@@ -13,6 +13,7 @@
 BC = (7, 8)
 EE = (8, 7)
 DD = (7, 8)
+STEP = 3
 GG = (5, 5, 5)
 ACROSS = [(4, 5), (5, 6), (6, 7), (7, 1), (1, 3), (3, 2), (2, 0), (0, 4)]
 
@@ -220,15 +221,18 @@
     count, width = from_up_arrived.shape[0], kept.shape[0]
     received = [part[i] for part, i in blocks_of(taken, width)[lowest:lowest + count]]
     slots = blocks_of(envs, width)[lowest:lowest + count]
-    copies = [pltpu.make_async_copy(new.at[t], out.at[t, pl.ds(lowest, count)], sems.at[t]) for t in range(2)]
-    for v in range(count):
-        here = total(1, live, from_up, kept[lowest + v], from_up_arrived[v])
-        new[0, v] = jnp.where(core == 0, received[v], here)
-    copies[0].start()
-    for v, (env, i) in enumerate(slots):
-        here = total(1, live, from_down, received[v], from_down_arrived[v])
-        new[1, v] = jnp.where(core == 0, env[i], here)
-    copies[1].start()
+    steps = [(low, min(low + STEP, count)) for low in range(0, count, STEP)]
+    copies = []
+    for low, high in steps:
+        for v in range(low, high):
+            env, i = slots[v]
+            zero = total(1, live, from_up, kept[lowest + v], from_up_arrived[v])
+            one = total(1, live, from_down, received[v], from_down_arrived[v])
+            new[0, v] = jnp.where(core == 0, received[v], zero)
+            new[1, v] = jnp.where(core == 0, env[i], one)
+        part = pl.ds(low, high - low)
+        copies.append(pltpu.make_async_copy(new.at[:, part], out.at[:, pl.ds(lowest + low, high - low)], sems.at[len(copies)]))
+        copies[-1].start()
     for copy in copies:
         copy.wait()
 
@@ -327,7 +331,7 @@
             out_shape=array(2, width, blk, blk),
             in_specs=[VMEM] * (4 + len(taken)) + [hbm] * len(result) + [VMEM] * len(envs),
             out_specs=hbm,
-            scratch_shapes=[pltpu.VMEM((2, ends[i], blk, blk), jnp.bfloat16), pltpu.SemaphoreType.DMA((2,))],
+            scratch_shapes=[pltpu.VMEM((2, ends[i], blk, blk), jnp.bfloat16), pltpu.SemaphoreType.DMA((-(-ends[i] // STEP),))],
             input_output_aliases={4 + len(taken): 0} if result else {},
             compiler_params=pltpu.CompilerParams(vmem_limit_bytes=24 << 20),
             cost_estimate=pl.CostEstimate(flops=1, bytes_accessed=1, transcendentals=0),

time: 41.6 us -> 41.5 us (level)
  no operation moved by 1% of the time
where the time goes in v5:
time: 41.5 us; the launch traced here: 41.3 us
  waiting for transfers between devices  15.6 us (38%)
  starting transfers between devices  14.5 us (35%)
  Pallas kernels  9.5 us (23%)
  between operations  0.85 us (2%)
  local copies, waits for them, and re-layouts  0.83 us (2%)
    ppermute x21, waiting for transfers between devices, on_device(): move = lambda value, name: lax.ppermute(value, AXES, pairs[name])  15.6 us
    ppermute x21, starting transfers between devices, on_device(): move = lambda value, name: lax.ppermute(value, AXES, pairs[name])  14.5 us
    pallas_call x2, Pallas kernels, on_device(): pl.pallas_call(functools.partial(last_kernel, low, len(taken), len(result...  1.85 us
    pallas_call x2, Pallas kernels, outgoing(): call(functools.partial(head_kernel, site, at), [blocks(counts[0]), blocks...  1.33 us
    pallas_call x1, Pallas kernels, on_device(): mine_q, mine_r, spread = own(0, given)(local, mpo, mpo_other, *env)  1.17 us
    pallas_call x1, Pallas kernels, on_device(): mine_q, mine_r, spread = own(1, lengths)(local, mpo, mpo_other, *envs)  1.17 us
    pallas_call x2, Pallas kernels, outgoing(): call(functools.partial(tail_kernel, site, at, low, len(projected)), block...  0.86 us
  transfers between devices with their start and end apart: 21, of which 13 were waited for; matrix products, arithmetic and copies ran while one was open for 0% of the time, Pallas kernels for 17%

profile of v5, /device:TPU:0, one launch (start us, length us, event | category | flops | bytes accessed | tf_op | source)
XLA Modules:
  0.0 41.3 jit_solution(9603366102344128478)
XLA Ops:
  0.0 0.5 %collective-permute-start = (bf16[2,4,128,128]{3,2,1,0:T(8,128)(2,1)}, bf16[2,4,128,128]{3,2,1,0:T(8,128)(2,1)S(1)}, u32[]{:S(2)}, u32[]{:S(2)}) collective-permute-start(bf16[2,4,128,128]{3,2,1,0:T(8,128)(2,1)} %bitcast.10), channel_id=1, source_target_pairs={{0,16},{1,17},{2,18},{3,19},{4,20},{5,21},{6,22},{7,23},{8,24},{9,... | collective-permute-start | bytes 786440 | tf_op jit(solution)/shard_map/ppermute | solution.py:259
  0.5 0.7 %copy-done = bf16[2,1,15,128,128]{4,3,2,1,0:T(8,128)(2,1)S(1)} copy-done((bf16[2,1,15,128,128]{4,3,2,1,0:T(8,128)(2,1)S(1)}, bf16[2,1,15,128,128]{4,3,2,1,0:T(8,128)(2,1)}, u32[]{:S(2)}) %copy-start) | copy-done | bytes 983064
  1.3 2.4 %collective-permute-start.7 = (bf16[15,128,128]{2,1,0:T(8,128)(2,1)S(1)}, bf16[15,128,128]{2,1,0:T(8,128)(2,1)S(1)}, u32[]{:S(2)}, u32[]{:S(2)}) collective-permute-start(bf16[15,128,128]{2,1,0:T(8,128)(2,1)S(1)} %dynamic-slice_bitcast_fusion), channel_id=1, source_target_pairs={{0,17},{1,18},{2,19},{3,16},{4,21},{5,22},{6,23},{7,20},{8,25},{9,... | collective-permute-start | bytes 1474568 | tf_op jit(solution)/shard_map/ppermute | solution.py:259
  3.7 0.8 %collective-permute-start.1 = (bf16[4,15,15]{2,1,0:T(8,128)(2,1)S(1)}, bf16[4,15,15]{2,1,0:T(8,128)(2,1)S(1)}, u32[]{:S(2)}, u32[]{:S(2)}) collective-permute-start(bf16[4,15,15]{2,1,0:T(8,128)(2,1)S(1)} %bitcast.12), channel_id=1, source_target_pairs={{0,16},{1,17},{2,18},{3,19},{4,20},{5,21},{6,22},{7,23},{8,24},{9,... | collective-permute-start | bytes 5408 | tf_op jit(solution)/shard_map/ppermute | solution.py:259
  4.5 0.6 %collective-permute-start.3 = (s32[1,4]{1,0:T(1,128)S(1)}, s32[1,4]{1,0:T(1,128)S(1)}, u32[]{:S(2)}, u32[]{:S(2)}) collective-permute-start(s32[1,4]{1,0:T(1,128)S(1)} %bitcast.15), channel_id=1, source_target_pairs={{0,16},{1,17},{2,18},{3,19},{4,20},{5,21},{6,22},{7,23},{8,24},{9,... | collective-permute-start | bytes 56 | tf_op jit(solution)/shard_map/ppermute | solution.py:259
  5.8 0.6 %collective-permute-done.2.rows_other = s32[1,1]{1,0:T(1,128)} collective-permute-done((s32[1,1]{1,0:T(1,128)}, s32[1,1]{1,0:T(1,128)}, u32[]{:S(2)}, u32[]{:S(2)}) %collective-permute-start.2) | collective-permute-done | bytes 36 | tf_op jit(solution)/shard_map/ppermute | solution.py:259
  6.4 0.8 %shard_map.55 = (bf16[2,2,128,128]{3,2,1,0:T(8,128)(2,1)S(1)}, bf16[2,128,128]{2,1,0:T(8,128)(2,1)S(1)}, bf16[2,128,128]{2,1,0:T(8,128)(2,1)S(1)}, s32[2,8,128]{2,1,0:T(8,128)S(1)}) custom-call(s32[1,4]{1,0:T(1,128)S(1)} %bitcast.16, s32[1,4]{1,0:T(1,128)S(1)} %collective-permute-done.3.other, s32[1,1]{1,0:T(1,128)S(6)} %copy.12.rows, ...), custom_call_target="tpu_custom_call" | custom-call | flops 1 | bytes 1 | tf_op jit(solution)/shard_map/pallas_call | solution.py:276
  7.2 0.3 collective-permute-start.5
  7.5 0.3 collective-permute-start.6
  7.8 1.3 %collective-permute-start.4 = (bf16[2,128,128]{2,1,0:T(8,128)(2,1)S(1)}, bf16[2,128,128]{2,1,0:T(8,128)(2,1)S(1)}, u32[]{:S(2)}, u32[]{:S(2)}) collective-permute-start(bf16[2,128,128]{2,1,0:T(8,128)(2,1)S(1)} %get-tuple-element.35), channel_id=1, source_target_pairs={{0,17},{1,18},{2,19},{3,16},{4,21},{5,22},{6,23},{7,20},{8,25},{9,... | collective-permute-start | bytes 196616 | tf_op jit(solution)/shard_map/ppermute | solution.py:259
  9.2 1.2 %shard_map.56 = (bf16[15,128,128]{2,1,0:T(8,128)(2,1)S(1)}, bf16[15,128,128]{2,1,0:T(8,128)(2,1)S(1)}, bf16[2,240,240]{2,1,0:T(8,128)(2,1)S(1)}) custom-call(bf16[2,2,128,128]{3,2,1,0:T(8,128)(2,1)S(1)} %get-tuple-element.34.local, bf16[4,15,15]{2,1,0:T(8,128)(2,1)S(1)} %bitcast.13, bf16[4,15,15]{2,1,0:T(8,128)(2,1)S(1)} %collective-permute-done.1.mpo_other, ...), custom_call_target="tpu_custom_call" | custom-call | flops 1 | bytes 1 | tf_op jit(solution)/shard_map/pallas_call | solution.py:300
  10.3 3.0 %collective-permute-done.4.sent = bf16[2,128,128]{2,1,0:T(8,128)(2,1)S(1)} collective-permute-done((bf16[2,128,128]{2,1,0:T(8,128)(2,1)S(1)}, bf16[2,128,128]{2,1,0:T(8,128)(2,1)S(1)}, u32[]{:S(2)}, u32[]{:S(2)}) %collective-permute-start.4) | collective-permute-done | bytes 65568 | tf_op jit(solution)/shard_map/ppermute | solution.py:259
  13.3 0.7 %shard_map.57 = (bf16[7,128,128]{2,1,0:T(8,128)(2,1)S(1)}, bf16[15,128,128]{2,1,0:T(8,128)(2,1)S(1)}) custom-call(bf16[2,2,128,128]{3,2,1,0:T(8,128)(2,1)S(1)} %get-tuple-element.34.local, bf16[2,128,128]{2,1,0:T(8,128)(2,1)S(1)} %collective-permute-done.4.sent, bf16[2,240,240]{2,1,0:T(8,128)(2,1)S(1)} %get-tuple-element.38.spread, ...), custom_call_target="tpu_custom_call" | custom-call | flops 1 | bytes 1 | tf_op jit(solution)/shard_map/pallas_call | solution.py:289
  14.0 1.7 %collective-permute-start.8 = (bf16[7,128,128]{2,1,0:T(8,128)(2,1)S(1)}, bf16[7,128,128]{2,1,0:T(8,128)(2,1)S(1)}, u32[]{:S(2)}, u32[]{:S(2)}) collective-permute-start(bf16[7,128,128]{2,1,0:T(8,128)(2,1)S(1)} %get-tuple-element.40.refs_1_), channel_id=1, source_target_pairs={{0,1},{1,2},{2,3},{3,0},{4,5},{5,6},{6,7},{7,4},{8,9},{9,10},{10,1... | collective-permute-start | bytes 688136 | tf_op jit(solution)/shard_map/ppermute | solution.py:259
  15.8 0.4 %shard_map.58.after = bf16[8,128,128]{2,1,0:T(8,128)(2,1)S(1)} custom-call(bf16[2,2,128,128]{3,2,1,0:T(8,128)(2,1)S(1)} %get-tuple-element.34.local, bf16[2,128,128]{2,1,0:T(8,128)(2,1)S(1)} %collective-permute-done.4.sent, bf16[2,240,240]{2,1,0:T(8,128)(2,1)S(1)} %get-tuple-element.38.spread, bf16[15,128,128]{2,1,0:T(8,128)(2,1)S(1)} %get-tuple-element.39.mine, ...), custom_call_target="tpu_custom_call" | custom-call | flops 1 | bytes 1 | tf_op jit(solution)/shard_map/pallas_call | solution.py:295
  16.2 1.5 %collective-permute-start.11 = (bf16[8,128,128]{2,1,0:T(8,128)(2,1)S(1)}, bf16[8,128,128]{2,1,0:T(8,128)(2,1)S(1)}, u32[]{:S(2)}, u32[]{:S(2)}) collective-permute-start(bf16[8,128,128]{2,1,0:T(8,128)(2,1)S(1)} %shard_map.58.after), channel_id=1, source_target_pairs={{0,1},{1,2},{2,3},{3,0},{4,5},{5,6},{6,7},{7,4},{8,9},{9,10},{10,1... | collective-permute-start | bytes 786440 | tf_op jit(solution)/shard_map/ppermute | solution.py:259
  17.8 0.8 %shard_map.59.kept = f32[15,128,128]{2,1,0:T(8,128)S(1)} custom-call(bf16[2,2,128,128]{3,2,1,0:T(8,128)(2,1)S(1)} %get-tuple-element.34.local, bf16[2,128,128]{2,1,0:T(8,128)(2,1)S(1)} %collective-permute-done.4.sent, bf16[2,240,240]{2,1,0:T(8,128)(2,1)S(1)} %get-tuple-element.38.spread, bf16[15,128,128]{2,1,0:T(8,128)(2,1)S(1)} %get-tuple-element.41.mine, ...), custom_call_target="tpu_custom_call" | custom-call | flops 1 | bytes 1 | tf_op jit(solution)/shard_map/pallas_call | solution.py:304
  18.6 2.4 %collective-permute-done.8.arrived = bf16[7,128,128]{2,1,0:T(8,128)(2,1)S(1)} collective-permute-done((bf16[7,128,128]{2,1,0:T(8,128)(2,1)S(1)}, bf16[7,128,128]{2,1,0:T(8,128)(2,1)S(1)}, u32[]{:S(2)}, u32[]{:S(2)}) %collective-permute-start.8) | collective-permute-done | bytes 229408 | tf_op jit(solution)/shard_map/ppermute | solution.py:259
  21.0 0.1 shard_map.60.refs_1_.refs_0_.refs_3_.refs_4_
  21.2 0.5 %collective-permute-start.9 = (bf16[9,128,128]{2,1,0:T(8,128)(2,1)S(1)}, bf16[9,128,128]{2,1,0:T(8,128)(2,1)S(1)}, u32[]{:S(2)}, u32[]{:S(2)}) collective-permute-start(bf16[9,128,128]{2,1,0:T(8,128)(2,1)S(1)} %shard_map.60.refs_1_.refs_0_.refs_3_.refs_4_), channel_id=1, source_target_pairs={{16,17},{17,18},{18,19},{19,1},{1,3},{3,2},{2,0},{0,16},{20,21},{2... | collective-permute-start | bytes 884744 | tf_op jit(solution)/shard_map/ppermute | solution.py:259
  21.6 2.2 %collective-permute-done.11.arrived = bf16[8,128,128]{2,1,0:T(8,128)(2,1)S(1)} collective-permute-done((bf16[8,128,128]{2,1,0:T(8,128)(2,1)S(1)}, bf16[8,128,128]{2,1,0:T(8,128)(2,1)S(1)}, u32[]{:S(2)}, u32[]{:S(2)}) %collective-permute-start.11) | collective-permute-done | bytes 262176 | tf_op jit(solution)/shard_map/ppermute | solution.py:259
  23.8 0.1 shard_map.62.refs_1_.refs_4_.refs_5_
  24.0 0.5 %collective-permute-start.12 = (bf16[8,128,128]{2,1,0:T(8,128)(2,1)S(1)}, bf16[8,128,128]{2,1,0:T(8,128)(2,1)S(1)}, u32[]{:S(2)}, u32[]{:S(2)}) collective-permute-start(bf16[8,128,128]{2,1,0:T(8,128)(2,1)S(1)} %shard_map.62.refs_1_.refs_4_.refs_5_), channel_id=1, source_target_pairs={{16,17},{17,18},{18,19},{19,1},{1,3},{3,2},{2,0},{0,16},{20,21},{2... | collective-permute-start | bytes 786440 | tf_op jit(solution)/shard_map/ppermute | solution.py:259
  24.5 0.9 %collective-permute-done.10.from_up = bf16[9,128,128]{2,1,0:T(8,128)(2,1)S(1)} collective-permute-done((bf16[9,128,128]{2,1,0:T(8,128)(2,1)S(1)}, bf16[9,128,128]{2,1,0:T(8,128)(2,1)S(1)}, u32[]{:S(2)}, u32[]{:S(2)}) %collective-permute-start.10) | collective-permute-done | bytes 294944 | tf_op jit(solution)/shard_map/ppermute | solution.py:259
  25.4 2.5 %collective-permute-done.9.from_down = bf16[9,128,128]{2,1,0:T(8,128)(2,1)S(1)} collective-permute-done((bf16[9,128,128]{2,1,0:T(8,128)(2,1)S(1)}, bf16[9,128,128]{2,1,0:T(8,128)(2,1)S(1)}, u32[]{:S(2)}, u32[]{:S(2)}) %collective-permute-start.9) | collective-permute-done | bytes 294944 | tf_op jit(solution)/shard_map/ppermute | solution.py:259
  27.9 0.1 shard_map.61.sent.part.refs_0_
  28.0 1.2 %shard_map.63 = (bf16[15,128,128]{2,1,0:T(8,128)(2,1)S(1)}, bf16[15,128,128]{2,1,0:T(8,128)(2,1)S(1)}, bf16[2,240,240]{2,1,0:T(8,128)(2,1)S(1)}) custom-call(bf16[2,2,128,128]{3,2,1,0:T(8,128)(2,1)S(1)} %get-tuple-element.34.local, bf16[4,15,15]{2,1,0:T(8,128)(2,1)S(1)} %bitcast.14, bf16[4,15,15]{2,1,0:T(8,128)(2,1)S(1)} %collective-permute-done.1.mpo_other, ...), custom_call_target="tpu_custom_call" | custom-call | flops 1 | bytes 1 | tf_op jit(solution)/shard_map/pallas_call | solution.py:315
  29.2 0.2 shard_map.64.refs_0_
  29.4 1.3 %collective-permute-done.12.from_down = bf16[8,128,128]{2,1,0:T(8,128)(2,1)S(1)} collective-permute-done((bf16[8,128,128]{2,1,0:T(8,128)(2,1)S(1)}, bf16[8,128,128]{2,1,0:T(8,128)(2,1)S(1)}, u32[]{:S(2)}, u32[]{:S(2)}) %collective-permute-start.12) | collective-permute-done | bytes 262176 | tf_op jit(solution)/shard_map/ppermute | solution.py:259
  30.7 0.1 shard_map.65.refs_1_
  30.8 0.6 %shard_map.66 = (bf16[7,128,128]{2,1,0:T(8,128)(2,1)S(1)}, bf16[8,128,128]{2,1,0:T(8,128)(2,1)S(1)}) custom-call(bf16[2,2,128,128]{3,2,1,0:T(8,128)(2,1)S(1)} %get-tuple-element.34.local, bf16[9,128,128]{2,1,0:T(8,128)(2,1)S(1)} %shard_map.61.sent.part.refs_0_, bf16[2,240,240]{2,1,0:T(8,128)(2,1)S(1)} %get-tuple-element.44.spread, ...), custom_call_target="tpu_custom_call" | custom-call | flops 1 | bytes 1 | tf_op jit(solution)/shard_map/pallas_call | solution.py:289
  31.4 0.1 collective-permute-start.16
  31.5 0.5 %collective-permute-start.20 = (bf16[7,128,128]{2,1,0:T(8,128)(2,1)S(1)}, bf16[7,128,128]{2,1,0:T(8,128)(2,1)S(1)}, u32[]{:S(2)}, u32[]{:S(2)}) collective-permute-start(bf16[7,128,128]{2,1,0:T(8,128)(2,1)S(1)} %get-tuple-element.47.refs_2_), channel_id=1, source_target_pairs={{16,20},{17,21},{18,22},{19,23},{20,24},{21,25},{22,26},{23,27},{2... | collective-permute-start | bytes 688136 | tf_op jit(solution)/shard_map/ppermute | solution.py:259
  32.0 0.4 %shard_map.67.after = bf16[8,128,128]{2,1,0:T(8,128)(2,1)S(1)} custom-call(bf16[2,2,128,128]{3,2,1,0:T(8,128)(2,1)S(1)} %get-tuple-element.34.local, bf16[9,128,128]{2,1,0:T(8,128)(2,1)S(1)} %shard_map.61.sent.part.refs_0_, bf16[2,240,240]{2,1,0:T(8,128)(2,1)S(1)} %get-tuple-element.44.spread, bf16[15,128,128]{2,1,0:T(8,128)(2,1)S(1)} %get-tuple-element.45.mine, ...), custom_call_target="tpu_custom_call" | custom-call | flops 1 | bytes 1 | tf_op jit(solution)/shard_map/pallas_call | solution.py:295
  32.4 1.1 %collective-permute-start.15 = (bf16[8,128,128]{2,1,0:T(8,128)(2,1)S(1)}, bf16[8,128,128]{2,1,0:T(8,128)(2,1)S(1)}, u32[]{:S(2)}, u32[]{:S(2)}) collective-permute-start(bf16[8,128,128]{2,1,0:T(8,128)(2,1)S(1)} %shard_map.67.after), channel_id=1, source_target_pairs={{0,17},{1,18},{2,19},{3,16},{4,21},{5,22},{6,23},{7,20},{8,25},{9,... | collective-permute-start | bytes 786440 | tf_op jit(solution)/shard_map/ppermute | solution.py:259
  33.6 0.2 collective-permute-start.14
  33.7 0.8 %shard_map.68.kept = f32[15,128,128]{2,1,0:T(8,128)S(1)} custom-call(bf16[2,2,128,128]{3,2,1,0:T(8,128)(2,1)S(1)} %get-tuple-element.34.local, bf16[9,128,128]{2,1,0:T(8,128)(2,1)S(1)} %shard_map.61.sent.part.refs_0_, bf16[2,240,240]{2,1,0:T(8,128)(2,1)S(1)} %get-tuple-element.44.spread, bf16[15,128,128]{2,1,0:T(8,128)(2,1)S(1)} %get-tuple-element.48.mine, ...), custom_call_target="tpu_custom_call" | custom-call | flops 1 | bytes 1 | tf_op jit(solution)/shard_map/pallas_call | solution.py:322
  34.6 0.1 shard_map.69
  34.7 0.4 collective-permute-done.16.from_down_arrived
  35.0 2.0 %collective-permute-start.17 = (bf16[5,128,128]{2,1,0:T(8,128)(2,1)S(1)}, bf16[5,128,128]{2,1,0:T(8,128)(2,1)S(1)}, u32[]{:S(2)}, u32[]{:S(2)}) collective-permute-start(bf16[5,128,128]{2,1,0:T(8,128)(2,1)S(1)} %get-tuple-element.52), channel_id=1, source_target_pairs={{0,16},{1,17},{2,18},{3,19},{4,20},{5,21},{6,22},{7,23},{8,24},{9,... | collective-permute-start | bytes 491528 | tf_op jit(solution)/shard_map/ppermute | solution.py:259
  37.1 0.5 %collective-permute-done.20.from_up_arrived = bf16[7,128,128]{2,1,0:T(8,128)(2,1)S(1)} collective-permute-done((bf16[7,128,128]{2,1,0:T(8,128)(2,1)S(1)}, bf16[7,128,128]{2,1,0:T(8,128)(2,1)S(1)}, u32[]{:S(2)}, u32[]{:S(2)}) %collective-permute-start.20) | collective-permute-done | bytes 229408 | tf_op jit(solution)/shard_map/ppermute | solution.py:259
  37.5 0.0 collective-permute-start.19
  37.6 0.5 %collective-permute-done.17.refs_0_ = bf16[5,128,128]{2,1,0:T(8,128)(2,1)S(1)} collective-permute-done((bf16[5,128,128]{2,1,0:T(8,128)(2,1)S(1)}, bf16[5,128,128]{2,1,0:T(8,128)(2,1)S(1)}, u32[]{:S(2)}, u32[]{:S(2)}) %collective-permute-start.17) | collective-permute-done | bytes 163872 | tf_op jit(solution)/shard_map/ppermute | solution.py:259
  38.1 0.4 collective-permute-done.18.refs_1_
  38.5 0.5 %collective-permute-done.19.refs_2_ = bf16[5,128,128]{2,1,0:T(8,128)(2,1)S(1)} collective-permute-done((bf16[5,128,128]{2,1,0:T(8,128)(2,1)S(1)}, bf16[5,128,128]{2,1,0:T(8,128)(2,1)S(1)}, u32[]{:S(2)}, u32[]{:S(2)}) %collective-permute-start.19) | collective-permute-done | bytes 163872 | tf_op jit(solution)/shard_map/ppermute | solution.py:259
  38.9 0.9 %shard_map.70.refs_3_ = bf16[2,15,128,128]{3,2,1,0:T(8,128)(2,1)} custom-call(s32[2,8,128]{2,1,0:T(8,128)S(1)} %get-tuple-element.33.live, bf16[7,128,128]{2,1,0:T(8,128)(2,1)S(1)} %collective-permute-done.20.from_up_arrived, bf16[7,128,128]{2,1,0:T(8,128)(2,1)S(1)} %collective-permute-done.16.from_down_arrived, f32[15,128,128]{2,1,0:T(8,128)S(1)} %shard_map.68.kept, ...), custom_call_target="tpu_custom_call" | custom-call | flops 1 | bytes 1 | tf_op jit(solution)/shard_map/pallas_call | solution.py:329
  39.9 0.5 %collective-permute-done.14.from_up_arrived = bf16[8,128,128]{2,1,0:T(8,128)(2,1)S(1)} collective-permute-done((bf16[8,128,128]{2,1,0:T(8,128)(2,1)S(1)}, bf16[8,128,128]{2,1,0:T(8,128)(2,1)S(1)}, u32[]{:S(2)}, u32[]{:S(2)}) %collective-permute-start.14) | collective-permute-done | bytes 262176 | tf_op jit(solution)/shard_map/ppermute | solution.py:259
  40.4 0.9 %shard_map.71 = bf16[2,15,128,128]{3,2,1,0:T(8,128)(2,1)} custom-call(s32[2,8,128]{2,1,0:T(8,128)S(1)} %get-tuple-element.33.live, bf16[8,128,128]{2,1,0:T(8,128)(2,1)S(1)} %collective-permute-done.14.from_up_arrived, bf16[8,128,128]{2,1,0:T(8,128)(2,1)S(1)} %collective-permute-done.15.from_down_arrived, ...), custom_call_target="tpu_custom_call", output_to_operand_aliasing={{}: (7, {})} | custom-call | flops 1 | bytes 1 | tf_op jit(solution)/shard_map/pallas_call | solution.py:329
  (23 shorter events, 0.2 us)
Async XLA Ops:
  0.0 1.2 %copy-start = (bf16[2,1,15,128,128]{4,3,2,1,0:T(8,128)(2,1)S(1)}, bf16[2,1,15,128,128]{4,3,2,1,0:T(8,128)(2,1)}, u32[]{:S(2)}) copy-start(bf16[2,1,15,128,128]{4,3,2,1,0:T(8,128)(2,1)} %param.5) | copy-start | bytes 2949124
  0.0 6.3 %collective-permute-start = (bf16[2,4,128,128]{3,2,1,0:T(8,128)(2,1)}, bf16[2,4,128,128]{3,2,1,0:T(8,128)(2,1)S(1)}, u32[]{:S(2)}, u32[]{:S(2)}) collective-permute-start(bf16[2,4,128,128]{3,2,1,0:T(8,128)(2,1)} %bitcast.10), channel_id=1, source_target_pairs={{0,16},{1,17},{2,18},{3,19},{4,20},{5,21},{6,22},{7,23},{8,24},{9,... | collective-permute-start | bytes 786440 | tf_op jit(solution)/shard_map/ppermute | solution.py:259
  1.2 2.5 %copy-start.3 = (bf16[1,4,15,15]{3,1,2,0:T(4,128)(2,1)S(1)}, bf16[1,4,15,15]{3,1,2,0:T(4,128)(2,1)}, u32[]{:S(2)}) copy-start(bf16[1,4,15,15]{3,1,2,0:T(4,128)(2,1)} %param.7) | copy-start | bytes 5404
  1.2 5.2 %copy-start.1 = (bf16[1,2,4,1,128,128]{5,4,3,2,1,0:T(8,128)(2,1)S(1)}, bf16[1,2,4,1,128,128]{5,4,3,2,1,0:T(8,128)(2,1)}, u32[]{:S(2)}) copy-start(bf16[1,2,4,1,128,128]{5,4,3,2,1,0:T(8,128)(2,1)} %param.6) | copy-start | bytes 786436
  1.3 12.1 %collective-permute-start.7 = (bf16[15,128,128]{2,1,0:T(8,128)(2,1)S(1)}, bf16[15,128,128]{2,1,0:T(8,128)(2,1)S(1)}, u32[]{:S(2)}, u32[]{:S(2)}) collective-permute-start(bf16[15,128,128]{2,1,0:T(8,128)(2,1)S(1)} %dynamic-slice_bitcast_fusion), channel_id=1, source_target_pairs={{0,17},{1,18},{2,19},{3,16},{4,21},{5,22},{6,23},{7,20},{8,25},{9,... | collective-permute-start | bytes 1474568 | tf_op jit(solution)/shard_map/ppermute | solution.py:259
  3.7 0.8 %copy-start.2 = (s32[1,4,1]{1,2,0:T(1,128)S(1)}, s32[1,4,1]{1,2,0:T(1,128)}, u32[]{:S(2)}) copy-start(s32[1,4,1]{1,2,0:T(1,128)} %param.9) | copy-start | bytes 52
  3.7 2.7 %collective-permute-start.1 = (bf16[4,15,15]{2,1,0:T(8,128)(2,1)S(1)}, bf16[4,15,15]{2,1,0:T(8,128)(2,1)S(1)}, u32[]{:S(2)}, u32[]{:S(2)}) collective-permute-start(bf16[4,15,15]{2,1,0:T(8,128)(2,1)S(1)} %bitcast.12), channel_id=1, source_target_pairs={{0,16},{1,17},{2,18},{3,19},{4,20},{5,21},{6,22},{7,23},{8,24},{9,... | collective-permute-start | bytes 5408 | tf_op jit(solution)/shard_map/ppermute | solution.py:259
  4.5 1.8 %collective-permute-start.3 = (s32[1,4]{1,0:T(1,128)S(1)}, s32[1,4]{1,0:T(1,128)S(1)}, u32[]{:S(2)}, u32[]{:S(2)}) collective-permute-start(s32[1,4]{1,0:T(1,128)S(1)} %bitcast.15), channel_id=1, source_target_pairs={{0,16},{1,17},{2,18},{3,19},{4,20},{5,21},{6,22},{7,23},{8,24},{9,... | collective-permute-start | bytes 56 | tf_op jit(solution)/shard_map/ppermute | solution.py:259
  5.1 1.2 %collective-permute-start.2 = (s32[1,1]{1,0:T(1,128)}, s32[1,1]{1,0:T(1,128)}, u32[]{:S(2)}, u32[]{:S(2)}) collective-permute-start(s32[1,1]{1,0:T(1,128)} %param.8), channel_id=1, source_target_pairs={{0,16},{1,17},{2,18},{3,19},{4,20},{5,21},{6,22},{7,23},{8,24},{9,... | collective-permute-start | bytes 20 | tf_op jit(solution)/shard_map/ppermute | solution.py:259
  7.2 2.0 %collective-permute-start.5 = (bf16[8,128,128]{2,1,0:T(8,128)(2,1)S(1)}, bf16[8,128,128]{2,1,0:T(8,128)(2,1)S(1)}, u32[]{:S(2)}, u32[]{:S(2)}) collective-permute-start(bf16[8,128,128]{2,1,0:T(8,128)(2,1)S(1)} %slice.6), channel_id=1, source_target_pairs={{0,16},{1,17},{2,18},{3,19},{4,20},{5,21},{6,22},{7,23},{8,24},{9,... | collective-permute-start | bytes 786440 | tf_op jit(solution)/shard_map/ppermute | solution.py:259
  7.5 1.7 %collective-permute-start.6 = (bf16[7,128,128]{2,1,0:T(8,128)(2,1)S(1)}, bf16[7,128,128]{2,1,0:T(8,128)(2,1)S(1)}, u32[]{:S(2)}, u32[]{:S(2)}) collective-permute-start(bf16[7,128,128]{2,1,0:T(8,128)(2,1)S(1)} %slice.7), channel_id=1, source_target_pairs={{0,16},{1,17},{2,18},{3,19},{4,20},{5,21},{6,22},{7,23},{8,24},{9,... | collective-permute-start | bytes 688136 | tf_op jit(solution)/shard_map/ppermute | solution.py:259
  7.8 5.5 %collective-permute-start.4 = (bf16[2,128,128]{2,1,0:T(8,128)(2,1)S(1)}, bf16[2,128,128]{2,1,0:T(8,128)(2,1)S(1)}, u32[]{:S(2)}, u32[]{:S(2)}) collective-permute-start(bf16[2,128,128]{2,1,0:T(8,128)(2,1)S(1)} %get-tuple-element.35), channel_id=1, source_target_pairs={{0,17},{1,18},{2,19},{3,16},{4,21},{5,22},{6,23},{7,20},{8,25},{9,... | collective-permute-start | bytes 196616 | tf_op jit(solution)/shard_map/ppermute | solution.py:259
  14.0 7.0 %collective-permute-start.8 = (bf16[7,128,128]{2,1,0:T(8,128)(2,1)S(1)}, bf16[7,128,128]{2,1,0:T(8,128)(2,1)S(1)}, u32[]{:S(2)}, u32[]{:S(2)}) collective-permute-start(bf16[7,128,128]{2,1,0:T(8,128)(2,1)S(1)} %get-tuple-element.40.refs_1_), channel_id=1, source_target_pairs={{0,1},{1,2},{2,3},{3,0},{4,5},{5,6},{6,7},{7,4},{8,9},{9,10},{10,1... | collective-permute-start | bytes 688136 | tf_op jit(solution)/shard_map/ppermute | solution.py:259
  16.2 7.6 %collective-permute-start.11 = (bf16[8,128,128]{2,1,0:T(8,128)(2,1)S(1)}, bf16[8,128,128]{2,1,0:T(8,128)(2,1)S(1)}, u32[]{:S(2)}, u32[]{:S(2)}) collective-permute-start(bf16[8,128,128]{2,1,0:T(8,128)(2,1)S(1)} %shard_map.58.after), channel_id=1, source_target_pairs={{0,1},{1,2},{2,3},{3,0},{4,5},{5,6},{6,7},{7,4},{8,9},{9,10},{10,1... | collective-permute-start | bytes 786440 | tf_op jit(solution)/shard_map/ppermute | solution.py:259
  21.1 4.3 %collective-permute-start.10 = (bf16[9,128,128]{2,1,0:T(8,128)(2,1)S(1)}, bf16[9,128,128]{2,1,0:T(8,128)(2,1)S(1)}, u32[]{:S(2)}, u32[]{:S(2)}) collective-permute-start(bf16[9,128,128]{2,1,0:T(8,128)(2,1)S(1)} %shard_map.60.refs_1_.refs_0_.refs_3_.refs_4_), channel_id=1, source_target_pairs={{0,4},{1,5},{2,6},{3,7},{4,8},{5,9},{6,10},{7,11},{8,12},{9,13},{1... | collective-permute-start | bytes 884744 | tf_op jit(solution)/shard_map/ppermute | solution.py:259
  21.2 6.8 %collective-permute-start.9 = (bf16[9,128,128]{2,1,0:T(8,128)(2,1)S(1)}, bf16[9,128,128]{2,1,0:T(8,128)(2,1)S(1)}, u32[]{:S(2)}, u32[]{:S(2)}) collective-permute-start(bf16[9,128,128]{2,1,0:T(8,128)(2,1)S(1)} %shard_map.60.refs_1_.refs_0_.refs_3_.refs_4_), channel_id=1, source_target_pairs={{16,17},{17,18},{18,19},{19,1},{1,3},{3,2},{2,0},{0,16},{20,21},{2... | collective-permute-start | bytes 884744 | tf_op jit(solution)/shard_map/ppermute | solution.py:259
  23.9 5.5 %collective-permute-start.13 = (bf16[8,128,128]{2,1,0:T(8,128)(2,1)S(1)}, bf16[8,128,128]{2,1,0:T(8,128)(2,1)S(1)}, u32[]{:S(2)}, u32[]{:S(2)}) collective-permute-start(bf16[8,128,128]{2,1,0:T(8,128)(2,1)S(1)} %shard_map.62.refs_1_.refs_4_.refs_5_), channel_id=1, source_target_pairs={{0,4},{1,5},{2,6},{3,7},{4,8},{5,9},{6,10},{7,11},{8,12},{9,13},{1... | collective-permute-start | bytes 786440 | tf_op jit(solution)/shard_map/ppermute | solution.py:259
  24.0 6.8 %collective-permute-start.12 = (bf16[8,128,128]{2,1,0:T(8,128)(2,1)S(1)}, bf16[8,128,128]{2,1,0:T(8,128)(2,1)S(1)}, u32[]{:S(2)}, u32[]{:S(2)}) collective-permute-start(bf16[8,128,128]{2,1,0:T(8,128)(2,1)S(1)} %shard_map.62.refs_1_.refs_4_.refs_5_), channel_id=1, source_target_pairs={{16,17},{17,18},{18,19},{19,1},{1,3},{3,2},{2,0},{0,16},{20,21},{2... | collective-permute-start | bytes 786440 | tf_op jit(solution)/shard_map/ppermute | solution.py:259
  31.4 3.6 %collective-permute-start.16 = (bf16[7,128,128]{2,1,0:T(8,128)(2,1)S(1)}, bf16[7,128,128]{2,1,0:T(8,128)(2,1)S(1)}, u32[]{:S(2)}, u32[]{:S(2)}) collective-permute-start(bf16[7,128,128]{2,1,0:T(8,128)(2,1)S(1)} %get-tuple-element.47.refs_2_), channel_id=1, source_target_pairs={{0,17},{1,18},{2,19},{3,16},{4,21},{5,22},{6,23},{7,20},{8,25},{9,... | collective-permute-start | bytes 688136 | tf_op jit(solution)/shard_map/ppermute | solution.py:259
  31.5 6.0 %collective-permute-start.20 = (bf16[7,128,128]{2,1,0:T(8,128)(2,1)S(1)}, bf16[7,128,128]{2,1,0:T(8,128)(2,1)S(1)}, u32[]{:S(2)}, u32[]{:S(2)}) collective-permute-start(bf16[7,128,128]{2,1,0:T(8,128)(2,1)S(1)} %get-tuple-element.47.refs_2_), channel_id=1, source_target_pairs={{16,20},{17,21},{18,22},{19,23},{20,24},{21,25},{22,26},{23,27},{2... | collective-permute-start | bytes 688136 | tf_op jit(solution)/shard_map/ppermute | solution.py:259
  32.4 7.4 %collective-permute-start.15 = (bf16[8,128,128]{2,1,0:T(8,128)(2,1)S(1)}, bf16[8,128,128]{2,1,0:T(8,128)(2,1)S(1)}, u32[]{:S(2)}, u32[]{:S(2)}) collective-permute-start(bf16[8,128,128]{2,1,0:T(8,128)(2,1)S(1)} %shard_map.67.after), channel_id=1, source_target_pairs={{0,17},{1,18},{2,19},{3,16},{4,21},{5,22},{6,23},{7,20},{8,25},{9,... | collective-permute-start | bytes 786440 | tf_op jit(solution)/shard_map/ppermute | solution.py:259
  33.6 6.8 %collective-permute-start.14 = (bf16[8,128,128]{2,1,0:T(8,128)(2,1)S(1)}, bf16[8,128,128]{2,1,0:T(8,128)(2,1)S(1)}, u32[]{:S(2)}, u32[]{:S(2)}) collective-permute-start(bf16[8,128,128]{2,1,0:T(8,128)(2,1)S(1)} %shard_map.67.after), channel_id=1, source_target_pairs={{16,20},{17,21},{18,22},{19,23},{20,24},{21,25},{22,26},{23,27},{2... | collective-permute-start | bytes 786440 | tf_op jit(solution)/shard_map/ppermute | solution.py:259
  35.0 3.1 %collective-permute-start.17 = (bf16[5,128,128]{2,1,0:T(8,128)(2,1)S(1)}, bf16[5,128,128]{2,1,0:T(8,128)(2,1)S(1)}, u32[]{:S(2)}, u32[]{:S(2)}) collective-permute-start(bf16[5,128,128]{2,1,0:T(8,128)(2,1)S(1)} %get-tuple-element.52), channel_id=1, source_target_pairs={{0,16},{1,17},{2,18},{3,19},{4,20},{5,21},{6,22},{7,23},{8,24},{9,... | collective-permute-start | bytes 491528 | tf_op jit(solution)/shard_map/ppermute | solution.py:259
  37.1 1.4 %collective-permute-start.18 = (bf16[5,128,128]{2,1,0:T(8,128)(2,1)S(1)}, bf16[5,128,128]{2,1,0:T(8,128)(2,1)S(1)}, u32[]{:S(2)}, u32[]{:S(2)}) collective-permute-start(bf16[5,128,128]{2,1,0:T(8,128)(2,1)S(1)} %get-tuple-element.53), channel_id=1, source_target_pairs={{0,16},{1,17},{2,18},{3,19},{4,20},{5,21},{6,22},{7,23},{8,24},{9,... | collective-permute-start | bytes 491528 | tf_op jit(solution)/shard_map/ppermute | solution.py:259
  37.5 1.4 %collective-permute-start.19 = (bf16[5,128,128]{2,1,0:T(8,128)(2,1)S(1)}, bf16[5,128,128]{2,1,0:T(8,128)(2,1)S(1)}, u32[]{:S(2)}, u32[]{:S(2)}) collective-permute-start(bf16[5,128,128]{2,1,0:T(8,128)(2,1)S(1)} %get-tuple-element.54), channel_id=1, source_target_pairs={{0,16},{1,17},{2,18},{3,19},{4,20},{5,21},{6,22},{7,23},{8,24},{9,... | collective-permute-start | bytes 491528 | tf_op jit(solution)/shard_map/ppermute | solution.py:259

commit v6 on v5

--- a/solution.py
+++ b/solution.py
@@ -14,7 +14,7 @@
 EE = (8, 7)
 DD = (7, 8)
 STEP = 3
-GG = (5, 5, 5)
+GG = (6, 6, 3)
 ACROSS = [(4, 5), (5, 6), (6, 7), (7, 1), (1, 3), (3, 2), (2, 0), (0, 4)]
 
 

time: 41.5 us -> 41.5 us (level)
  transfers between devices with their start and end apart: 21 -> 21, of which waited for: 13 -> 11; matrix products, arithmetic and copies ran while one was open for 0% -> 0% of each run, Pallas kernels for 17% -> 17%
where the time goes in v6:
time: 41.5 us; the launch traced here: 41.3 us
  waiting for transfers between devices  15.6 us (38%)
  starting transfers between devices  14.5 us (35%)
  Pallas kernels  9.5 us (23%)
  between operations  0.85 us (2%)
  local copies, waits for them, and re-layouts  0.83 us (2%)
    ppermute x21, waiting for transfers between devices, on_device(): move = lambda value, name: lax.ppermute(value, AXES, pairs[name])  15.6 us
    ppermute x21, starting transfers between devices, on_device(): move = lambda value, name: lax.ppermute(value, AXES, pairs[name])  14.5 us
    pallas_call x2, Pallas kernels, on_device(): pl.pallas_call(functools.partial(last_kernel, low, len(taken), len(result...  1.86 us
    pallas_call x2, Pallas kernels, outgoing(): call(functools.partial(head_kernel, site, at), [blocks(counts[0]), blocks...  1.33 us
    pallas_call x1, Pallas kernels, on_device(): mine_q, mine_r, spread = own(0, given)(local, mpo, mpo_other, *env)  1.17 us
    pallas_call x1, Pallas kernels, on_device(): mine_q, mine_r, spread = own(1, lengths)(local, mpo, mpo_other, *envs)  1.17 us
    pallas_call x2, Pallas kernels, outgoing(): call(functools.partial(tail_kernel, site, at, low, len(projected)), block...  0.86 us
  transfers between devices with their start and end apart: 21, of which 11 were waited for; matrix products, arithmetic and copies ran while one was open for 0% of the time, Pallas kernels for 17%

profile of v6, /device:TPU:0, one launch (start us, length us, event | category | flops | bytes accessed | tf_op | source)
XLA Modules:
  0.0 41.3 jit_solution(17346075661530458676)
XLA Ops:
  0.0 0.5 %collective-permute-start = (bf16[2,4,128,128]{3,2,1,0:T(8,128)(2,1)}, bf16[2,4,128,128]{3,2,1,0:T(8,128)(2,1)S(1)}, u32[]{:S(2)}, u32[]{:S(2)}) collective-permute-start(bf16[2,4,128,128]{3,2,1,0:T(8,128)(2,1)} %bitcast.10), channel_id=1, source_target_pairs={{0,16},{1,17},{2,18},{3,19},{4,20},{5,21},{6,22},{7,23},{8,24},{9,... | collective-permute-start | bytes 786440 | tf_op jit(solution)/shard_map/ppermute | solution.py:259
  0.5 0.7 %copy-done = bf16[2,1,15,128,128]{4,3,2,1,0:T(8,128)(2,1)S(1)} copy-done((bf16[2,1,15,128,128]{4,3,2,1,0:T(8,128)(2,1)S(1)}, bf16[2,1,15,128,128]{4,3,2,1,0:T(8,128)(2,1)}, u32[]{:S(2)}) %copy-start) | copy-done | bytes 983064
  1.3 2.4 %collective-permute-start.7 = (bf16[15,128,128]{2,1,0:T(8,128)(2,1)S(1)}, bf16[15,128,128]{2,1,0:T(8,128)(2,1)S(1)}, u32[]{:S(2)}, u32[]{:S(2)}) collective-permute-start(bf16[15,128,128]{2,1,0:T(8,128)(2,1)S(1)} %dynamic-slice_bitcast_fusion), channel_id=1, source_target_pairs={{0,17},{1,18},{2,19},{3,16},{4,21},{5,22},{6,23},{7,20},{8,25},{9,... | collective-permute-start | bytes 1474568 | tf_op jit(solution)/shard_map/ppermute | solution.py:259
  3.7 0.8 %collective-permute-start.1 = (bf16[4,15,15]{2,1,0:T(8,128)(2,1)S(1)}, bf16[4,15,15]{2,1,0:T(8,128)(2,1)S(1)}, u32[]{:S(2)}, u32[]{:S(2)}) collective-permute-start(bf16[4,15,15]{2,1,0:T(8,128)(2,1)S(1)} %bitcast.12), channel_id=1, source_target_pairs={{0,16},{1,17},{2,18},{3,19},{4,20},{5,21},{6,22},{7,23},{8,24},{9,... | collective-permute-start | bytes 5408 | tf_op jit(solution)/shard_map/ppermute | solution.py:259
  4.5 0.6 %collective-permute-start.3 = (s32[1,4]{1,0:T(1,128)S(1)}, s32[1,4]{1,0:T(1,128)S(1)}, u32[]{:S(2)}, u32[]{:S(2)}) collective-permute-start(s32[1,4]{1,0:T(1,128)S(1)} %bitcast.15), channel_id=1, source_target_pairs={{0,16},{1,17},{2,18},{3,19},{4,20},{5,21},{6,22},{7,23},{8,24},{9,... | collective-permute-start | bytes 56 | tf_op jit(solution)/shard_map/ppermute | solution.py:259
  5.8 0.6 %collective-permute-done.2.rows_other = s32[1,1]{1,0:T(1,128)} collective-permute-done((s32[1,1]{1,0:T(1,128)}, s32[1,1]{1,0:T(1,128)}, u32[]{:S(2)}, u32[]{:S(2)}) %collective-permute-start.2) | collective-permute-done | bytes 36 | tf_op jit(solution)/shard_map/ppermute | solution.py:259
  6.4 0.8 %shard_map.55 = (bf16[2,2,128,128]{3,2,1,0:T(8,128)(2,1)S(1)}, bf16[2,128,128]{2,1,0:T(8,128)(2,1)S(1)}, bf16[2,128,128]{2,1,0:T(8,128)(2,1)S(1)}, s32[2,8,128]{2,1,0:T(8,128)S(1)}) custom-call(s32[1,4]{1,0:T(1,128)S(1)} %bitcast.16, s32[1,4]{1,0:T(1,128)S(1)} %collective-permute-done.3.other, s32[1,1]{1,0:T(1,128)S(6)} %copy.12.rows, ...), custom_call_target="tpu_custom_call" | custom-call | flops 1 | bytes 1 | tf_op jit(solution)/shard_map/pallas_call | solution.py:276
  7.2 0.3 collective-permute-start.5
  7.5 0.3 collective-permute-start.6
  7.8 1.3 %collective-permute-start.4 = (bf16[2,128,128]{2,1,0:T(8,128)(2,1)S(1)}, bf16[2,128,128]{2,1,0:T(8,128)(2,1)S(1)}, u32[]{:S(2)}, u32[]{:S(2)}) collective-permute-start(bf16[2,128,128]{2,1,0:T(8,128)(2,1)S(1)} %get-tuple-element.35), channel_id=1, source_target_pairs={{0,17},{1,18},{2,19},{3,16},{4,21},{5,22},{6,23},{7,20},{8,25},{9,... | collective-permute-start | bytes 196616 | tf_op jit(solution)/shard_map/ppermute | solution.py:259
  9.2 1.2 %shard_map.56 = (bf16[15,128,128]{2,1,0:T(8,128)(2,1)S(1)}, bf16[15,128,128]{2,1,0:T(8,128)(2,1)S(1)}, bf16[2,240,240]{2,1,0:T(8,128)(2,1)S(1)}) custom-call(bf16[2,2,128,128]{3,2,1,0:T(8,128)(2,1)S(1)} %get-tuple-element.34.local, bf16[4,15,15]{2,1,0:T(8,128)(2,1)S(1)} %bitcast.13, bf16[4,15,15]{2,1,0:T(8,128)(2,1)S(1)} %collective-permute-done.1.mpo_other, ...), custom_call_target="tpu_custom_call" | custom-call | flops 1 | bytes 1 | tf_op jit(solution)/shard_map/pallas_call | solution.py:300
  10.3 3.0 %collective-permute-done.4.sent = bf16[2,128,128]{2,1,0:T(8,128)(2,1)S(1)} collective-permute-done((bf16[2,128,128]{2,1,0:T(8,128)(2,1)S(1)}, bf16[2,128,128]{2,1,0:T(8,128)(2,1)S(1)}, u32[]{:S(2)}, u32[]{:S(2)}) %collective-permute-start.4) | collective-permute-done | bytes 65568 | tf_op jit(solution)/shard_map/ppermute | solution.py:259
  13.3 0.7 %shard_map.57 = (bf16[7,128,128]{2,1,0:T(8,128)(2,1)S(1)}, bf16[15,128,128]{2,1,0:T(8,128)(2,1)S(1)}) custom-call(bf16[2,2,128,128]{3,2,1,0:T(8,128)(2,1)S(1)} %get-tuple-element.34.local, bf16[2,128,128]{2,1,0:T(8,128)(2,1)S(1)} %collective-permute-done.4.sent, bf16[2,240,240]{2,1,0:T(8,128)(2,1)S(1)} %get-tuple-element.38.spread, ...), custom_call_target="tpu_custom_call" | custom-call | flops 1 | bytes 1 | tf_op jit(solution)/shard_map/pallas_call | solution.py:289
  14.0 1.7 %collective-permute-start.8 = (bf16[7,128,128]{2,1,0:T(8,128)(2,1)S(1)}, bf16[7,128,128]{2,1,0:T(8,128)(2,1)S(1)}, u32[]{:S(2)}, u32[]{:S(2)}) collective-permute-start(bf16[7,128,128]{2,1,0:T(8,128)(2,1)S(1)} %get-tuple-element.40.refs_1_), channel_id=1, source_target_pairs={{0,1},{1,2},{2,3},{3,0},{4,5},{5,6},{6,7},{7,4},{8,9},{9,10},{10,1... | collective-permute-start | bytes 688136 | tf_op jit(solution)/shard_map/ppermute | solution.py:259
  15.8 0.4 %shard_map.58.after = bf16[8,128,128]{2,1,0:T(8,128)(2,1)S(1)} custom-call(bf16[2,2,128,128]{3,2,1,0:T(8,128)(2,1)S(1)} %get-tuple-element.34.local, bf16[2,128,128]{2,1,0:T(8,128)(2,1)S(1)} %collective-permute-done.4.sent, bf16[2,240,240]{2,1,0:T(8,128)(2,1)S(1)} %get-tuple-element.38.spread, bf16[15,128,128]{2,1,0:T(8,128)(2,1)S(1)} %get-tuple-element.39.mine, ...), custom_call_target="tpu_custom_call" | custom-call | flops 1 | bytes 1 | tf_op jit(solution)/shard_map/pallas_call | solution.py:295
  16.2 1.5 %collective-permute-start.11 = (bf16[8,128,128]{2,1,0:T(8,128)(2,1)S(1)}, bf16[8,128,128]{2,1,0:T(8,128)(2,1)S(1)}, u32[]{:S(2)}, u32[]{:S(2)}) collective-permute-start(bf16[8,128,128]{2,1,0:T(8,128)(2,1)S(1)} %shard_map.58.after), channel_id=1, source_target_pairs={{0,1},{1,2},{2,3},{3,0},{4,5},{5,6},{6,7},{7,4},{8,9},{9,10},{10,1... | collective-permute-start | bytes 786440 | tf_op jit(solution)/shard_map/ppermute | solution.py:259
  17.8 0.8 %shard_map.59.kept = f32[15,128,128]{2,1,0:T(8,128)S(1)} custom-call(bf16[2,2,128,128]{3,2,1,0:T(8,128)(2,1)S(1)} %get-tuple-element.34.local, bf16[2,128,128]{2,1,0:T(8,128)(2,1)S(1)} %collective-permute-done.4.sent, bf16[2,240,240]{2,1,0:T(8,128)(2,1)S(1)} %get-tuple-element.38.spread, bf16[15,128,128]{2,1,0:T(8,128)(2,1)S(1)} %get-tuple-element.41.mine, ...), custom_call_target="tpu_custom_call" | custom-call | flops 1 | bytes 1 | tf_op jit(solution)/shard_map/pallas_call | solution.py:304
  18.6 2.4 %collective-permute-done.8.arrived = bf16[7,128,128]{2,1,0:T(8,128)(2,1)S(1)} collective-permute-done((bf16[7,128,128]{2,1,0:T(8,128)(2,1)S(1)}, bf16[7,128,128]{2,1,0:T(8,128)(2,1)S(1)}, u32[]{:S(2)}, u32[]{:S(2)}) %collective-permute-start.8) | collective-permute-done | bytes 229408 | tf_op jit(solution)/shard_map/ppermute | solution.py:259
  21.0 0.1 shard_map.60.refs_1_.refs_0_.refs_3_.refs_4_
  21.1 0.0 collective-permute-start.10
  21.2 0.5 %collective-permute-start.9 = (bf16[9,128,128]{2,1,0:T(8,128)(2,1)S(1)}, bf16[9,128,128]{2,1,0:T(8,128)(2,1)S(1)}, u32[]{:S(2)}, u32[]{:S(2)}) collective-permute-start(bf16[9,128,128]{2,1,0:T(8,128)(2,1)S(1)} %shard_map.60.refs_1_.refs_0_.refs_3_.refs_4_), channel_id=1, source_target_pairs={{16,17},{17,18},{18,19},{19,1},{1,3},{3,2},{2,0},{0,16},{20,21},{2... | collective-permute-start | bytes 884744 | tf_op jit(solution)/shard_map/ppermute | solution.py:259
  21.6 2.2 %collective-permute-done.11.arrived = bf16[8,128,128]{2,1,0:T(8,128)(2,1)S(1)} collective-permute-done((bf16[8,128,128]{2,1,0:T(8,128)(2,1)S(1)}, bf16[8,128,128]{2,1,0:T(8,128)(2,1)S(1)}, u32[]{:S(2)}, u32[]{:S(2)}) %collective-permute-start.11) | collective-permute-done | bytes 262176 | tf_op jit(solution)/shard_map/ppermute | solution.py:259
  23.8 0.1 shard_map.62.refs_1_.refs_4_.refs_5_
  23.9 0.0 collective-permute-start.13
  24.0 0.5 %collective-permute-start.12 = (bf16[8,128,128]{2,1,0:T(8,128)(2,1)S(1)}, bf16[8,128,128]{2,1,0:T(8,128)(2,1)S(1)}, u32[]{:S(2)}, u32[]{:S(2)}) collective-permute-start(bf16[8,128,128]{2,1,0:T(8,128)(2,1)S(1)} %shard_map.62.refs_1_.refs_4_.refs_5_), channel_id=1, source_target_pairs={{16,17},{17,18},{18,19},{19,1},{1,3},{3,2},{2,0},{0,16},{20,21},{2... | collective-permute-start | bytes 786440 | tf_op jit(solution)/shard_map/ppermute | solution.py:259
  24.5 0.9 %collective-permute-done.10.from_up = bf16[9,128,128]{2,1,0:T(8,128)(2,1)S(1)} collective-permute-done((bf16[9,128,128]{2,1,0:T(8,128)(2,1)S(1)}, bf16[9,128,128]{2,1,0:T(8,128)(2,1)S(1)}, u32[]{:S(2)}, u32[]{:S(2)}) %collective-permute-start.10) | collective-permute-done | bytes 294944 | tf_op jit(solution)/shard_map/ppermute | solution.py:259
  25.4 2.5 %collective-permute-done.9.from_down = bf16[9,128,128]{2,1,0:T(8,128)(2,1)S(1)} collective-permute-done((bf16[9,128,128]{2,1,0:T(8,128)(2,1)S(1)}, bf16[9,128,128]{2,1,0:T(8,128)(2,1)S(1)}, u32[]{:S(2)}, u32[]{:S(2)}) %collective-permute-start.9) | collective-permute-done | bytes 294944 | tf_op jit(solution)/shard_map/ppermute | solution.py:259
  27.9 0.1 shard_map.61.sent.part.refs_0_
  28.0 1.2 %shard_map.63 = (bf16[15,128,128]{2,1,0:T(8,128)(2,1)S(1)}, bf16[15,128,128]{2,1,0:T(8,128)(2,1)S(1)}, bf16[2,240,240]{2,1,0:T(8,128)(2,1)S(1)}) custom-call(bf16[2,2,128,128]{3,2,1,0:T(8,128)(2,1)S(1)} %get-tuple-element.34.local, bf16[4,15,15]{2,1,0:T(8,128)(2,1)S(1)} %bitcast.14, bf16[4,15,15]{2,1,0:T(8,128)(2,1)S(1)} %collective-permute-done.1.mpo_other, ...), custom_call_target="tpu_custom_call" | custom-call | flops 1 | bytes 1 | tf_op jit(solution)/shard_map/pallas_call | solution.py:315
  29.2 0.2 shard_map.64.refs_0_
  29.4 1.3 %collective-permute-done.12.from_down = bf16[8,128,128]{2,1,0:T(8,128)(2,1)S(1)} collective-permute-done((bf16[8,128,128]{2,1,0:T(8,128)(2,1)S(1)}, bf16[8,128,128]{2,1,0:T(8,128)(2,1)S(1)}, u32[]{:S(2)}, u32[]{:S(2)}) %collective-permute-start.12) | collective-permute-done | bytes 262176 | tf_op jit(solution)/shard_map/ppermute | solution.py:259
  30.7 0.1 shard_map.65.refs_1_
  30.8 0.6 %shard_map.66 = (bf16[7,128,128]{2,1,0:T(8,128)(2,1)S(1)}, bf16[8,128,128]{2,1,0:T(8,128)(2,1)S(1)}) custom-call(bf16[2,2,128,128]{3,2,1,0:T(8,128)(2,1)S(1)} %get-tuple-element.34.local, bf16[9,128,128]{2,1,0:T(8,128)(2,1)S(1)} %shard_map.61.sent.part.refs_0_, bf16[2,240,240]{2,1,0:T(8,128)(2,1)S(1)} %get-tuple-element.44.spread, ...), custom_call_target="tpu_custom_call" | custom-call | flops 1 | bytes 1 | tf_op jit(solution)/shard_map/pallas_call | solution.py:289
  31.4 0.1 collective-permute-start.16
  31.5 0.5 %collective-permute-start.20 = (bf16[7,128,128]{2,1,0:T(8,128)(2,1)S(1)}, bf16[7,128,128]{2,1,0:T(8,128)(2,1)S(1)}, u32[]{:S(2)}, u32[]{:S(2)}) collective-permute-start(bf16[7,128,128]{2,1,0:T(8,128)(2,1)S(1)} %get-tuple-element.47.refs_2_), channel_id=1, source_target_pairs={{16,20},{17,21},{18,22},{19,23},{20,24},{21,25},{22,26},{23,27},{2... | collective-permute-start | bytes 688136 | tf_op jit(solution)/shard_map/ppermute | solution.py:259
  32.0 0.4 %shard_map.67.after = bf16[8,128,128]{2,1,0:T(8,128)(2,1)S(1)} custom-call(bf16[2,2,128,128]{3,2,1,0:T(8,128)(2,1)S(1)} %get-tuple-element.34.local, bf16[9,128,128]{2,1,0:T(8,128)(2,1)S(1)} %shard_map.61.sent.part.refs_0_, bf16[2,240,240]{2,1,0:T(8,128)(2,1)S(1)} %get-tuple-element.44.spread, bf16[15,128,128]{2,1,0:T(8,128)(2,1)S(1)} %get-tuple-element.45.mine, ...), custom_call_target="tpu_custom_call" | custom-call | flops 1 | bytes 1 | tf_op jit(solution)/shard_map/pallas_call | solution.py:295
  32.4 1.1 %collective-permute-start.15 = (bf16[8,128,128]{2,1,0:T(8,128)(2,1)S(1)}, bf16[8,128,128]{2,1,0:T(8,128)(2,1)S(1)}, u32[]{:S(2)}, u32[]{:S(2)}) collective-permute-start(bf16[8,128,128]{2,1,0:T(8,128)(2,1)S(1)} %shard_map.67.after), channel_id=1, source_target_pairs={{0,17},{1,18},{2,19},{3,16},{4,21},{5,22},{6,23},{7,20},{8,25},{9,... | collective-permute-start | bytes 786440 | tf_op jit(solution)/shard_map/ppermute | solution.py:259
  33.6 0.2 collective-permute-start.14
  33.7 0.8 %shard_map.68.kept = f32[15,128,128]{2,1,0:T(8,128)S(1)} custom-call(bf16[2,2,128,128]{3,2,1,0:T(8,128)(2,1)S(1)} %get-tuple-element.34.local, bf16[9,128,128]{2,1,0:T(8,128)(2,1)S(1)} %shard_map.61.sent.part.refs_0_, bf16[2,240,240]{2,1,0:T(8,128)(2,1)S(1)} %get-tuple-element.44.spread, bf16[15,128,128]{2,1,0:T(8,128)(2,1)S(1)} %get-tuple-element.48.mine, ...), custom_call_target="tpu_custom_call" | custom-call | flops 1 | bytes 1 | tf_op jit(solution)/shard_map/pallas_call | solution.py:322
  34.6 0.1 shard_map.69
  34.7 0.4 collective-permute-done.16.from_down_arrived
  35.0 2.0 %collective-permute-start.17 = (bf16[6,128,128]{2,1,0:T(8,128)(2,1)S(1)}, bf16[6,128,128]{2,1,0:T(8,128)(2,1)S(1)}, u32[]{:S(2)}, u32[]{:S(2)}) collective-permute-start(bf16[6,128,128]{2,1,0:T(8,128)(2,1)S(1)} %get-tuple-element.52), channel_id=1, source_target_pairs={{0,16},{1,17},{2,18},{3,19},{4,20},{5,21},{6,22},{7,23},{8,24},{9,... | collective-permute-start | bytes 589832 | tf_op jit(solution)/shard_map/ppermute | solution.py:259
  37.1 0.5 %collective-permute-done.20.from_up_arrived = bf16[7,128,128]{2,1,0:T(8,128)(2,1)S(1)} collective-permute-done((bf16[7,128,128]{2,1,0:T(8,128)(2,1)S(1)}, bf16[7,128,128]{2,1,0:T(8,128)(2,1)S(1)}, u32[]{:S(2)}, u32[]{:S(2)}) %collective-permute-start.20) | collective-permute-done | bytes 229408 | tf_op jit(solution)/shard_map/ppermute | solution.py:259
  37.5 0.0 collective-permute-start.19
  37.6 1.3 %collective-permute-done.19.refs_2_ = bf16[3,128,128]{2,1,0:T(8,128)(2,1)S(1)} collective-permute-done((bf16[3,128,128]{2,1,0:T(8,128)(2,1)S(1)}, bf16[3,128,128]{2,1,0:T(8,128)(2,1)S(1)}, u32[]{:S(2)}, u32[]{:S(2)}) %collective-permute-start.19) | collective-permute-done | bytes 98336 | tf_op jit(solution)/shard_map/ppermute | solution.py:259
  38.9 0.9 %shard_map.70.refs_3_ = bf16[2,15,128,128]{3,2,1,0:T(8,128)(2,1)} custom-call(s32[2,8,128]{2,1,0:T(8,128)S(1)} %get-tuple-element.33.live, bf16[7,128,128]{2,1,0:T(8,128)(2,1)S(1)} %collective-permute-done.20.from_up_arrived, bf16[7,128,128]{2,1,0:T(8,128)(2,1)S(1)} %collective-permute-done.16.from_down_arrived, f32[15,128,128]{2,1,0:T(8,128)S(1)} %shard_map.68.kept, ...), custom_call_target="tpu_custom_call" | custom-call | flops 1 | bytes 1 | tf_op jit(solution)/shard_map/pallas_call | solution.py:329
  39.8 0.6 %collective-permute-done.14.from_up_arrived = bf16[8,128,128]{2,1,0:T(8,128)(2,1)S(1)} collective-permute-done((bf16[8,128,128]{2,1,0:T(8,128)(2,1)S(1)}, bf16[8,128,128]{2,1,0:T(8,128)(2,1)S(1)}, u32[]{:S(2)}, u32[]{:S(2)}) %collective-permute-start.14) | collective-permute-done | bytes 262176 | tf_op jit(solution)/shard_map/ppermute | solution.py:259
  40.4 0.9 %shard_map.71 = bf16[2,15,128,128]{3,2,1,0:T(8,128)(2,1)} custom-call(s32[2,8,128]{2,1,0:T(8,128)S(1)} %get-tuple-element.33.live, bf16[8,128,128]{2,1,0:T(8,128)(2,1)S(1)} %collective-permute-done.14.from_up_arrived, bf16[8,128,128]{2,1,0:T(8,128)(2,1)S(1)} %collective-permute-done.15.from_down_arrived, ...), custom_call_target="tpu_custom_call", output_to_operand_aliasing={{}: (7, {})} | custom-call | flops 1 | bytes 1 | tf_op jit(solution)/shard_map/pallas_call | solution.py:329
  (23 shorter events, 0.1 us)
Async XLA Ops:
  0.0 1.2 %copy-start = (bf16[2,1,15,128,128]{4,3,2,1,0:T(8,128)(2,1)S(1)}, bf16[2,1,15,128,128]{4,3,2,1,0:T(8,128)(2,1)}, u32[]{:S(2)}) copy-start(bf16[2,1,15,128,128]{4,3,2,1,0:T(8,128)(2,1)} %param.5) | copy-start | bytes 2949124
  0.0 6.3 %collective-permute-start = (bf16[2,4,128,128]{3,2,1,0:T(8,128)(2,1)}, bf16[2,4,128,128]{3,2,1,0:T(8,128)(2,1)S(1)}, u32[]{:S(2)}, u32[]{:S(2)}) collective-permute-start(bf16[2,4,128,128]{3,2,1,0:T(8,128)(2,1)} %bitcast.10), channel_id=1, source_target_pairs={{0,16},{1,17},{2,18},{3,19},{4,20},{5,21},{6,22},{7,23},{8,24},{9,... | collective-permute-start | bytes 786440 | tf_op jit(solution)/shard_map/ppermute | solution.py:259
  1.2 2.5 %copy-start.3 = (bf16[1,4,15,15]{3,1,2,0:T(4,128)(2,1)S(1)}, bf16[1,4,15,15]{3,1,2,0:T(4,128)(2,1)}, u32[]{:S(2)}) copy-start(bf16[1,4,15,15]{3,1,2,0:T(4,128)(2,1)} %param.7) | copy-start | bytes 5404
  1.2 5.2 %copy-start.1 = (bf16[1,2,4,1,128,128]{5,4,3,2,1,0:T(8,128)(2,1)S(1)}, bf16[1,2,4,1,128,128]{5,4,3,2,1,0:T(8,128)(2,1)}, u32[]{:S(2)}) copy-start(bf16[1,2,4,1,128,128]{5,4,3,2,1,0:T(8,128)(2,1)} %param.6) | copy-start | bytes 786436
  1.3 12.1 %collective-permute-start.7 = (bf16[15,128,128]{2,1,0:T(8,128)(2,1)S(1)}, bf16[15,128,128]{2,1,0:T(8,128)(2,1)S(1)}, u32[]{:S(2)}, u32[]{:S(2)}) collective-permute-start(bf16[15,128,128]{2,1,0:T(8,128)(2,1)S(1)} %dynamic-slice_bitcast_fusion), channel_id=1, source_target_pairs={{0,17},{1,18},{2,19},{3,16},{4,21},{5,22},{6,23},{7,20},{8,25},{9,... | collective-permute-start | bytes 1474568 | tf_op jit(solution)/shard_map/ppermute | solution.py:259
  3.7 0.8 %copy-start.2 = (s32[1,4,1]{1,2,0:T(1,128)S(1)}, s32[1,4,1]{1,2,0:T(1,128)}, u32[]{:S(2)}) copy-start(s32[1,4,1]{1,2,0:T(1,128)} %param.9) | copy-start | bytes 52
  3.7 2.7 %collective-permute-start.1 = (bf16[4,15,15]{2,1,0:T(8,128)(2,1)S(1)}, bf16[4,15,15]{2,1,0:T(8,128)(2,1)S(1)}, u32[]{:S(2)}, u32[]{:S(2)}) collective-permute-start(bf16[4,15,15]{2,1,0:T(8,128)(2,1)S(1)} %bitcast.12), channel_id=1, source_target_pairs={{0,16},{1,17},{2,18},{3,19},{4,20},{5,21},{6,22},{7,23},{8,24},{9,... | collective-permute-start | bytes 5408 | tf_op jit(solution)/shard_map/ppermute | solution.py:259
  4.5 1.8 %collective-permute-start.3 = (s32[1,4]{1,0:T(1,128)S(1)}, s32[1,4]{1,0:T(1,128)S(1)}, u32[]{:S(2)}, u32[]{:S(2)}) collective-permute-start(s32[1,4]{1,0:T(1,128)S(1)} %bitcast.15), channel_id=1, source_target_pairs={{0,16},{1,17},{2,18},{3,19},{4,20},{5,21},{6,22},{7,23},{8,24},{9,... | collective-permute-start | bytes 56 | tf_op jit(solution)/shard_map/ppermute | solution.py:259
  5.1 1.2 %collective-permute-start.2 = (s32[1,1]{1,0:T(1,128)}, s32[1,1]{1,0:T(1,128)}, u32[]{:S(2)}, u32[]{:S(2)}) collective-permute-start(s32[1,1]{1,0:T(1,128)} %param.8), channel_id=1, source_target_pairs={{0,16},{1,17},{2,18},{3,19},{4,20},{5,21},{6,22},{7,23},{8,24},{9,... | collective-permute-start | bytes 20 | tf_op jit(solution)/shard_map/ppermute | solution.py:259
  7.2 2.0 %collective-permute-start.5 = (bf16[8,128,128]{2,1,0:T(8,128)(2,1)S(1)}, bf16[8,128,128]{2,1,0:T(8,128)(2,1)S(1)}, u32[]{:S(2)}, u32[]{:S(2)}) collective-permute-start(bf16[8,128,128]{2,1,0:T(8,128)(2,1)S(1)} %slice.6), channel_id=1, source_target_pairs={{0,16},{1,17},{2,18},{3,19},{4,20},{5,21},{6,22},{7,23},{8,24},{9,... | collective-permute-start | bytes 786440 | tf_op jit(solution)/shard_map/ppermute | solution.py:259
  7.5 1.7 %collective-permute-start.6 = (bf16[7,128,128]{2,1,0:T(8,128)(2,1)S(1)}, bf16[7,128,128]{2,1,0:T(8,128)(2,1)S(1)}, u32[]{:S(2)}, u32[]{:S(2)}) collective-permute-start(bf16[7,128,128]{2,1,0:T(8,128)(2,1)S(1)} %slice.7), channel_id=1, source_target_pairs={{0,16},{1,17},{2,18},{3,19},{4,20},{5,21},{6,22},{7,23},{8,24},{9,... | collective-permute-start | bytes 688136 | tf_op jit(solution)/shard_map/ppermute | solution.py:259
  7.8 5.5 %collective-permute-start.4 = (bf16[2,128,128]{2,1,0:T(8,128)(2,1)S(1)}, bf16[2,128,128]{2,1,0:T(8,128)(2,1)S(1)}, u32[]{:S(2)}, u32[]{:S(2)}) collective-permute-start(bf16[2,128,128]{2,1,0:T(8,128)(2,1)S(1)} %get-tuple-element.35), channel_id=1, source_target_pairs={{0,17},{1,18},{2,19},{3,16},{4,21},{5,22},{6,23},{7,20},{8,25},{9,... | collective-permute-start | bytes 196616 | tf_op jit(solution)/shard_map/ppermute | solution.py:259
  14.0 7.0 %collective-permute-start.8 = (bf16[7,128,128]{2,1,0:T(8,128)(2,1)S(1)}, bf16[7,128,128]{2,1,0:T(8,128)(2,1)S(1)}, u32[]{:S(2)}, u32[]{:S(2)}) collective-permute-start(bf16[7,128,128]{2,1,0:T(8,128)(2,1)S(1)} %get-tuple-element.40.refs_1_), channel_id=1, source_target_pairs={{0,1},{1,2},{2,3},{3,0},{4,5},{5,6},{6,7},{7,4},{8,9},{9,10},{10,1... | collective-permute-start | bytes 688136 | tf_op jit(solution)/shard_map/ppermute | solution.py:259
  16.2 7.6 %collective-permute-start.11 = (bf16[8,128,128]{2,1,0:T(8,128)(2,1)S(1)}, bf16[8,128,128]{2,1,0:T(8,128)(2,1)S(1)}, u32[]{:S(2)}, u32[]{:S(2)}) collective-permute-start(bf16[8,128,128]{2,1,0:T(8,128)(2,1)S(1)} %shard_map.58.after), channel_id=1, source_target_pairs={{0,1},{1,2},{2,3},{3,0},{4,5},{5,6},{6,7},{7,4},{8,9},{9,10},{10,1... | collective-permute-start | bytes 786440 | tf_op jit(solution)/shard_map/ppermute | solution.py:259
  21.1 4.3 %collective-permute-start.10 = (bf16[9,128,128]{2,1,0:T(8,128)(2,1)S(1)}, bf16[9,128,128]{2,1,0:T(8,128)(2,1)S(1)}, u32[]{:S(2)}, u32[]{:S(2)}) collective-permute-start(bf16[9,128,128]{2,1,0:T(8,128)(2,1)S(1)} %shard_map.60.refs_1_.refs_0_.refs_3_.refs_4_), channel_id=1, source_target_pairs={{0,4},{1,5},{2,6},{3,7},{4,8},{5,9},{6,10},{7,11},{8,12},{9,13},{1... | collective-permute-start | bytes 884744 | tf_op jit(solution)/shard_map/ppermute | solution.py:259
  21.2 6.8 %collective-permute-start.9 = (bf16[9,128,128]{2,1,0:T(8,128)(2,1)S(1)}, bf16[9,128,128]{2,1,0:T(8,128)(2,1)S(1)}, u32[]{:S(2)}, u32[]{:S(2)}) collective-permute-start(bf16[9,128,128]{2,1,0:T(8,128)(2,1)S(1)} %shard_map.60.refs_1_.refs_0_.refs_3_.refs_4_), channel_id=1, source_target_pairs={{16,17},{17,18},{18,19},{19,1},{1,3},{3,2},{2,0},{0,16},{20,21},{2... | collective-permute-start | bytes 884744 | tf_op jit(solution)/shard_map/ppermute | solution.py:259
  23.9 5.5 %collective-permute-start.13 = (bf16[8,128,128]{2,1,0:T(8,128)(2,1)S(1)}, bf16[8,128,128]{2,1,0:T(8,128)(2,1)S(1)}, u32[]{:S(2)}, u32[]{:S(2)}) collective-permute-start(bf16[8,128,128]{2,1,0:T(8,128)(2,1)S(1)} %shard_map.62.refs_1_.refs_4_.refs_5_), channel_id=1, source_target_pairs={{0,4},{1,5},{2,6},{3,7},{4,8},{5,9},{6,10},{7,11},{8,12},{9,13},{1... | collective-permute-start | bytes 786440 | tf_op jit(solution)/shard_map/ppermute | solution.py:259
  24.0 6.8 %collective-permute-start.12 = (bf16[8,128,128]{2,1,0:T(8,128)(2,1)S(1)}, bf16[8,128,128]{2,1,0:T(8,128)(2,1)S(1)}, u32[]{:S(2)}, u32[]{:S(2)}) collective-permute-start(bf16[8,128,128]{2,1,0:T(8,128)(2,1)S(1)} %shard_map.62.refs_1_.refs_4_.refs_5_), channel_id=1, source_target_pairs={{16,17},{17,18},{18,19},{19,1},{1,3},{3,2},{2,0},{0,16},{20,21},{2... | collective-permute-start | bytes 786440 | tf_op jit(solution)/shard_map/ppermute | solution.py:259
  31.4 3.6 %collective-permute-start.16 = (bf16[7,128,128]{2,1,0:T(8,128)(2,1)S(1)}, bf16[7,128,128]{2,1,0:T(8,128)(2,1)S(1)}, u32[]{:S(2)}, u32[]{:S(2)}) collective-permute-start(bf16[7,128,128]{2,1,0:T(8,128)(2,1)S(1)} %get-tuple-element.47.refs_2_), channel_id=1, source_target_pairs={{0,17},{1,18},{2,19},{3,16},{4,21},{5,22},{6,23},{7,20},{8,25},{9,... | collective-permute-start | bytes 688136 | tf_op jit(solution)/shard_map/ppermute | solution.py:259
  31.5 6.0 %collective-permute-start.20 = (bf16[7,128,128]{2,1,0:T(8,128)(2,1)S(1)}, bf16[7,128,128]{2,1,0:T(8,128)(2,1)S(1)}, u32[]{:S(2)}, u32[]{:S(2)}) collective-permute-start(bf16[7,128,128]{2,1,0:T(8,128)(2,1)S(1)} %get-tuple-element.47.refs_2_), channel_id=1, source_target_pairs={{16,20},{17,21},{18,22},{19,23},{20,24},{21,25},{22,26},{23,27},{2... | collective-permute-start | bytes 688136 | tf_op jit(solution)/shard_map/ppermute | solution.py:259
  32.4 7.3 %collective-permute-start.15 = (bf16[8,128,128]{2,1,0:T(8,128)(2,1)S(1)}, bf16[8,128,128]{2,1,0:T(8,128)(2,1)S(1)}, u32[]{:S(2)}, u32[]{:S(2)}) collective-permute-start(bf16[8,128,128]{2,1,0:T(8,128)(2,1)S(1)} %shard_map.67.after), channel_id=1, source_target_pairs={{0,17},{1,18},{2,19},{3,16},{4,21},{5,22},{6,23},{7,20},{8,25},{9,... | collective-permute-start | bytes 786440 | tf_op jit(solution)/shard_map/ppermute | solution.py:259
  33.6 6.8 %collective-permute-start.14 = (bf16[8,128,128]{2,1,0:T(8,128)(2,1)S(1)}, bf16[8,128,128]{2,1,0:T(8,128)(2,1)S(1)}, u32[]{:S(2)}, u32[]{:S(2)}) collective-permute-start(bf16[8,128,128]{2,1,0:T(8,128)(2,1)S(1)} %shard_map.67.after), channel_id=1, source_target_pairs={{16,20},{17,21},{18,22},{19,23},{20,24},{21,25},{22,26},{23,27},{2... | collective-permute-start | bytes 786440 | tf_op jit(solution)/shard_map/ppermute | solution.py:259
  35.0 3.8 %collective-permute-start.17 = (bf16[6,128,128]{2,1,0:T(8,128)(2,1)S(1)}, bf16[6,128,128]{2,1,0:T(8,128)(2,1)S(1)}, u32[]{:S(2)}, u32[]{:S(2)}) collective-permute-start(bf16[6,128,128]{2,1,0:T(8,128)(2,1)S(1)} %get-tuple-element.52), channel_id=1, source_target_pairs={{0,16},{1,17},{2,18},{3,19},{4,20},{5,21},{6,22},{7,23},{8,24},{9,... | collective-permute-start | bytes 589832 | tf_op jit(solution)/shard_map/ppermute | solution.py:259
  37.1 1.8 %collective-permute-start.18 = (bf16[6,128,128]{2,1,0:T(8,128)(2,1)S(1)}, bf16[6,128,128]{2,1,0:T(8,128)(2,1)S(1)}, u32[]{:S(2)}, u32[]{:S(2)}) collective-permute-start(bf16[6,128,128]{2,1,0:T(8,128)(2,1)S(1)} %get-tuple-element.53), channel_id=1, source_target_pairs={{0,16},{1,17},{2,18},{3,19},{4,20},{5,21},{6,22},{7,23},{8,24},{9,... | collective-permute-start | bytes 589832 | tf_op jit(solution)/shard_map/ppermute | solution.py:259
  37.5 1.3 %collective-permute-start.19 = (bf16[3,128,128]{2,1,0:T(8,128)(2,1)S(1)}, bf16[3,128,128]{2,1,0:T(8,128)(2,1)S(1)}, u32[]{:S(2)}, u32[]{:S(2)}) collective-permute-start(bf16[3,128,128]{2,1,0:T(8,128)(2,1)S(1)} %get-tuple-element.54), channel_id=1, source_target_pairs={{0,16},{1,17},{2,18},{3,19},{4,20},{5,21},{6,22},{7,23},{8,24},{9,... | collective-permute-start | bytes 294920 | tf_op jit(solution)/shard_map/ppermute | solution.py:259
